TPU v7x, 512 devices: a whole 4x4x16 slice. The times are simulated.
512 devices in a mesh: shot: 8 (over z_lo, core), gx: 16 (over x, y), gy: 4 (over z_hi).
Axes of the slice: x: 4, y: 4, z: 16 (z_hi: 4, z_lo: 4; z = z_hi * 4 + z_lo), core: 2. Of those that a mesh axis runs over, the one named last changes fastest.
Arguments:
- velocity: float32 [16, 256, 512], P('shot', 'gx', 'gy'), may hold values from 0.5 to 1
- buoyancy: float32 [16, 256, 512], P('shot', 'gx', 'gy'), may hold values from 0.5 to 1
- fwd_field: bfloat16 [8, 8, 16, 256, 512], P('shot', None, None, 'gx', 'gy'), may hold values from -6 to 6
- adjoint_now: float32 [8, 16, 256, 512], P('shot', None, 'gx', 'gy'), may hold values from -6 to 6
- adjoint_prev: float32 [8, 16, 256, 512], P('shot', None, 'gx', 'gy'), may hold values from -6 to 6
- recv_cell: int32 [8, 256], P('shot'), may hold values from 0 to 2097151
- traces: float32 [8, 8, 256], P('shot'), may hold values from -6 to 6
Outputs:
- grad_vel: float32 [16, 256, 512], P('shot', 'gx', 'gy')
- grad_buoy: float32 [16, 256, 512], P('shot', 'gx', 'gy')
- adjoint_out: float32 [8, 16, 256, 512], P('shot', None, 'gx', 'gy')
- adjoint_out_prev: float32 [8, 16, 256, 512], P('shot', None, 'gx', 'gy')
Inputs may be any that keep to these rules, and one draw needn't show every extreme that they name: `recv_cell`: z*256*512 + x*512 + y of a cell inside the grid.
All inputs are finite; a program needn't handle non-finite values.
Results may differ from a plain program's by a relative error of at most 0.0003.
Values sent between devices are 32-bit elements; how exact they have to be, the bound alone decides.
No kernel may reach another device: no remote copies, remote signals or barrier semaphores. Data moves between devices by JAX's collectives and lax.ppermute only.
A program may use at most 64 MiB of HBM per device.

v0:
```python
import jax
import jax.numpy as jnp
from jax import lax
from jax.sharding import PartitionSpec as P

STEPS = 8


second_coef = (-205.0 / 72.0, 8.0 / 5.0, -1.0 / 5.0, 8.0 / 315.0, -1.0 / 560.0)
first_coef = (4.0 / 5.0, -1.0 / 5.0, 4.0 / 105.0, -1.0 / 280.0)
courant = 0.15


def extended(block, sides, width):
    for axis, dim in sides:
        count = lax.axis_size(axis)
        forward = [(i, i + 1) for i in range(count - 1)]
        backward = [(target, source) for source, target in forward]
        low = lax.ppermute(
            lax.slice_in_dim(block, block.shape[dim] - width, None, axis=dim), axis, forward
        )
        high = lax.ppermute(lax.slice_in_dim(block, 0, width, axis=dim), axis, backward)
        block = jnp.concatenate([low, block, high], axis=dim)
    return block


def derivs(padded):
    nz = padded.shape[-3]
    length_x = padded.shape[-2] - 8
    length_y = padded.shape[-1] - 8
    zpadded = jnp.pad(padded, [(0, 0)] * (padded.ndim - 3) + [(4, 4), (0, 0), (0, 0)])

    def cut(dz, dx, dy):
        return zpadded[
            ..., 4 + dz : 4 + dz + nz, 4 + dx : 4 + dx + length_x, 4 + dy : 4 + dy + length_y
        ]

    lap = 3.0 * second_coef[0] * cut(0, 0, 0)
    grad_z = jnp.zeros_like(lap)
    grad_x = jnp.zeros_like(lap)
    grad_y = jnp.zeros_like(lap)
    for k in range(1, 5):
        lap = lap + second_coef[k] * (
            cut(k, 0, 0)
            + cut(-k, 0, 0)
            + cut(0, k, 0)
            + cut(0, -k, 0)
            + cut(0, 0, k)
            + cut(0, 0, -k)
        )
        grad_z = grad_z + first_coef[k - 1] * (cut(k, 0, 0) - cut(-k, 0, 0))
        grad_x = grad_x + first_coef[k - 1] * (cut(0, k, 0) - cut(0, -k, 0))
        grad_y = grad_y + first_coef[k - 1] * (cut(0, 0, k) - cut(0, 0, -k))
    return (lap, grad_z, grad_x, grad_y)


def crop(field, margin):
    return field[..., margin : field.shape[-2] - margin, margin : field.shape[-1] - margin]


def shards(velocity, buoyancy, fwd_field, adjoint_now, adjoint_prev, recv_cell, traces):
    shots_here = adjoint_now.shape[0]
    width_x = adjoint_now.shape[2]
    width_y = adjoint_now.shape[3]
    per_block = 1
    model_margin = 4 * per_block + 4
    layers = (
        lax.all_gather(velocity, "shot", axis=0, tiled=True),
        lax.all_gather(buoyancy, "shot", axis=0, tiled=True),
    )
    model = extended(jnp.stack([layers[0], layers[1]]), (("gx", 2), ("gy", 3)), model_margin)
    unused, bgrad_z, bgrad_x, bgrad_y = derivs(model[1])
    buoy_wide = crop(model[1], 4)
    speed_wide = crop(courant * model[0] * model[0], 4)
    full_x = width_x * lax.axis_size("gx")
    full_y = width_y * lax.axis_size("gy")
    anchor_x = lax.axis_index("gx") * width_x
    anchor_y = lax.axis_index("gy") * width_y
    depth_idx = recv_cell // (full_x * full_y)
    rest = recv_cell % (full_x * full_y)
    x_idx = rest // full_y
    y_idx = rest % full_y
    shot_ids = jnp.arange(shots_here, dtype=jnp.int32)[:, None]
    image_v = jnp.zeros(adjoint_now.shape[1:], jnp.float32)
    image_b = jnp.zeros(adjoint_now.shape[1:], jnp.float32)
    now = adjoint_now
    prev = adjoint_prev
    for step in range(STEPS):
        now_pad = extended(now, (("gx", 2), ("gy", 3)), 4)
        advance_image_v = image_v
        advance_image_b = image_b
        local_x = x_idx - anchor_x + 4
        local_y = y_idx - anchor_y + 4
        valid = (
            (local_x >= 0)
            & (local_x < now_pad.shape[2])
            & (local_y >= 0)
            & (local_y < now_pad.shape[3])
        )
        local_x = jnp.where(valid, local_x, now_pad.shape[2])
        local_y = jnp.where(valid, local_y, now_pad.shape[3])
        advance_field = now_pad.at[shot_ids, depth_idx, local_x, local_y].add(
            traces[:, step, :], mode="drop"
        )
        lap, grad_z, grad_x, grad_y = derivs(advance_field)
        offset = 4 * per_block - (4 - 4)
        operated = (
            crop(buoy_wide, offset) * lap
            + crop(bgrad_z, offset) * grad_z
            + crop(bgrad_x, offset) * grad_x
            + crop(bgrad_y, offset) * grad_y
        )
        inner = 4 - 4
        snapshot = fwd_field[:, step]
        advance_image_v = advance_image_v + jnp.sum(snapshot * crop(operated, inner), axis=0)
        advance_image_b = advance_image_b + jnp.sum(snapshot * crop(lap, inner), axis=0)
        centre = crop(advance_field, 4)
        excess = (prev.shape[-2] - centre.shape[-2]) // 2
        updated = 2.0 * centre - crop(prev, excess) + crop(speed_wide, offset) * operated
        now = updated
        prev = centre
        image_v = advance_image_v
        image_b = advance_image_b
    summed = (
        lax.psum_scatter(image_v, "shot", scatter_dimension=0, tiled=True),
        lax.psum_scatter(image_b, "shot", scatter_dimension=0, tiled=True),
    )
    scale = 1.0 / (shots_here * lax.axis_size("shot") * STEPS) ** 0.5
    grad_vel = 2.0 * courant * velocity * summed[0] * scale
    grad_buoy = courant * velocity * velocity * summed[1] * scale
    return (grad_vel, grad_buoy, now, prev)


def solution(mesh):
    return jax.shard_map(
        shards,
        mesh=mesh,
        in_specs=(
            P("shot", "gx", "gy"),
            P("shot", "gx", "gy"),
            P("shot", None, None, "gx", "gy"),
            P("shot", None, "gx", "gy"),
            P("shot", None, "gx", "gy"),
            P("shot", None),
            P("shot", None, None),
        ),
        out_specs=(
            P("shot", "gx", "gy"),
            P("shot", "gx", "gy"),
            P("shot", None, "gx", "gy"),
            P("shot", None, "gx", "gy"),
        ),
        check_vma=False,
    )
```

profile of v0, /device:TPU:6, one launch (start us, length us, event | category | flops | bytes accessed | tf_op | source)
XLA Modules:
  0.0 552.1 jit_solution(5738777004207092474)
XLA Ops:
  16.1 14.9 %all_gather.7 = f32[16,16,128]{2,1,0:T(8,128)S(1)} all-gather(f32[2,16,128]{2,1,0:T(8,128)S(1)} %copy-done.13), channel_id=1, replica_groups=mesh['shot'=8,'gx'=16,'gy'=4] {'shot'}, dimensions={0}, use_global_device_ids=true | all-gather | bytes 147456 | tf_op jit(solution)/shard_map/all_gather | solution.py:69
  31.0 14.2 %all_gather.6 = f32[16,16,128]{2,1,0:T(8,128)S(1)} all-gather(f32[2,16,128]{2,1,0:T(8,128)S(1)} %copy-done.11), channel_id=1, replica_groups=mesh['shot'=8,'gx'=16,'gy'=4] {'shot'}, dimensions={0}, use_global_device_ids=true | all-gather | bytes 147456 | tf_op jit(solution)/shard_map/all_gather | solution.py:68
  54.9 9.1 %collective-permute-start.6 = (f32[1,16,24,4]{3,2,1,0:T(8,128)S(1)}, f32[1,16,24,4]{3,2,1,0:T(8,128)S(1)}, u32[]{:S(2)}, u32[]{:S(2)}) collective-permute-start(f32[1,16,24,4]{3,2,1,0:T(8,128)S(1)} %get-tuple-element.83), channel_id=1, source_target_pairs={{0,1},{1,2},{2,3},{4,5},{5,6},{6,7},{8,9},{9,10},{10,11},{12,13},{... | collective-permute-start | bytes 18440 | tf_op jit(solution)/shard_map/ppermute | solution.py:19
  65.6 8.6 %collective-permute-start.2 = (f32[2,16,32,8]{3,2,1,0:T(8,128)S(1)}, f32[2,16,32,8]{3,2,1,0:T(8,128)S(1)}, u32[]{:S(2)}, u32[]{:S(2)}) collective-permute-start(f32[2,16,32,8]{3,2,1,0:T(8,128)S(1)} %get-tuple-element.65), channel_id=1, source_target_pairs={{0,1},{1,2},{2,3},{4,5},{5,6},{6,7},{8,9},{9,10},{10,11},{12,13},{... | collective-permute-start | bytes 98312 | tf_op jit(solution)/shard_map/ppermute | solution.py:19
  75.5 47.5 %collective-permute-done.7 = f32[1,16,24,4]{3,2,1,0:T(8,128)S(1)} collective-permute-done((f32[1,16,24,4]{3,2,1,0:T(8,128)S(1)}, f32[1,16,24,4]{3,2,1,0:T(8,128)S(1)}, u32[]{:S(2)}, u32[]{:S(2)}) %collective-permute-start.7) | collective-permute-done | bytes 6176 | tf_op jit(solution)/shard_map/ppermute | solution.py:22
  123.3 16.3 %scatter_fusion = f32[16,24,136]{2,1,0:T(8,128)S(1)} fusion(f32[16,24,136]{2,1,0:T(8,128)S(1)} %maximum_bitcast_fusion, s32[256]{0:T(256)S(1)} %bitcast.137, f32[256]{0:T(256)S(1)} %bitcast.173), kind=kCustom, calls=%fused_computation | custom fusion | flops 256 | bytes 6144 | tf_op jit(solution)/shard_map/scatter-add | solution.py:102
  155.9 7.1 %collective-permute-start.10 = (f32[1,16,24,4]{3,2,1,0:T(8,128)S(1)}, f32[1,16,24,4]{3,2,1,0:T(8,128)S(1)}, u32[]{:S(2)}, u32[]{:S(2)}) collective-permute-start(f32[1,16,24,4]{3,2,1,0:T(8,128)S(1)} %get-tuple-element.81), channel_id=1, source_target_pairs={{0,1},{1,2},{2,3},{4,5},{5,6},{6,7},{8,9},{9,10},{10,11},{12,13},{... | collective-permute-start | bytes 18440 | tf_op jit(solution)/shard_map/ppermute | solution.py:19
  166.2 9.1 %collective-permute-done.11 = f32[1,16,24,4]{3,2,1,0:T(8,128)S(1)} collective-permute-done((f32[1,16,24,4]{3,2,1,0:T(8,128)S(1)}, f32[1,16,24,4]{3,2,1,0:T(8,128)S(1)}, u32[]{:S(2)}, u32[]{:S(2)}) %collective-permute-start.11) | collective-permute-done | bytes 6176 | tf_op jit(solution)/shard_map/ppermute | solution.py:22
  176.2 16.3 %scatter_fusion.1 = f32[16,24,136]{2,1,0:T(8,128)S(1)} fusion(f32[16,24,136]{2,1,0:T(8,128)S(1)} %maximum_bitcast_fusion.1, s32[256]{0:T(256)S(1)} %bitcast.138, f32[256]{0:T(256)S(1)} %bitcast.172), kind=kCustom, calls=%fused_computation.1 | custom fusion | flops 256 | bytes 6144 | tf_op jit(solution)/shard_map/scatter-add | solution.py:102
  211.6 8.9 %collective-permute-done.15 = f32[1,16,24,4]{3,2,1,0:T(8,128)S(1)} collective-permute-done((f32[1,16,24,4]{3,2,1,0:T(8,128)S(1)}, f32[1,16,24,4]{3,2,1,0:T(8,128)S(1)}, u32[]{:S(2)}, u32[]{:S(2)}) %collective-permute-start.15) | collective-permute-done | bytes 6176 | tf_op jit(solution)/shard_map/ppermute | solution.py:22
  221.5 16.3 %scatter_fusion.2 = f32[16,24,136]{2,1,0:T(8,128)S(1)} fusion(f32[16,24,136]{2,1,0:T(8,128)S(1)} %maximum_bitcast_fusion.2, s32[256]{0:T(256)S(1)} %bitcast.139, f32[256]{0:T(256)S(1)} %bitcast.171), kind=kCustom, calls=%fused_computation.2 | custom fusion | flops 256 | bytes 6144 | tf_op jit(solution)/shard_map/scatter-add | solution.py:102
  255.8 9.2 %collective-permute-done.19 = f32[1,16,24,4]{3,2,1,0:T(8,128)S(1)} collective-permute-done((f32[1,16,24,4]{3,2,1,0:T(8,128)S(1)}, f32[1,16,24,4]{3,2,1,0:T(8,128)S(1)}, u32[]{:S(2)}, u32[]{:S(2)}) %collective-permute-start.19) | collective-permute-done | bytes 6176 | tf_op jit(solution)/shard_map/ppermute | solution.py:22
  266.0 16.3 %scatter_fusion.3 = f32[16,24,136]{2,1,0:T(8,128)S(1)} fusion(f32[16,24,136]{2,1,0:T(8,128)S(1)} %maximum_bitcast_fusion.3, s32[256]{0:T(256)S(1)} %bitcast.140, f32[256]{0:T(256)S(1)} %bitcast.170), kind=kCustom, calls=%fused_computation.3 | custom fusion | flops 256 | bytes 6144 | tf_op jit(solution)/shard_map/scatter-add | solution.py:102
  300.1 9.4 %collective-permute-done.23 = f32[1,16,24,4]{3,2,1,0:T(8,128)S(1)} collective-permute-done((f32[1,16,24,4]{3,2,1,0:T(8,128)S(1)}, f32[1,16,24,4]{3,2,1,0:T(8,128)S(1)}, u32[]{:S(2)}, u32[]{:S(2)}) %collective-permute-start.23) | collective-permute-done | bytes 6176 | tf_op jit(solution)/shard_map/ppermute | solution.py:22
  310.4 16.3 %scatter_fusion.4 = f32[16,24,136]{2,1,0:T(8,128)S(1)} fusion(f32[16,24,136]{2,1,0:T(8,128)S(1)} %maximum_bitcast_fusion.4, s32[256]{0:T(256)S(1)} %bitcast.141, f32[256]{0:T(256)S(1)} %bitcast.169), kind=kCustom, calls=%fused_computation.4 | custom fusion | flops 256 | bytes 6144 | tf_op jit(solution)/shard_map/scatter-add | solution.py:102
  344.6 9.2 %collective-permute-done.27 = f32[1,16,24,4]{3,2,1,0:T(8,128)S(1)} collective-permute-done((f32[1,16,24,4]{3,2,1,0:T(8,128)S(1)}, f32[1,16,24,4]{3,2,1,0:T(8,128)S(1)}, u32[]{:S(2)}, u32[]{:S(2)}) %collective-permute-start.27) | collective-permute-done | bytes 6176 | tf_op jit(solution)/shard_map/ppermute | solution.py:22
  354.0 16.3 %scatter_fusion.5 = f32[16,24,136]{2,1,0:T(8,128)S(1)} fusion(f32[16,24,136]{2,1,0:T(8,128)S(1)} %maximum_bitcast_fusion.5, s32[256]{0:T(256)S(1)} %bitcast.142, f32[256]{0:T(256)S(1)} %bitcast.168), kind=kCustom, calls=%fused_computation.5 | custom fusion | flops 256 | bytes 6144 | tf_op jit(solution)/shard_map/scatter-add | solution.py:102
  374.1 6.3 %collective-permute-start.29 = (f32[1,16,4,128]{3,2,1,0:T(4,128)S(1)}, f32[1,16,4,128]{3,2,1,0:T(4,128)S(1)}, u32[]{:S(2)}, u32[]{:S(2)}) collective-permute-start(f32[1,16,4,128]{3,2,1,0:T(4,128)S(1)} %get-tuple-element.88), channel_id=1, source_target_pairs={{4,0},{8,4},{12,8},{16,12},{20,16},{24,20},{28,24},{32,28},{36,32}... | collective-permute-start | bytes 98312 | tf_op jit(solution)/shard_map/ppermute | solution.py:22
  390.7 13.3 %collective-permute-done.31 = f32[1,16,24,4]{3,2,1,0:T(8,128)S(1)} collective-permute-done((f32[1,16,24,4]{3,2,1,0:T(8,128)S(1)}, f32[1,16,24,4]{3,2,1,0:T(8,128)S(1)}, u32[]{:S(2)}, u32[]{:S(2)}) %collective-permute-start.31) | collective-permute-done | bytes 6176 | tf_op jit(solution)/shard_map/ppermute | solution.py:22
  404.3 16.3 %scatter_fusion.6 = f32[16,24,136]{2,1,0:T(8,128)S(1)} fusion(f32[16,24,136]{2,1,0:T(8,128)S(1)} %maximum_bitcast_fusion.6, s32[256]{0:T(256)S(1)} %bitcast.143, f32[256]{0:T(256)S(1)} %bitcast.167), kind=kCustom, calls=%fused_computation.6 | custom fusion | flops 256 | bytes 6144 | tf_op jit(solution)/shard_map/scatter-add | solution.py:102
  438.3 9.2 %collective-permute-done.35 = f32[1,16,24,4]{3,2,1,0:T(8,128)S(1)} collective-permute-done((f32[1,16,24,4]{3,2,1,0:T(8,128)S(1)}, f32[1,16,24,4]{3,2,1,0:T(8,128)S(1)}, u32[]{:S(2)}, u32[]{:S(2)}) %collective-permute-start.35) | collective-permute-done | bytes 6176 | tf_op jit(solution)/shard_map/ppermute | solution.py:22
  447.9 16.3 %scatter_fusion.7 = f32[16,24,136]{2,1,0:T(8,128)S(1)} fusion(f32[16,24,136]{2,1,0:T(8,128)S(1)} %maximum_bitcast_fusion.7, s32[256]{0:T(256)S(1)} %bitcast.144, f32[256]{0:T(256)S(1)} %bitcast.166), kind=kCustom, calls=%fused_computation.7 | custom fusion | flops 256 | bytes 6144 | tf_op jit(solution)/shard_map/scatter-add | solution.py:102
  468.6 33.0 %reduce-scatter.3.cloned.1.call-done = f32[2,16,128]{2,1,0:T(8,128)} async-done(((f32[16,16,128]{2,1,0:T(8,128)}), f32[2,16,128]{2,1,0:T(8,128)}) %reduce-scatter.3.cloned.1.call-update) | async-done | bytes 16400 | tf_op jit(solution)/shard_map/reduce_scatter | solution.py:125
  501.6 42.3 %reduce-scatter.5.cloned.1.call-done = f32[2,16,128]{2,1,0:T(8,128)} async-done(((f32[16,16,128]{2,1,0:T(8,128)}), f32[2,16,128]{2,1,0:T(8,128)}) %reduce-scatter.5.cloned.1.call-update) | async-done | bytes 16400 | tf_op jit(solution)/shard_map/reduce_scatter | solution.py:126
  (162 shorter events, 155.8 us)
Async XLA Ops:
  7.2 494.4 %reduce-scatter.3.cloned.1.call-start = ((), (), s32[]{:S(2)}) async-start(), calls=%async_computation.2 | async-start | bytes 147456 | tf_op jit(solution)/shard_map/reduce_scatter | solution.py:125
  8.1 46.6 %collective-permute-start.4 = (f32[1,16,4,128]{3,2,1,0:T(4,128)S(1)}, f32[1,16,4,128]{3,2,1,0:T(4,128)S(1)}, u32[]{:S(2)}, u32[]{:S(2)}) collective-permute-start(f32[1,16,4,128]{3,2,1,0:T(4,128)S(1)} %get-tuple-element.99), channel_id=1, source_target_pairs={{0,4},{4,8},{8,12},{12,16},{16,20},{20,24},{24,28},{28,32},{32,36}... | collective-permute-start | bytes 98312 | tf_op jit(solution)/shard_map/ppermute | solution.py:19
  11.6 43.2 %collective-permute-start.5 = (f32[1,16,4,128]{3,2,1,0:T(4,128)S(1)}, f32[1,16,4,128]{3,2,1,0:T(4,128)S(1)}, u32[]{:S(2)}, u32[]{:S(2)}) collective-permute-start(f32[1,16,4,128]{3,2,1,0:T(4,128)S(1)} %get-tuple-element.100), channel_id=1, source_target_pairs={{4,0},{8,4},{12,8},{16,12},{20,16},{24,20},{28,24},{32,28},{36,32}... | collective-permute-start | bytes 98312 | tf_op jit(solution)/shard_map/ppermute | solution.py:22
  45.2 20.2 %collective-permute-start = (f32[2,16,8,128]{3,2,1,0:T(8,128)S(1)}, f32[2,16,8,128]{3,2,1,0:T(8,128)S(1)}, u32[]{:S(2)}, u32[]{:S(2)}) collective-permute-start(f32[2,16,8,128]{3,2,1,0:T(8,128)S(1)} %get-tuple-element.67), channel_id=1, source_target_pairs={{0,4},{4,8},{8,12},{12,16},{16,20},{20,24},{24,28},{28,32},{32,36}... | collective-permute-start | bytes 393224 | tf_op jit(solution)/shard_map/ppermute | solution.py:19
  47.3 18.1 %collective-permute-start.1 = (f32[2,16,8,128]{3,2,1,0:T(8,128)S(1)}, f32[2,16,8,128]{3,2,1,0:T(8,128)S(1)}, u32[]{:S(2)}, u32[]{:S(2)}) collective-permute-start(f32[2,16,8,128]{3,2,1,0:T(8,128)S(1)} %get-tuple-element.68), channel_id=1, source_target_pairs={{4,0},{8,4},{12,8},{16,12},{20,16},{24,20},{28,24},{32,28},{36,32}... | collective-permute-start | bytes 393224 | tf_op jit(solution)/shard_map/ppermute | solution.py:22
  54.9 20.6 %collective-permute-start.6 = (f32[1,16,24,4]{3,2,1,0:T(8,128)S(1)}, f32[1,16,24,4]{3,2,1,0:T(8,128)S(1)}, u32[]{:S(2)}, u32[]{:S(2)}) collective-permute-start(f32[1,16,24,4]{3,2,1,0:T(8,128)S(1)} %get-tuple-element.83), channel_id=1, source_target_pairs={{0,1},{1,2},{2,3},{4,5},{5,6},{6,7},{8,9},{9,10},{10,11},{12,13},{... | collective-permute-start | bytes 18440 | tf_op jit(solution)/shard_map/ppermute | solution.py:19
  64.1 58.9 %collective-permute-start.7 = (f32[1,16,24,4]{3,2,1,0:T(8,128)S(1)}, f32[1,16,24,4]{3,2,1,0:T(8,128)S(1)}, u32[]{:S(2)}, u32[]{:S(2)}) collective-permute-start(f32[1,16,24,4]{3,2,1,0:T(8,128)S(1)} %get-tuple-element.84), channel_id=1, source_target_pairs={{1,0},{2,1},{3,2},{5,4},{6,5},{7,6},{9,8},{10,9},{11,10},{13,12},{... | collective-permute-start | bytes 18440 | tf_op jit(solution)/shard_map/ppermute | solution.py:22
  65.6 73.9 %collective-permute-start.2 = (f32[2,16,32,8]{3,2,1,0:T(8,128)S(1)}, f32[2,16,32,8]{3,2,1,0:T(8,128)S(1)}, u32[]{:S(2)}, u32[]{:S(2)}) collective-permute-start(f32[2,16,32,8]{3,2,1,0:T(8,128)S(1)} %get-tuple-element.65), channel_id=1, source_target_pairs={{0,1},{1,2},{2,3},{4,5},{5,6},{6,7},{8,9},{9,10},{10,11},{12,13},{... | collective-permute-start | bytes 98312 | tf_op jit(solution)/shard_map/ppermute | solution.py:19
  74.2 65.4 %collective-permute-start.3 = (f32[2,16,32,8]{3,2,1,0:T(8,128)S(1)}, f32[2,16,32,8]{3,2,1,0:T(8,128)S(1)}, u32[]{:S(2)}, u32[]{:S(2)}) collective-permute-start(f32[2,16,32,8]{3,2,1,0:T(8,128)S(1)} %get-tuple-element.66), channel_id=1, source_target_pairs={{1,0},{2,1},{3,2},{5,4},{6,5},{7,6},{9,8},{10,9},{11,10},{13,12},{... | collective-permute-start | bytes 98312 | tf_op jit(solution)/shard_map/ppermute | solution.py:22
  155.9 10.3 %collective-permute-start.10 = (f32[1,16,24,4]{3,2,1,0:T(8,128)S(1)}, f32[1,16,24,4]{3,2,1,0:T(8,128)S(1)}, u32[]{:S(2)}, u32[]{:S(2)}) collective-permute-start(f32[1,16,24,4]{3,2,1,0:T(8,128)S(1)} %get-tuple-element.81), channel_id=1, source_target_pairs={{0,1},{1,2},{2,3},{4,5},{5,6},{6,7},{8,9},{9,10},{10,11},{12,13},{... | collective-permute-start | bytes 18440 | tf_op jit(solution)/shard_map/ppermute | solution.py:19
  163.0 12.2 %collective-permute-start.11 = (f32[1,16,24,4]{3,2,1,0:T(8,128)S(1)}, f32[1,16,24,4]{3,2,1,0:T(8,128)S(1)}, u32[]{:S(2)}, u32[]{:S(2)}) collective-permute-start(f32[1,16,24,4]{3,2,1,0:T(8,128)S(1)} %get-tuple-element.82), channel_id=1, source_target_pairs={{1,0},{2,1},{3,2},{5,4},{6,5},{7,6},{9,8},{10,9},{11,10},{13,12},{... | collective-permute-start | bytes 18440 | tf_op jit(solution)/shard_map/ppermute | solution.py:22
  193.7 8.3 %collective-permute-start.12 = (f32[1,16,4,128]{3,2,1,0:T(4,128)S(1)}, f32[1,16,4,128]{3,2,1,0:T(4,128)S(1)}, u32[]{:S(2)}, u32[]{:S(2)}) collective-permute-start(f32[1,16,4,128]{3,2,1,0:T(4,128)S(1)} %get-tuple-element.95), channel_id=1, source_target_pairs={{0,4},{4,8},{8,12},{12,16},{16,20},{20,24},{24,28},{28,32},{32,36}... | collective-permute-start | bytes 98312 | tf_op jit(solution)/shard_map/ppermute | solution.py:19
  208.5 12.1 %collective-permute-start.15 = (f32[1,16,24,4]{3,2,1,0:T(8,128)S(1)}, f32[1,16,24,4]{3,2,1,0:T(8,128)S(1)}, u32[]{:S(2)}, u32[]{:S(2)}) collective-permute-start(f32[1,16,24,4]{3,2,1,0:T(8,128)S(1)} %get-tuple-element.80), channel_id=1, source_target_pairs={{1,0},{2,1},{3,2},{5,4},{6,5},{7,6},{9,8},{10,9},{11,10},{13,12},{... | collective-permute-start | bytes 18440 | tf_op jit(solution)/shard_map/ppermute | solution.py:22
  239.0 8.3 %collective-permute-start.16 = (f32[1,16,4,128]{3,2,1,0:T(4,128)S(1)}, f32[1,16,4,128]{3,2,1,0:T(4,128)S(1)}, u32[]{:S(2)}, u32[]{:S(2)}) collective-permute-start(f32[1,16,4,128]{3,2,1,0:T(4,128)S(1)} %get-tuple-element.93), channel_id=1, source_target_pairs={{0,4},{4,8},{8,12},{12,16},{16,20},{20,24},{24,28},{28,32},{32,36}... | collective-permute-start | bytes 98312 | tf_op jit(solution)/shard_map/ppermute | solution.py:19
  252.6 12.4 %collective-permute-start.19 = (f32[1,16,24,4]{3,2,1,0:T(8,128)S(1)}, f32[1,16,24,4]{3,2,1,0:T(8,128)S(1)}, u32[]{:S(2)}, u32[]{:S(2)}) collective-permute-start(f32[1,16,24,4]{3,2,1,0:T(8,128)S(1)} %get-tuple-element.78), channel_id=1, source_target_pairs={{1,0},{2,1},{3,2},{5,4},{6,5},{7,6},{9,8},{10,9},{11,10},{13,12},{... | collective-permute-start | bytes 18440 | tf_op jit(solution)/shard_map/ppermute | solution.py:22
  284.1 8.3 %collective-permute-start.20 = (f32[1,16,4,128]{3,2,1,0:T(4,128)S(1)}, f32[1,16,4,128]{3,2,1,0:T(4,128)S(1)}, u32[]{:S(2)}, u32[]{:S(2)}) collective-permute-start(f32[1,16,4,128]{3,2,1,0:T(4,128)S(1)} %get-tuple-element.91), channel_id=1, source_target_pairs={{0,4},{4,8},{8,12},{12,16},{16,20},{20,24},{24,28},{28,32},{32,36}... | collective-permute-start | bytes 98312 | tf_op jit(solution)/shard_map/ppermute | solution.py:19
  296.9 12.5 %collective-permute-start.23 = (f32[1,16,24,4]{3,2,1,0:T(8,128)S(1)}, f32[1,16,24,4]{3,2,1,0:T(8,128)S(1)}, u32[]{:S(2)}, u32[]{:S(2)}) collective-permute-start(f32[1,16,24,4]{3,2,1,0:T(8,128)S(1)} %get-tuple-element.76), channel_id=1, source_target_pairs={{1,0},{2,1},{3,2},{5,4},{6,5},{7,6},{9,8},{10,9},{11,10},{13,12},{... | collective-permute-start | bytes 18440 | tf_op jit(solution)/shard_map/ppermute | solution.py:22
  328.6 8.3 %collective-permute-start.24 = (f32[1,16,4,128]{3,2,1,0:T(4,128)S(1)}, f32[1,16,4,128]{3,2,1,0:T(4,128)S(1)}, u32[]{:S(2)}, u32[]{:S(2)}) collective-permute-start(f32[1,16,4,128]{3,2,1,0:T(4,128)S(1)} %get-tuple-element.89), channel_id=1, source_target_pairs={{0,4},{4,8},{8,12},{12,16},{16,20},{20,24},{24,28},{28,32},{32,36}... | collective-permute-start | bytes 98312 | tf_op jit(solution)/shard_map/ppermute | solution.py:19
  341.4 12.3 %collective-permute-start.27 = (f32[1,16,24,4]{3,2,1,0:T(8,128)S(1)}, f32[1,16,24,4]{3,2,1,0:T(8,128)S(1)}, u32[]{:S(2)}, u32[]{:S(2)}) collective-permute-start(f32[1,16,24,4]{3,2,1,0:T(8,128)S(1)} %get-tuple-element.74), channel_id=1, source_target_pairs={{1,0},{2,1},{3,2},{5,4},{6,5},{7,6},{9,8},{10,9},{11,10},{13,12},{... | collective-permute-start | bytes 18440 | tf_op jit(solution)/shard_map/ppermute | solution.py:22
  372.2 8.3 %collective-permute-start.28 = (f32[1,16,4,128]{3,2,1,0:T(4,128)S(1)}, f32[1,16,4,128]{3,2,1,0:T(4,128)S(1)}, u32[]{:S(2)}, u32[]{:S(2)}) collective-permute-start(f32[1,16,4,128]{3,2,1,0:T(4,128)S(1)} %get-tuple-element.87), channel_id=1, source_target_pairs={{0,4},{4,8},{8,12},{12,16},{16,20},{20,24},{24,28},{28,32},{32,36}... | collective-permute-start | bytes 98312 | tf_op jit(solution)/shard_map/ppermute | solution.py:19
  382.2 8.5 %collective-permute-start.30 = (f32[1,16,24,4]{3,2,1,0:T(8,128)S(1)}, f32[1,16,24,4]{3,2,1,0:T(8,128)S(1)}, u32[]{:S(2)}, u32[]{:S(2)}) collective-permute-start(f32[1,16,24,4]{3,2,1,0:T(8,128)S(1)} %get-tuple-element.71), channel_id=1, source_target_pairs={{0,1},{1,2},{2,3},{4,5},{5,6},{6,7},{8,9},{9,10},{10,11},{12,13},{... | collective-permute-start | bytes 18440 | tf_op jit(solution)/shard_map/ppermute | solution.py:19
  387.4 16.5 %collective-permute-start.31 = (f32[1,16,24,4]{3,2,1,0:T(8,128)S(1)}, f32[1,16,24,4]{3,2,1,0:T(8,128)S(1)}, u32[]{:S(2)}, u32[]{:S(2)}) collective-permute-start(f32[1,16,24,4]{3,2,1,0:T(8,128)S(1)} %get-tuple-element.72), channel_id=1, source_target_pairs={{1,0},{2,1},{3,2},{5,4},{6,5},{7,6},{9,8},{10,9},{11,10},{13,12},{... | collective-permute-start | bytes 18440 | tf_op jit(solution)/shard_map/ppermute | solution.py:22
  435.2 12.4 %collective-permute-start.35 = (f32[1,16,24,4]{3,2,1,0:T(8,128)S(1)}, f32[1,16,24,4]{3,2,1,0:T(8,128)S(1)}, u32[]{:S(2)}, u32[]{:S(2)}) collective-permute-start(f32[1,16,24,4]{3,2,1,0:T(8,128)S(1)} %get-tuple-element.70), channel_id=1, source_target_pairs={{1,0},{2,1},{3,2},{5,4},{6,5},{7,6},{9,8},{10,9},{11,10},{13,12},{... | collective-permute-start | bytes 18440 | tf_op jit(solution)/shard_map/ppermute | solution.py:22
  466.9 76.9 %reduce-scatter.5.cloned.1.call-start = ((), (), s32[]{:S(2)}) async-start(), calls=%async_computation.3 | async-start | bytes 147456 | tf_op jit(solution)/shard_map/reduce_scatter | solution.py:126
  (34 other events, 236.4 us)
Sparse Core Ops, SparseCore 0:
  467.1 34.4 reduce-scatter.2
  504.6 39.2 reduce-scatter.4
where the time goes:
time: 554 us; the launch traced here: 552 us
  waiting for transfers between devices  215 us (39%)
  other arithmetic  152 us (27%)
  starting transfers between devices  132 us (24%)
  blocking collectives  29.1 us (5%)
  between operations  15 us (3%)
  local copies, waits for them, and re-layouts  9.39 us (2%)
    scatter-add x8, other arithmetic, shards(): now_pad.at[shot_ids, depth_idx, local_x, local_y]  130 us
    ppermute x18, waiting for transfers between devices, extended(): lax.ppermute(lax.slice_in_dim(block, 0, width, axis=dim), axis, backward)  127 us
    ppermute x18, starting transfers between devices, extended(): lax.ppermute(lax.slice_in_dim(block, 0, width, axis=dim), axis, backward)  66.5 us
    ppermute x18, starting transfers between devices, extended(): lax.ppermute(lax.slice_in_dim(block, block.shape[dim] - width, None, axis...  65.7 us
    reduce_scatter x1, waiting for transfers between devices, shards(): lax.psum_scatter(image_b, 'shot', scatter_dimension=0, tiled=True)  42.3 us
    reduce_scatter x1, waiting for transfers between devices, shards(): lax.psum_scatter(image_v, 'shot', scatter_dimension=0, tiled=True)  33 us
    add x8, other arithmetic, shards(): 2.0 * centre - crop(prev, excess) + crop(speed_wide, offset) * operated  15.4 us
    all_gather x1, blocking collectives, shards(): lax.all_gather(buoyancy, 'shot', axis=0, tiled=True)  14.9 us
  transfers between devices with their start and end apart: 38, of which 24 were waited for; matrix products, arithmetic and copies ran while one was open for 3% of the time, Pallas kernels for 0%

commit v1 on v0

v1 whole, which is shorter than its diff:
```python
import functools

import jax
import jax.numpy as jnp
from jax import lax
from jax.experimental import pallas as pl
from jax.experimental.pallas import tpu as pltpu
from jax.sharding import PartitionSpec as P

NZ, BX, BY = 16, 16, 128
FULL_X, FULL_Y = 256, 512
STEPS, SHOTS, RECV = 8, 8, 256
ROUND = 4
HY = 32
EXT = 3 * BX
PAD = 8
ROWS = EXT + 2 * PAD
LAYERS = NZ + 8
FAR = BY - HY

second_coef = (-205.0 / 72.0, 8.0 / 5.0, -1.0 / 5.0, 8.0 / 315.0, -1.0 / 560.0)
first_coef = (4.0 / 5.0, -1.0 / 5.0, 4.0 / 105.0, -1.0 / 280.0)
courant = 0.15

VM = pl.BlockSpec(memory_space=pltpu.VMEM)
SM = pl.BlockSpec(memory_space=pltpu.SMEM)


def lane_of(rows):
    return lax.broadcasted_iota(jnp.int32, (rows, BY), 1)


def find_kernel(where_ref, recv_ref, place_ref, which_ref, count_ref):
    base_x = where_ref[0] - BX
    base_y = where_ref[1]

    def body(j, count):
        cell = recv_ref[j]
        z = lax.shift_right_logical(cell, 17)
        x = (lax.shift_right_logical(cell, 9) & (FULL_X - 1)) - base_x
        y = (cell & (FULL_Y - 1)) - base_y
        inside = (x >= 0) & (x < EXT) & (y >= -HY) & (y < BY + HY)
        place_ref[count] = z * 16384 + (x & 63) * 256 + (y & 255)
        which_ref[count] = j
        return count + inside.astype(jnp.int32)

    count_ref[0] = lax.fori_loop(0, RECV, body, jnp.int32(0))


def pack_kernel(where_ref, now_ref, prev_ref, model_ref, first_ref, second_ref):
    even = where_ref[2] == 0
    lane = lane_of(BX)
    out = 0
    for ref in (now_ref, prev_ref, model_ref):
        for q in range(ref.shape[0] // 4):
            right = left = jnp.zeros((BX, BY), jnp.float32)
            for j in range(4):
                plane = ref[4 * q + j]
                mine = (lane >= HY * j) & (lane < HY * (j + 1))
                right = jnp.where(mine, pltpu.roll(plane, (HY * j + HY) % BY, 1), right)
                left = jnp.where(mine, pltpu.roll(plane, HY * j, 1) if j else plane, left)
            first_ref[out] = jnp.where(even, right, left)
            second_ref[out] = jnp.where(even, left, right)
            out += 1


def rolled(main, side, lane, shift):
    a = pltpu.roll(main, -shift % BY, 1)
    b = pltpu.roll(side, -shift % BY, 1)
    keep = lane < BY - shift if shift > 0 else lane >= -shift
    return jnp.where(keep, a, b), jnp.where(keep, b, a)


def derivs(main, side, z, lo, n, sides=True):
    refs = (main, side)
    row = PAD + lo
    centre = [r[z + 4, pl.ds(row, n), :] for r in refs]
    lane = lane_of(n)
    use = (0, 1) if sides else (0,)
    lap = [3.0 * second_coef[0] * centre[i] for i in use]
    dz, dx, dy = [None, None], [None, None], [None, None]
    for k in range(1, 5):
        up = rolled(*centre, lane, k)
        down = rolled(*centre, lane, -k)
        for i in use:
            r = refs[i]
            zp = r[z + 4 + k, pl.ds(row, n), :]
            zm = r[z + 4 - k, pl.ds(row, n), :]
            xp = r[z + 4, pl.ds(row + k, n), :]
            xm = r[z + 4, pl.ds(row - k, n), :]
            lap[i] += second_coef[k] * (((zp + zm) + (xp + xm)) + (up[i] + down[i]))
            for total, p, m in ((dz, zp, zm), (dx, xp, xm), (dy, up[i], down[i])):
                term = first_coef[k - 1] * (p - m)
                total[i] = term if total[i] is None else total[i] + term
    return lap, dz, dx, dy


def run_steps(first_step, cur, old, coefs, fwd_ref, image, place_ref, which_ref, count_ref, trace_ref, last):
    speed, buoy, bz, bx, by = coefs
    plans = (
        ((0, 16), (16, 16), (32, 16)),
        ((8, 8), (16, 16), (32, 8)),
        ((8, 8), (16, 16), (32, 8)),
        ((16, 16),),
    )
    lane1 = lane_of(1)
    for j, plan in enumerate(plans):
        step = first_step + j

        def add(i, _, cur=cur, step=step):
            place = place_ref[i]
            value = trace_ref[step, which_ref[i]]
            z = lax.shift_right_logical(place, 14) + 4
            x = (lax.shift_right_logical(place, 8) & 63) + PAD
            y = place & 255
            for t in (0, 1):
                spot = (z, pl.ds(x, 1), slice(None))
                cur[t][spot] = cur[t][spot] + jnp.where(lane1 + BY * t == y, value, 0.0)
            return 0

        lax.fori_loop(0, count_ref[0], add, 0)
        sides = not (last and j == ROUND - 1)

        def layer(z, _, cur=cur, old=old, plan=plan, j=j, sides=sides):
            for lo, n in plan:
                lap, dz, dx, dy = derivs(cur[0], cur[1], z, lo, n, sides)
                rows = pl.ds(lo, n)
                for i in (0, 1) if sides else (0,):
                    operated = (
                        buoy[i][z + 4, pl.ds(lo + PAD, n), :] * lap[i]
                        + bz[i][z, rows, :] * dz[i]
                        + bx[i][z, rows, :] * dx[i]
                        + by[i][z, rows, :] * dy[i]
                    )
                    spot = (z + 4, pl.ds(lo + PAD, n), slice(None))
                    old[i][spot] = (2.0 * cur[i][spot] - old[i][spot]) + speed[i][z, rows, :] * operated
                    if i == 0 and lo == BX:
                        snapshot = fwd_ref[j, z].astype(jnp.float32)
                        image[0][z] += snapshot * operated
                        image[1][z] += snapshot * lap[0]
            return 0

        lax.fori_loop(0, NZ, layer, 0)
        cur, old = old, cur
    return cur, old


def clear(ref):
    def body(z, _):
        ref[z] = jnp.zeros(ref.shape[1:], jnp.float32)
        return 0

    lax.fori_loop(0, ref.shape[0], body, 0)


def unpack(first, second, even, lane, j):
    right = jnp.where(even, first, second)
    left = jnp.where(even, second, first)
    right = pltpu.roll(right, -HY * j % BY, 1) if j else right
    left = pltpu.roll(left, (FAR - HY * j) % BY, 1) if j < 3 else left
    return jnp.where(lane < HY, right, jnp.where(lane >= FAR, left, 0.0))


def first_kernel(
    where_ref, place_ref, which_ref, count_ref, trace_ref,
    centre_ref, low_ref, high_ref, other_ref, fwd_ref,
    send_ref, iv_ref, ib_ref,
    s0, s1, b0, b1, bz0, bz1, bx0, bx1, by0, by1,
    cm, cs, om, os_,
):
    even = where_ref[2] == 0
    core = where_ref[3]
    lane = lane_of(BX)
    for ref in (cm, cs, om, os_, b0, b1):
        clear(ref)
    for block, ref in enumerate((low_ref, centre_ref, high_ref)):
        rows = pl.ds(PAD + block * BX, BX)
        for f, (main, side) in enumerate(((cm, cs), (om, os_))):
            for q in range(4):
                a, b = ref[48 + 4 * f + q], ref[60 + 4 * f + q]
                for j in range(4):
                    z = 4 * q + j
                    main[4 + z, rows, :] = ref[NZ * f + z]
                    side[4 + z, rows, :] = unpack(a, b, even, lane, j)
        for half in (0, 1):
            turn = core if half == 0 else 1 - core
            spot = (1, 0, 2)[block]
            for q in range(4):
                if half == 0:
                    a, b = ref[56 + q], ref[68 + q]
                else:
                    a, b = other_ref[24 * spot + 16 + q], other_ref[24 * spot + 20 + q]
                for j in range(4):
                    plane = ref[32 + 4 * q + j] if half == 0 else other_ref[24 * spot + 4 * q + j]
                    edge = unpack(a, b, even, lane, j)
                    z = 4 * q + 2 * turn + j % 2
                    if j < 2:
                        s0[z, pl.ds(block * BX, BX), :] = courant * plane * plane
                        s1[z, pl.ds(block * BX, BX), :] = courant * edge * edge
                    else:
                        b0[4 + z, rows, :] = plane
                        b1[4 + z, rows, :] = edge

    def slopes(z, _):
        for lo, n in ((0, 16), (16, 16), (32, 16)):
            _, dz, dx, dy = derivs(b0, b1, z, lo, n)
            for pair, d in (((bz0, bz1), dz), ((bx0, bx1), dx), ((by0, by1), dy)):
                for i in (0, 1):
                    pair[i][z, pl.ds(lo, n), :] = d[i]
        return 0

    lax.fori_loop(0, NZ, slopes, 0)
    clear(iv_ref)
    clear(ib_ref)
    cur, old = run_steps(
        0, (cm, cs), (om, os_), ((s0, s1), (b0, b1), (bz0, bz1), (bx0, bx1), (by0, by1)),
        fwd_ref, (iv_ref, ib_ref), place_ref, which_ref, count_ref, trace_ref, False,
    )
    rows = pl.ds(PAD + BX, BX)
    for f, (main, side) in enumerate((cur, old)):
        for q in range(4):
            total = jnp.zeros((BX, BY), jnp.float32)
            for j in range(4):
                z = 4 * q + j
                send_ref[NZ * f + z] = main[4 + z, rows, :]
                mine = (lane >= HY * j) & (lane < HY * (j + 1))
                total = jnp.where(mine, pltpu.roll(side[4 + z, rows, :], (16 + HY * j) % BY, 1), total)
            send_ref[32 + 4 * f + q] = total


def second_kernel(
    place_ref, which_ref, count_ref, trace_ref,
    centre_ref, low_ref, high_ref, fwd_ref, iv_ref, ib_ref,
    s0, s1, b0, b1, bz0, bz1, bx0, bx1, by0, by1,
    now_ref, prev_ref, images_ref,
    cm, cs, om, os_, iv, ib,
):
    lane = lane_of(BX)
    for ref in (cm, cs, om, os_):
        clear(ref)
    iv[...] = iv_ref[...]
    ib[...] = ib_ref[...]
    for block, ref in enumerate((low_ref, centre_ref, high_ref)):
        rows = pl.ds(PAD + block * BX, BX)
        for f, (main, side) in enumerate(((cm, cs), (om, os_))):
            for q in range(4):
                packed = ref[32 + 4 * f + q]
                for j in range(4):
                    z = 4 * q + j
                    main[4 + z, rows, :] = ref[NZ * f + z]
                    edge = pltpu.roll(packed, -(16 + HY * j) % BY, 1)
                    side[4 + z, rows, :] = jnp.where((lane < 16) | (lane >= BY - 16), edge, 0.0)
    cur, old = run_steps(
        ROUND, (cm, cs), (om, os_), ((s0, s1), (b0, b1), (bz0, bz1), (bx0, bx1), (by0, by1)),
        fwd_ref, (iv, ib), place_ref, which_ref, count_ref, trace_ref, True,
    )
    rows = pl.ds(PAD + BX, BX)
    for z in range(NZ):
        now_ref[z] = cur[0][4 + z, rows, :]
        prev_ref[z] = old[0][4 + z, rows, :]
        images_ref[z // 2, z % 2] = iv[z]
        images_ref[z // 2, 2 + z % 2] = ib[z]


def shape(*dims, dtype=jnp.float32):
    return jax.ShapeDtypeStruct(dims, dtype)


PARAMS = pltpu.CompilerParams(vmem_limit_bytes=32 * 1024 * 1024)


def swap(x, axis, pairs):
    return lax.ppermute(x, axis, [(a, b) for a, b in pairs] + [(b, a) for a, b in pairs])


def shards(velocity, buoyancy, fwd_field, adjoint_now, adjoint_prev, recv_cell, traces):
    now, prev, fwd = adjoint_now[0], adjoint_prev[0], fwd_field[0]
    gx, gy, shot = lax.axis_index("gx"), lax.axis_index("gy"), lax.axis_index("shot")
    where = jnp.stack([gx * BX, gy * BY, gy % 2, shot % 2]).astype(jnp.int32)
    count_y, count_x = lax.axis_size("gy"), lax.axis_size("gx")

    place, which, count = pl.pallas_call(
        find_kernel,
        out_shape=(shape(RECV + 8, dtype=jnp.int32), shape(RECV + 8, dtype=jnp.int32), shape(1, dtype=jnp.int32)),
        in_specs=[SM, SM],
        out_specs=(SM, SM, SM),
        name="find_receivers",
    )(where, recv_cell[0])

    own = jnp.concatenate([velocity, buoyancy], axis=0)
    half = lax.all_to_all(
        jnp.broadcast_to(own, (4,) + own.shape), "shot", 0, 0, axis_index_groups=[[0, 2, 4, 6], [1, 3, 5, 7]]
    ).reshape(16, BX, BY)

    first, second = pl.pallas_call(
        pack_kernel,
        out_shape=(shape(12, BX, BY), shape(12, BX, BY)),
        in_specs=[SM, VM, VM, VM],
        out_specs=(VM, VM),
        name="pack_sides",
    )(where, now, prev, half)
    first = swap(first, "gy", [(i, i + 1) for i in range(0, count_y, 2)])
    second = swap(second, "gy", [(i, i + 1) for i in range(1, count_y - 1, 2)])

    up = [(i, i + 1) for i in range(count_x - 1)]
    down = [(b, a) for a, b in up]
    centre = jnp.concatenate([now, prev, half, first, second], axis=0)
    low = lax.ppermute(centre, "gx", up)
    high = lax.ppermute(centre, "gx", down)

    model = jnp.concatenate(
        [part for block in (centre, low, high) for part in (block[32:48], block[56:60], block[68:72])], axis=0
    )
    other = lax.ppermute(model, "shot", [(i, i ^ 1) for i in range(SHOTS)])

    ext = shape(NZ, EXT, BY)
    pad = shape(LAYERS, ROWS, BY)
    scratch = [pltpu.VMEM((LAYERS, ROWS, BY), jnp.float32)] * 4
    image = shape(NZ, BX, BY)
    outs = pl.pallas_call(
        first_kernel,
        out_shape=(shape(40, BX, BY), image, image, ext, ext, pad, pad) + (ext,) * 6,
        in_specs=[SM] * 5 + [VM] * 5,
        out_specs=(VM,) * 13,
        scratch_shapes=scratch,
        compiler_params=PARAMS,
        name="first_steps",
    )(where, place, which, count, traces[0], centre, low, high, other, fwd[:ROUND])
    send, iv, ib, coefs = outs[0], outs[1], outs[2], outs[3:]
    low = lax.ppermute(send, "gx", up)
    high = lax.ppermute(send, "gx", down)
    now, prev, images = pl.pallas_call(
        second_kernel,
        out_shape=(image, image, shape(SHOTS, 4, BX, BY)),
        in_specs=[SM] * 4 + [VM] * 16,
        out_specs=(VM,) * 3,
        scratch_shapes=scratch + [pltpu.VMEM((NZ, BX, BY), jnp.float32)] * 2,
        compiler_params=PARAMS,
        name="second_steps",
    )(place, which, count, traces[0], send, low, high, fwd[ROUND:], iv, ib, *coefs)
    parts = jnp.sum(lax.all_to_all(images, "shot", 0, 0), axis=0)
    scale = 1.0 / (SHOTS * STEPS) ** 0.5
    grad_vel = 2.0 * courant * velocity * parts[:2] * scale
    grad_buoy = courant * velocity * velocity * parts[2:] * scale
    return grad_vel, grad_buoy, now[None], prev[None]


def solution(mesh):
    return jax.shard_map(
        shards,
        mesh=mesh,
        in_specs=(
            P("shot", "gx", "gy"),
            P("shot", "gx", "gy"),
            P("shot", None, None, "gx", "gy"),
            P("shot", None, "gx", "gy"),
            P("shot", None, "gx", "gy"),
            P("shot", None),
            P("shot", None, None),
        ),
        out_specs=(
            P("shot", "gx", "gy"),
            P("shot", "gx", "gy"),
            P("shot", None, "gx", "gy"),
            P("shot", None, "gx", "gy"),
        ),
        check_vma=False,
    )
```

time: 554 us -> 126 us (0.23)
  waiting for transfers between devices: 215 us -> 35.3 us
  other arithmetic: 152 us -> 2.04 us
  starting transfers between devices: 132 us -> 34.1 us
  Pallas kernels: 0 us -> 37.1 us
  blocking collectives: 29.1 us -> 12.2 us
  between operations: 15 us -> 0.88 us
    scatter-add x8 -> x0, other arithmetic: 130 us -> none  [shards(): now_pad.at[shot_ids, depth_idx, local_x, local_y]]
    ppermute x36 -> x7, waiting for transfers between devices: 139 us -> 30.2 us  [the longest x1 10.6 us: shards(): low = lax.ppermute(centre, 'gx', up)]
    ppermute x36 -> x7, starting transfers between devices: 132 us -> 28 us  [the longest x2 9.75 us: swap(): lax.ppermute(x, axis, [(a, b) for a, b in pairs] + [(b, a) for a, b in pa...]
    reduce_scatter x2 -> x0, waiting for transfers between devices: 75.2 us -> none  [the longest x1 42.3 us: shards(): lax.psum_scatter(image_b, 'shot', scatter_dimension=0, tiled=True)]
    pallas_call x0 -> x4, Pallas kernels: none -> 37.1 us  [the longest x1 16.7 us: shards(): pl.pallas_call(first_kernel, out_shape=(shape(40, BX, BY), image, image,...]
    all_gather x2 -> x0, blocking collectives: 29.1 us -> none  [the longest x1 14.9 us: shards(): lax.all_gather(buoyancy, 'shot', axis=0, tiled=True)]
    add x11 -> x0, other arithmetic: 16.9 us -> none  [the longest x8 15.4 us: shards(): 2.0 * centre - crop(prev, excess) + crop(speed_wide, offset) * operated]
    all_to_all x0 -> x1, blocking collectives: none -> 12.2 us  [shards(): parts = jnp.sum(lax.all_to_all(images, 'shot', 0, 0), axis=0)]
  transfers between devices with their start and end apart: 38 -> 8, of which waited for: 24 -> 6; matrix products, arithmetic and copies ran while one was open for 3% -> 1% of each run, Pallas kernels for 0% -> 4%
where the time goes in v1:
time: 126 us
  Pallas kernels  37.1 us (29%)
  waiting for transfers between devices  35.3 us (28%)
  starting transfers between devices  34.1 us (27%)
  blocking collectives  12.2 us (10%)
  local copies, waits for them, and re-layouts  3.96 us (3%)
  other arithmetic  2.04 us (2%)
    pallas_call x1, Pallas kernels, shards(): pl.pallas_call(first_kernel, out_shape=(shape(40, BX, BY), image, image,...  16.7 us
    pallas_call x1, Pallas kernels, shards(): pl.pallas_call(second_kernel, out_shape=(image, image, shape(SHOTS, 4, BX...  13.6 us
    all_to_all x1, blocking collectives, shards(): parts = jnp.sum(lax.all_to_all(images, 'shot', 0, 0), axis=0)  12.2 us
    ppermute x1, waiting for transfers between devices, shards(): low = lax.ppermute(centre, 'gx', up)  10.6 us
    ppermute x2, starting transfers between devices, swap(): lax.ppermute(x, axis, [(a, b) for a, b in pairs] + [(b, a) for a, b in pa...  9.75 us
    ppermute x1, starting transfers between devices, shards(): high = lax.ppermute(send, 'gx', down)  6.37 us
    ppermute x1, waiting for transfers between devices, shards(): low = lax.ppermute(send, 'gx', up)  6.21 us
    ppermute x2, waiting for transfers between devices, swap(): lax.ppermute(x, axis, [(a, b) for a, b in pairs] + [(b, a) for a, b in pa...  6.16 us
  transfers between devices with their start and end apart: 8, of which 6 were waited for; matrix products, arithmetic and copies ran while one was open for 1% of the time, Pallas kernels for 4%

profile of v1, /device:TPU:6, one launch (start us, length us, event | category | flops | bytes accessed | tf_op | source)
XLA Modules:
  0.0 125.6 jit_solution(3681466852076076492)
XLA Ops:
  0.6 0.7 pad_maximum_fusion
  1.4 0.7 broadcast_in_dim.9
  2.0 6.0 %all-to-all-start = ((f32[4,4,16,128]{3,2,1,0:T(8,128)}), f32[4,4,16,128]{3,2,1,0:T(8,128)S(1)}, u32[]{:S(2)}, u32[]{:S(2)}) async-start(f32[4,4,16,128]{3,2,1,0:T(8,128)} %broadcast_in_dim.9), calls=%async_computation | async-start | bytes 262144 | tf_op jit(solution)/shard_map/all_to_all | solution.py:291
  8.1 0.7 pad_add_fusion.where_ref
  9.0 5.2 %all-to-all-done = f32[4,4,16,128]{3,2,1,0:T(8,128)S(1)} async-done(((f32[4,4,16,128]{3,2,1,0:T(8,128)}), f32[4,4,16,128]{3,2,1,0:T(8,128)S(1)}, u32[]{:S(2)}, u32[]{:S(2)}) %all-to-all-start) | async-done | bytes 131104 | tf_op jit(solution)/shard_map/all_to_all | solution.py:291
  14.8 1.9 %pack_sides.1 = (f32[12,16,128]{2,1,0:T(8,128)}, f32[12,16,128]{2,1,0:T(8,128)}) custom-call(s32[4]{0:T(128)} %pad_add_fusion.where_ref, f32[16,16,128]{2,1,0:T(8,128)} %bitcast.21, f32[16,16,128]{2,1,0:T(8,128)} %bitcast.22, f32[16,16,128]{2,1,0:T(8,128)} %bitcast.19), custom_call_target="tpu_custom_call" | custom-call | tf_op jit(solution)/shard_map/pack_sides/pallas_call | solution.py:295
  16.7 9.1 %collective-permute-start = (f32[12,16,128]{2,1,0:T(8,128)}, f32[12,16,128]{2,1,0:T(8,128)S(1)}, u32[]{:S(2)}, u32[]{:S(2)}) collective-permute-start(f32[12,16,128]{2,1,0:T(8,128)} %get-tuple-element.28), channel_id=1, source_target_pairs={{0,1},{2,3},{1,0},{3,2},{4,5},{6,7},{5,4},{7,6},{8,9},{10,11},{9,8... | collective-permute-start | bytes 294920 | tf_op jit(solution)/shard_map/ppermute | solution.py:273
  25.8 0.7 collective-permute-start.1
  26.5 0.9 constant_dynamic-update-slice_fusion.5
  27.4 6.2 %collective-permute-done = f32[12,16,128]{2,1,0:T(8,128)S(1)} collective-permute-done((f32[12,16,128]{2,1,0:T(8,128)}, f32[12,16,128]{2,1,0:T(8,128)S(1)}, u32[]{:S(2)}, u32[]{:S(2)}) %collective-permute-start) | collective-permute-done | bytes 98336 | tf_op jit(solution)/shard_map/ppermute | solution.py:273
  33.6 3.6 %collective-permute-start.2 = (f32[72,16,128]{2,1,0:T(8,128)S(1)}, f32[72,16,128]{2,1,0:T(8,128)S(1)}, u32[]{:S(2)}, u32[]{:S(2)}) collective-permute-start(f32[72,16,128]{2,1,0:T(8,128)S(1)} %constant_dynamic-update-slice_fusion.centre_ref), channel_id=1, source_target_pairs={{0,4},{4,8},{8,12},{12,16},{16,20},{20,24},{24,28},{28,32},{32,36}... | collective-permute-start | bytes 1769480 | tf_op jit(solution)/shard_map/ppermute | solution.py:308
  37.3 4.5 %collective-permute-start.3 = (f32[72,16,128]{2,1,0:T(8,128)S(1)}, f32[72,16,128]{2,1,0:T(8,128)S(1)}, u32[]{:S(2)}, u32[]{:S(2)}) collective-permute-start(f32[72,16,128]{2,1,0:T(8,128)S(1)} %constant_dynamic-update-slice_fusion.centre_ref), channel_id=1, source_target_pairs={{4,0},{8,4},{12,8},{16,12},{20,16},{24,20},{28,24},{32,28},{36,32}... | collective-permute-start | bytes 1769480 | tf_op jit(solution)/shard_map/ppermute | solution.py:309
  41.8 10.6 %collective-permute-done.2.low_ref = f32[72,16,128]{2,1,0:T(8,128)S(1)} collective-permute-done((f32[72,16,128]{2,1,0:T(8,128)S(1)}, f32[72,16,128]{2,1,0:T(8,128)S(1)}, u32[]{:S(2)}, u32[]{:S(2)}) %collective-permute-start.2) | collective-permute-done | bytes 589856 | tf_op jit(solution)/shard_map/ppermute | solution.py:308
  52.4 1.1 collective-permute-done.3.high_ref
  53.6 1.9 %collective-permute-start.4 = (f32[72,16,128]{2,1,0:T(8,128)S(1)}, f32[72,16,128]{2,1,0:T(8,128)S(1)}, u32[]{:S(2)}, u32[]{:S(2)}) collective-permute-start(f32[72,16,128]{2,1,0:T(8,128)S(1)} %slice_dynamic-update-slice_fusion.2), channel_id=1, source_target_pairs={{0,64},{64,0},{128,192},{192,128},{256,320},{320,256},{384,448},{4... | collective-permute-start | bytes 1769480 | tf_op jit(solution)/shard_map/ppermute | solution.py:314
  55.5 4.8 %find_receivers.1 = (s32[264]{0:T(512)}, s32[264]{0:T(512)}, s32[1]{0:T(128)}) custom-call(s32[4]{0:T(128)} %pad_add_fusion.where_ref, s32[256]{0:T(256)} %bitcast.25), custom_call_target="tpu_custom_call" | custom-call | tf_op jit(solution)/shard_map/find_receivers/pallas_call | solution.py:282
  61.1 16.7 %first_steps.1 = (f32[40,16,128]{2,1,0:T(8,128)S(1)}, f32[16,16,128]{2,1,0:T(8,128)S(1)}, f32[16,16,128]{2,1,0:T(8,128)S(1)}, f32[16,48,128]{2,1,0:T(8,128)S(1)}...) custom-call(s32[4]{0:T(128)S(1)} %copy-done.3, ...), custom_call_target="tpu_custom_call" | custom-call | tf_op jit(solution)/shard_map/first_steps/pallas_call | solution.py:320
  77.8 6.4 %collective-permute-start.6 = (f32[40,16,128]{2,1,0:T(8,128)S(1)}, f32[40,16,128]{2,1,0:T(8,128)S(1)}, u32[]{:S(2)}, u32[]{:S(2)}) collective-permute-start(f32[40,16,128]{2,1,0:T(8,128)S(1)} %get-tuple-element.30.centre_ref), channel_id=1, source_target_pairs={{4,0},{8,4},{12,8},{16,12},{20,16},{24,20},{28,24},{32,28},{36,32}... | collective-permute-start | bytes 983048 | tf_op jit(solution)/shard_map/ppermute | solution.py:331
  84.2 1.9 %collective-permute-start.5 = (f32[40,16,128]{2,1,0:T(8,128)S(1)}, f32[40,16,128]{2,1,0:T(8,128)S(1)}, u32[]{:S(2)}, u32[]{:S(2)}) collective-permute-start(f32[40,16,128]{2,1,0:T(8,128)S(1)} %get-tuple-element.30.centre_ref), channel_id=1, source_target_pairs={{0,4},{4,8},{8,12},{12,16},{16,20},{20,24},{24,28},{28,32},{32,36}... | collective-permute-start | bytes 983048 | tf_op jit(solution)/shard_map/ppermute | solution.py:330
  86.1 6.1 %collective-permute-done.6.high_ref = f32[40,16,128]{2,1,0:T(8,128)S(1)} collective-permute-done((f32[40,16,128]{2,1,0:T(8,128)S(1)}, f32[40,16,128]{2,1,0:T(8,128)S(1)}, u32[]{:S(2)}, u32[]{:S(2)}) %collective-permute-start.6) | collective-permute-done | bytes 327712 | tf_op jit(solution)/shard_map/ppermute | solution.py:331
  92.2 6.2 %collective-permute-done.5.low_ref = f32[40,16,128]{2,1,0:T(8,128)S(1)} collective-permute-done((f32[40,16,128]{2,1,0:T(8,128)S(1)}, f32[40,16,128]{2,1,0:T(8,128)S(1)}, u32[]{:S(2)}, u32[]{:S(2)}) %collective-permute-start.5) | collective-permute-done | bytes 327712 | tf_op jit(solution)/shard_map/ppermute | solution.py:330
  98.4 13.6 %second_steps.1 = (f32[16,16,128]{2,1,0:T(8,128)}, f32[16,16,128]{2,1,0:T(8,128)}, f32[8,4,16,128]{3,2,1,0:T(8,128)S(1)}) custom-call(s32[264]{0:T(512)S(1)} %copy-done.1, s32[264]{0:T(512)S(1)} %copy-done.2, s32[1]{0:T(128)} %get-tuple-element.27.count_ref, f32[8,256]{1,0:T(8,128)S(1)} %bitcast.18, f32[40,16,128]{2,1,0:T(8,128)S(1)} %get-tuple-element.30.centre_ref, ...), custom_call_target="tpu_custom_call" | custom-call | tf_op jit(solution)/shard_map/second_steps/pallas_call | solution.py:332
  112.0 12.2 %all_to_all.10 = f32[8,4,16,128]{3,2,1,0:T(8,128)S(1)} all-to-all(f32[8,4,16,128]{3,2,1,0:T(8,128)S(1)} %get-tuple-element.43), channel_id=1, replica_groups=mesh['shot'=8,'gx'=16,'gy'=4] {'shot'}, dimensions={0} | all-to-all | bytes 524288 | tf_op jit(solution)/shard_map/all_to_all | solution.py:341
  124.2 0.7 copy-done.8
  (34 shorter events, 2.3 us)
Async XLA Ops:
  2.0 6.0 %copy-start.6 = (f32[1,16,16,128]{3,2,1,0:T(8,128)S(1)}, f32[1,16,16,128]{3,2,1,0:T(8,128)}, u32[]{:S(2)}) copy-start(f32[1,16,16,128]{3,2,1,0:T(8,128)} %param.10) | copy-start | bytes 393220
  2.0 12.1 %all-to-all-start = ((f32[4,4,16,128]{3,2,1,0:T(8,128)}), f32[4,4,16,128]{3,2,1,0:T(8,128)S(1)}, u32[]{:S(2)}, u32[]{:S(2)}) async-start(f32[4,4,16,128]{3,2,1,0:T(8,128)} %broadcast_in_dim.9), calls=%async_computation | async-start | bytes 262144 | tf_op jit(solution)/shard_map/all_to_all | solution.py:291
  8.1 0.9 copy-start.7
  14.1 0.7 copy-start.4
  16.7 16.9 %collective-permute-start = (f32[12,16,128]{2,1,0:T(8,128)}, f32[12,16,128]{2,1,0:T(8,128)S(1)}, u32[]{:S(2)}, u32[]{:S(2)}) collective-permute-start(f32[12,16,128]{2,1,0:T(8,128)} %get-tuple-element.28), channel_id=1, source_target_pairs={{0,1},{2,3},{1,0},{3,2},{4,5},{6,7},{5,4},{7,6},{8,9},{10,11},{9,8... | collective-permute-start | bytes 294920 | tf_op jit(solution)/shard_map/ppermute | solution.py:273
  25.8 7.8 %collective-permute-start.1 = (f32[12,16,128]{2,1,0:T(8,128)}, f32[12,16,128]{2,1,0:T(8,128)S(1)}, u32[]{:S(2)}, u32[]{:S(2)}) collective-permute-start(f32[12,16,128]{2,1,0:T(8,128)} %get-tuple-element.29), channel_id=1, source_target_pairs={{1,2},{2,1},{5,6},{6,5},{9,10},{10,9},{13,14},{14,13},{17,18},{18,... | collective-permute-start | bytes 294920 | tf_op jit(solution)/shard_map/ppermute | solution.py:273
  33.6 26.7 %copy-start.5 = (bf16[1,8,16,16,128]{4,3,2,1,0:T(8,128)(2,1)S(1)}, bf16[1,8,16,16,128]{4,3,2,1,0:T(8,128)(2,1)}, u32[]{:S(2)}) copy-start(bf16[1,8,16,16,128]{4,3,2,1,0:T(8,128)(2,1)} %param.9) | copy-start | bytes 1572868
  33.6 18.7 %collective-permute-start.2 = (f32[72,16,128]{2,1,0:T(8,128)S(1)}, f32[72,16,128]{2,1,0:T(8,128)S(1)}, u32[]{:S(2)}, u32[]{:S(2)}) collective-permute-start(f32[72,16,128]{2,1,0:T(8,128)S(1)} %constant_dynamic-update-slice_fusion.centre_ref), channel_id=1, source_target_pairs={{0,4},{4,8},{8,12},{12,16},{16,20},{20,24},{24,28},{28,32},{32,36}... | collective-permute-start | bytes 1769480 | tf_op jit(solution)/shard_map/ppermute | solution.py:308
  37.3 16.3 %collective-permute-start.3 = (f32[72,16,128]{2,1,0:T(8,128)S(1)}, f32[72,16,128]{2,1,0:T(8,128)S(1)}, u32[]{:S(2)}, u32[]{:S(2)}) collective-permute-start(f32[72,16,128]{2,1,0:T(8,128)S(1)} %constant_dynamic-update-slice_fusion.centre_ref), channel_id=1, source_target_pairs={{4,0},{8,4},{12,8},{16,12},{20,16},{24,20},{28,24},{32,28},{36,32}... | collective-permute-start | bytes 1769480 | tf_op jit(solution)/shard_map/ppermute | solution.py:309
  53.6 6.8 %collective-permute-start.4 = (f32[72,16,128]{2,1,0:T(8,128)S(1)}, f32[72,16,128]{2,1,0:T(8,128)S(1)}, u32[]{:S(2)}, u32[]{:S(2)}) collective-permute-start(f32[72,16,128]{2,1,0:T(8,128)S(1)} %slice_dynamic-update-slice_fusion.2), channel_id=1, source_target_pairs={{0,64},{64,0},{128,192},{192,128},{256,320},{320,256},{384,448},{4... | collective-permute-start | bytes 1769480 | tf_op jit(solution)/shard_map/ppermute | solution.py:314
  60.3 0.7 copy-start.1
  60.3 0.7 copy-start.2
  60.4 0.7 copy-start
  60.4 0.7 copy-start.3
  77.8 14.4 %collective-permute-start.6 = (f32[40,16,128]{2,1,0:T(8,128)S(1)}, f32[40,16,128]{2,1,0:T(8,128)S(1)}, u32[]{:S(2)}, u32[]{:S(2)}) collective-permute-start(f32[40,16,128]{2,1,0:T(8,128)S(1)} %get-tuple-element.30.centre_ref), channel_id=1, source_target_pairs={{4,0},{8,4},{12,8},{16,12},{20,16},{24,20},{28,24},{32,28},{36,32}... | collective-permute-start | bytes 983048 | tf_op jit(solution)/shard_map/ppermute | solution.py:331
  84.2 14.2 %collective-permute-start.5 = (f32[40,16,128]{2,1,0:T(8,128)S(1)}, f32[40,16,128]{2,1,0:T(8,128)S(1)}, u32[]{:S(2)}, u32[]{:S(2)}) collective-permute-start(f32[40,16,128]{2,1,0:T(8,128)S(1)} %get-tuple-element.30.centre_ref), channel_id=1, source_target_pairs={{0,4},{4,8},{8,12},{12,16},{16,20},{20,24},{24,28},{28,32},{32,36}... | collective-permute-start | bytes 983048 | tf_op jit(solution)/shard_map/ppermute | solution.py:330
  124.2 0.7 copy-start.8

commit v2 on v0

v2 whole, which is shorter than its diff:
```python
import functools

import jax
import jax.numpy as jnp
from jax import lax
from jax.experimental import pallas as pl
from jax.experimental.pallas import tpu as pltpu
from jax.sharding import PartitionSpec as P

NZ, BX, BY = 16, 16, 128
FULL_X, FULL_Y = 256, 512
STEPS, SHOTS, RECV = 8, 8, 256
ROUND = 4
HY = 32
EXT = 3 * BX
PAD = 8
ROWS = EXT + 2 * PAD
LAYERS = NZ + 8
FAR = BY - HY
IMG = BX + 8

second_coef = (-205.0 / 72.0, 8.0 / 5.0, -1.0 / 5.0, 8.0 / 315.0, -1.0 / 560.0)
first_coef = (4.0 / 5.0, -1.0 / 5.0, 4.0 / 105.0, -1.0 / 280.0)
courant = 0.15
lap_unit = second_coef[4]
slope_unit = first_coef[3]
lap_ratio = (3.0 * second_coef[0] / lap_unit,) + tuple(c / lap_unit for c in second_coef[1:4])
slope_ratio = tuple(c / slope_unit for c in first_coef[:3])

VM = pl.BlockSpec(memory_space=pltpu.VMEM)
SM = pl.BlockSpec(memory_space=pltpu.SMEM)


def side_planes(groups):
    return NZ // groups + 8


def lane_of(rows):
    return lax.broadcasted_iota(jnp.int32, (rows, BY), 1)


def roll(x, shift):
    shift %= BY
    return pltpu.roll(x, shift, 1) if shift else x


def find_kernel(where_ref, recv_ref, place_ref, place4_ref, which_ref, count_ref):
    base_x = where_ref[0] - BX
    base_y = where_ref[1]

    def body(j, count):
        cell = recv_ref[j]
        z = lax.shift_right_logical(cell, 17)
        x = (lax.shift_right_logical(cell, 9) & (FULL_X - 1)) - base_x
        y = (cell & (FULL_Y - 1)) - base_y
        inside = (x >= 0) & (x < EXT) & (y >= -HY) & (y < BY + HY)
        main = (y >= 0) & (y < BY)
        right = y >= BY
        row = (x & 63) + PAD
        plane = jnp.where(main, z + 4, LAYERS + 4 + (z & 7))
        lane = jnp.where(main, y, lax.shift_right_logical(z, 3) * 64 + jnp.where(right, y - BY, y + 64))
        place_ref[count] = (plane * 64 + row) * 256 + (lane & 255)
        near = (y >= -16) & (y < BY + 16)
        plane = jnp.where(main, z + 4, LAYERS + 4 + (z & 3))
        lane = jnp.where(main, y, lax.shift_right_logical(z, 2) * 32 + jnp.where(right, y - BY, y + 32))
        lane = jnp.where(near, lane, 255)
        place4_ref[count] = (plane * 64 + row) * 256 + (lane & 255)
        which_ref[count] = j
        return count + inside.astype(jnp.int32)

    count_ref[0] = lax.fori_loop(0, RECV, body, jnp.int32(0))


def pack_kernel(where_ref, fields_ref, model_ref, first_ref, second_ref):
    even = where_ref[2] == 0
    lane = lane_of(BX)
    out = 0
    for ref in (fields_ref, model_ref):
        for base in range(0, ref.shape[0], NZ):
            for q in range(4):
                right = left = None
                for i in range(4):
                    plane = ref[base + q + 4 * i]
                    j = i ^ 1
                    a, b = roll(plane, HY * j - FAR), roll(plane, HY * i)
                    right = a if right is None else jnp.where((lane >= HY * j) & (lane < HY * (j + 1)), a, right)
                    left = b if left is None else jnp.where((lane >= HY * i) & (lane < HY * (i + 1)), b, left)
                first_ref[out] = jnp.where(even, right, left)
                second_ref[out] = jnp.where(even, left, right)
                out += 1


def side_pair(first, second, even, lane):
    right = jnp.where(even, first, second)
    left = jnp.where(even, second, first)
    is_right = (lane & 63) < HY
    return (
        jnp.where(is_right, right, left),
        jnp.where(is_right, roll(right, -HY), roll(left, HY)),
    )


def four_from_two(near, far, lane):
    inner = (lane & 31) < 16
    own = (lane & 63) < 32
    return jnp.where(
        inner, jnp.where(own, near, roll(far, 32)), jnp.where(own, roll(near, -32), far)
    )


def repeat_sides(ref, groups):
    per = NZ // groups
    w = BY // groups
    rows = pl.ds(PAD, EXT)
    lane = lane_of(EXT)
    at = LAYERS + 4
    for i in range(4):
        after = roll(ref[at + i, rows, :], -w)
        ref[at + per + i, rows, :] = jnp.where(lane < BY - w, after, 0.0)
        before = roll(ref[at + per - 4 + i, rows, :], w)
        ref[at - 4 + i, rows, :] = jnp.where(lane >= w, before, 0.0)


def clear_ends(ref):
    for z in (0, 1, 2, 3, NZ + 4, NZ + 5, NZ + 6, NZ + 7):
        ref[z] = jnp.zeros(ref.shape[1:], jnp.float32)


def clear(ref):
    def body(z, _):
        ref[z] = jnp.zeros(ref.shape[1:], jnp.float32)
        return 0

    lax.fori_loop(0, ref.shape[0], body, 0)


def derivs(ref, at, row, n, here, edges, lane, width, lap_too=True):
    inner = lane & (width - 1)
    lap = lap_ratio[0] * here if lap_too else None
    dz = dx = dy = None
    for k in (4, 3, 2, 1):
        up = roll(jnp.where(inner < k, edges, here), -k)
        down = roll(jnp.where(inner >= width - k, edges, here), k)
        zp = ref[at + k, pl.ds(row, n), :]
        zm = ref[at - k, pl.ds(row, n), :]
        xp = ref[at, pl.ds(row + k, n), :]
        xm = ref[at, pl.ds(row - k, n), :]
        if lap_too:
            both = ((zp + zm) + (xp + xm)) + (up + down)
            lap = lap + (both if k == 4 else lap_ratio[k] * both)
        if k == 4:
            dz, dx, dy = zp - zm, xp - xm, up - down
        else:
            c = slope_ratio[k - 1]
            dz, dx, dy = dz + c * (zp - zm), dx + c * (xp - xm), dy + c * (up - down)
    return lap, dz, dx, dy


def group_derivs(ref, p, lo, n, groups, sides=True, lap_too=True):
    per = NZ // groups
    w = BY // groups
    lane = lane_of(n)
    row = PAD + lo
    spot = pl.ds(row, n)
    side_at = LAYERS + 4 + p
    side = ref[side_at, spot, :]
    mains = [ref[4 + p + g * per, spot, :] for g in range(groups)]
    for g in range(groups):
        edges = jnp.where(lane < 64, roll(side, -g * w), roll(side, -(g + 1) * w))
        at = 4 + p + g * per
        yield 0, p + g * per, at, mains[g], derivs(ref, at, row, n, mains[g], edges, lane, BY, lap_too)
    if sides:
        edges = None
        for g in range(groups):
            first = roll(mains[(g - 1) % groups], g * w)
            last = roll(mains[(g + 1) % groups], (g + 1) * w)
            for start, value in ((g * w, first), (g * w + w // 2, last)):
                edges = value if edges is None else jnp.where(lane >= start, value, edges)
        yield 1, p, side_at, side, derivs(ref, side_at, row, n, side, edges, lane, w, lap_too)


PLANS = ((4, 12, 20, 28, 36), (8, 16, 24, 32), (12, 20, 28), (16, 24))


def run_steps(first_step, groups, cur, old, coefs, fwd_ref, image, place_ref, which_ref, count_ref, trace_ref, last):
    lane1 = lane_of(1)
    for j, plan in enumerate(PLANS):

        def add(i, _, cur=cur, step=first_step + j):
            place = place_ref[i]
            value = trace_ref[step, which_ref[i]]
            spot = (lax.shift_right_logical(place, 14), pl.ds(lax.shift_right_logical(place, 8) & 63, 1), slice(None))
            cur[spot] = cur[spot] + jnp.where(lane1 == (place & 255), value, 0.0)
            return 0

        lax.fori_loop(0, count_ref[0], add, 0)
        repeat_sides(cur, groups)
        sides = not (last and j == ROUND - 1)

        def layers(p, _, cur=cur, old=old, plan=plan, j=j, sides=sides):
            for lo in plan:
                rows = pl.ds(lo, 8)
                for kind, z, at, here, found in group_derivs(cur, p, lo, 8, groups, sides):
                    terms = [coefs[c][kind][z, rows, :] * found[c] for c in range(4)]
                    change = (terms[0] + terms[1]) + (terms[2] + terms[3])
                    spot = (at, pl.ds(PAD + lo, 8), slice(None))
                    old[spot] = ((here + here) - old[spot]) + change
                    if kind == 0 and BX - 8 < lo < 2 * BX:
                        seen = pl.ds(lo - (BX - 4), 8)
                        snapshot = fwd_ref[j, z, seen, :]
                        image[0][z, seen, :] += snapshot * change
                        image[1][z, seen, :] += snapshot * found[0]
            return 0

        lax.fori_loop(0, NZ // groups, layers, 0)
        cur, old = old, cur
    return cur, old


def widen(fwd_ref, wide_ref):
    for step in range(ROUND):

        def body(z, _, step=step):
            wide_ref[step, z, pl.ds(4, BX), :] = fwd_ref[step, z].astype(jnp.float32)
            return 0

        lax.fori_loop(0, NZ, body, 0, unroll=4)


def first_kernel(
    where_ref, place_ref, which_ref, count_ref, trace_ref,
    centre_ref, low_ref, high_ref, centre_fields, low_fields, high_fields, other_ref, fwd_ref,
    send_ref, iv_ref, ib_ref, m0, m1, m2, m3, f0, f1, f2, f3,
    cur, old, buoy, speed, speed_side, t0, t1, t2, t3, wide,
):
    even = where_ref[2] == 0
    core = where_ref[3]
    lane = lane_of(BX)
    for ref in (cur, old, buoy):
        clear_ends(ref)
    clear(iv_ref)
    clear(ib_ref)
    widen(fwd_ref, wide)
    at = LAYERS + 4
    blocks = ((low_ref, low_fields), (centre_ref, centre_fields), (high_ref, high_fields))
    for block, (ref, fields) in enumerate(blocks):
        rows = pl.ds(PAD + block * BX, BX)
        bare = pl.ds(block * BX, BX)
        for f, field in enumerate((cur, old)):
            for z in range(NZ):
                field[4 + z, rows, :] = fields[NZ * f + z]
            for q in range(4):
                near, far = side_pair(ref[16 + 4 * f + q], ref[28 + 4 * f + q], even, lane)
                field[at + q, rows, :] = near
                field[at + q + 4, rows, :] = far
        for half in (0, 1):
            turn = core if half == 0 else 1 - core
            spot = (1, 0, 2)[block]
            for t in range(4):
                z = 2 * turn + t % 2
                if half == 0:
                    planes = [ref[4 * i + t] for i in range(4)]
                    packs = ref[24 + t], ref[36 + t]
                else:
                    planes = [other_ref[24 * spot + 4 * i + t] for i in range(4)]
                    packs = other_ref[24 * spot + 16 + t], other_ref[24 * spot + 20 + t]
                pair = side_pair(*packs, even, lane)
                if t < 2:
                    for i in range(4):
                        speed[z + 4 * i, bare, :] = courant * planes[i] * planes[i]
                    for i in range(2):
                        speed_side[z + 4 * i, bare, :] = courant * pair[i] * pair[i]
                else:
                    for i in range(4):
                        buoy[4 + z + 4 * i, rows, :] = planes[i]
                    for i in range(2):
                        buoy[at + z + 4 * i, rows, :] = pair[i]
    repeat_sides(buoy, 2)
    coefs = ((m0, t0), (m1, t1), (m2, t2), (m3, t3))

    def slopes(p, _):
        for lo in PLANS[0]:
            rows = pl.ds(lo, 8)
            for kind, z, _, here, found in group_derivs(buoy, p, lo, 8, 2, lap_too=False):
                pace = (speed, speed_side)[kind][z, rows, :]
                coefs[0][kind][z, rows, :] = (lap_unit * pace) * here
                steep = (slope_unit * slope_unit) * pace
                for c in (1, 2, 3):
                    coefs[c][kind][z, rows, :] = steep * found[c]
        return 0

    lax.fori_loop(0, NZ // 2, slopes, 0)
    lane8 = lane_of(8)
    for wide_side, side in ((t0, f0), (t1, f1), (t2, f2), (t3, f3)):
        for p in range(4):
            for lo in PLANS[0]:
                rows = pl.ds(lo, 8)
                side[p, rows, :] = four_from_two(wide_side[p, rows, :], wide_side[p + 4, rows, :], lane8)
    now, prev = run_steps(
        0, 2, cur, old, coefs, wide, (iv_ref, ib_ref), place_ref, which_ref, count_ref, trace_ref, False
    )
    rows = pl.ds(PAD + BX, BX)
    for f, field in enumerate((now, prev)):
        for z in range(NZ):
            send_ref[NZ * f + z] = field[4 + z, rows, :]
        for p in range(4):
            send_ref[2 * NZ + 4 * f + p] = four_from_two(field[at + p, rows, :], field[at + p + 4, rows, :], lane)


def second_kernel(
    place_ref, which_ref, count_ref, trace_ref,
    centre_ref, low_ref, high_ref, fwd_ref, iv_ref, ib_ref, m0, m1, m2, m3, f0, f1, f2, f3,
    now_ref, prev_ref, images_ref,
    cur, old, iv, ib, wide,
):
    for ref in (cur, old):
        clear_ends(ref)
    clear(iv)
    clear(ib)
    widen(fwd_ref, wide)
    at = LAYERS + 4
    for block, ref in enumerate((low_ref, centre_ref, high_ref)):
        rows = pl.ds(PAD + block * BX, BX)
        for f, field in enumerate((cur, old)):
            for z in range(NZ):
                field[4 + z, rows, :] = ref[NZ * f + z]
            for p in range(4):
                field[at + p, rows, :] = ref[2 * NZ + 4 * f + p]
    now, prev = run_steps(
        ROUND, 4, cur, old, ((m0, f0), (m1, f1), (m2, f2), (m3, f3)), wide, (iv, ib),
        place_ref, which_ref, count_ref, trace_ref, True,
    )
    rows = pl.ds(PAD + BX, BX)
    wanted = pl.ds(4, BX)
    for z in range(NZ):
        now_ref[z] = now[4 + z, rows, :]
        prev_ref[z] = prev[4 + z, rows, :]
        images_ref[z // 2, z % 2] = iv[z, wanted, :] + iv_ref[z, wanted, :]
        images_ref[z // 2, 2 + z % 2] = ib[z, wanted, :] + ib_ref[z, wanted, :]


def shape(*dims, dtype=jnp.float32):
    return jax.ShapeDtypeStruct(dims, dtype)


def room(mib):
    return pltpu.CompilerParams(vmem_limit_bytes=mib * 1024 * 1024)


PARAMS = room(32)


def buffer(*dims):
    return pltpu.VMEM(dims, jnp.float32)


def steps_one(*operands):
    ext, side_ext = shape(NZ, EXT, BY), shape(NZ // 4, EXT, BY)
    image = shape(NZ, IMG, BY)
    block = LAYERS + side_planes(2)
    return pl.pallas_call(
        first_kernel,
        out_shape=(shape(40, BX, BY), image, image) + (ext,) * 4 + (side_ext,) * 4,
        in_specs=[SM] * 5 + [VM] * 8,
        out_specs=(VM,) * 11,
        scratch_shapes=[buffer(block, ROWS, BY)] * 3
        + [buffer(NZ, EXT, BY)]
        + [buffer(NZ // 2, EXT, BY)] * 5
        + [buffer(ROUND, NZ, IMG, BY)],
        compiler_params=PARAMS,
        name="first_steps",
    )(*operands)


def steps_two(*operands):
    block = LAYERS + side_planes(4)
    return pl.pallas_call(
        second_kernel,
        out_shape=(shape(NZ, BX, BY), shape(NZ, BX, BY), shape(SHOTS, 4, BX, BY)),
        in_specs=[SM] * 4 + [VM] * 14,
        out_specs=(VM,) * 3,
        scratch_shapes=[buffer(block, ROWS, BY)] * 2 + [buffer(NZ, IMG, BY)] * 2 + [buffer(ROUND, NZ, IMG, BY)],
        compiler_params=PARAMS,
        name="second_steps",
    )(*operands)


def swap(x, axis, pairs):
    return lax.ppermute(x, axis, [(a, b) for a, b in pairs] + [(b, a) for a, b in pairs])


def shards(velocity, buoyancy, fwd_field, adjoint_now, adjoint_prev, recv_cell, traces):
    now, prev, fwd = adjoint_now[0], adjoint_prev[0], fwd_field[0]
    gx, gy, shot = lax.axis_index("gx"), lax.axis_index("gy"), lax.axis_index("shot")
    where = jnp.stack([gx * BX, gy * BY, gy % 2, shot % 2]).astype(jnp.int32)
    count_y, count_x = lax.axis_size("gy"), lax.axis_size("gx")

    listed = shape(RECV + 8, dtype=jnp.int32)
    place, place4, which, count = pl.pallas_call(
        find_kernel,
        out_shape=(listed, listed, listed, shape(1, dtype=jnp.int32)),
        in_specs=[SM, SM],
        out_specs=(SM,) * 4,
        compiler_params=room(4),
        cost_estimate=pl.CostEstimate(flops=8000, bytes_accessed=4000, transcendentals=0),
        name="find_receivers",
    )(where, recv_cell[0])

    up = [(i, i + 1) for i in range(count_x - 1)]
    down = [(b, a) for a, b in up]
    fields = jnp.concatenate([now, prev], axis=0)
    low_fields = lax.ppermute(fields, "gx", up)
    high_fields = lax.ppermute(fields, "gx", down)

    own = jnp.concatenate([jnp.broadcast_to(part, (4,) + part.shape) for part in (velocity, buoyancy)], axis=1)
    half = lax.all_to_all(own, "shot", 0, 0, axis_index_groups=[[0, 2, 4, 6], [1, 3, 5, 7]]).reshape(16, BX, BY)

    first, second = pl.pallas_call(
        pack_kernel,
        out_shape=(shape(12, BX, BY), shape(12, BX, BY)),
        in_specs=[SM, VM, VM],
        out_specs=(VM, VM),
        compiler_params=room(8),
        name="pack_sides",
    )(where, fields, half)
    first = swap(first, "gy", [(i, i + 1) for i in range(0, count_y, 2)])
    second = swap(second, "gy", [(i, i + 1) for i in range(1, count_y - 1, 2)])

    centre = jnp.concatenate([half, first, second], axis=0)
    centre, low_fields, high_fields, place, place4, which, count = lax.optimization_barrier(
        (centre, low_fields, high_fields, place, place4, which, count)
    )
    low = lax.ppermute(centre, "gx", up)
    high = lax.ppermute(centre, "gx", down)

    model = jnp.concatenate(
        [part for block in (centre, low, high) for part in (block[0:16], block[24:28], block[36:40])], axis=0
    )
    other = lax.ppermute(model, "shot", [(i, i ^ 1) for i in range(SHOTS)])

    outs = steps_one(
        where, place, which, count, traces[0], centre, low, high, fields, low_fields, high_fields, other, fwd[:ROUND]
    )
    send, iv, ib, coefs = outs[0], outs[1], outs[2], outs[3:]
    low = lax.ppermute(send, "gx", up)
    high = lax.ppermute(send, "gx", down)
    now, prev, images = steps_two(place4, which, count, traces[0], send, low, high, fwd[ROUND:], iv, ib, *coefs)
    parts = jnp.sum(lax.all_to_all(images, "shot", 0, 0), axis=0)
    scale = 1.0 / (SHOTS * STEPS) ** 0.5
    grad_vel = 2.0 * parts[:2] / velocity * scale
    grad_buoy = courant * velocity * velocity * (lap_unit * parts[2:]) * scale
    return grad_vel, grad_buoy, now[None], prev[None]


def solution(mesh):
    return jax.shard_map(
        shards,
        mesh=mesh,
        in_specs=(
            P("shot", "gx", "gy"),
            P("shot", "gx", "gy"),
            P("shot", None, None, "gx", "gy"),
            P("shot", None, "gx", "gy"),
            P("shot", None, "gx", "gy"),
            P("shot", None),
            P("shot", None, None),
        ),
        out_specs=(
            P("shot", "gx", "gy"),
            P("shot", "gx", "gy"),
            P("shot", None, "gx", "gy"),
            P("shot", None, "gx", "gy"),
        ),
        check_vma=False,
    )
```

time: 554 us -> 113 us (0.20)
  waiting for transfers between devices: 215 us -> 22.2 us
  other arithmetic: 152 us -> 1.42 us
  starting transfers between devices: 132 us -> 38.3 us
  Pallas kernels: 0 us -> 33.6 us
  blocking collectives: 29.1 us -> 15 us
  between operations: 15 us -> 0.91 us
  local copies, waits for them, and re-layouts: 9.39 us -> 0.86 us
    scatter-add x8 -> x0, other arithmetic: 130 us -> none  [shards(): now_pad.at[shot_ids, depth_idx, local_x, local_y]]
    ppermute x36 -> x9, waiting for transfers between devices: 139 us -> 22.2 us  [the longest x1 9.69 us: shards(): low = lax.ppermute(centre, 'gx', up)]
    ppermute x36 -> x9, starting transfers between devices: 132 us -> 32.3 us  [the longest x2 9.76 us: swap(): lax.ppermute(x, axis, [(a, b) for a, b in pairs] + [(b, a) for a, b in pa...]
    reduce_scatter x2 -> x0, waiting for transfers between devices: 75.2 us -> none  [the longest x1 42.3 us: shards(): lax.psum_scatter(image_b, 'shot', scatter_dimension=0, tiled=True)]
    pallas_call x0 -> x4, Pallas kernels: none -> 33.6 us  [the longest x1 13.5 us: steps_one(): pl.pallas_call(first_kernel, out_shape=(shape(40, BX, BY), image, image)...]
    all_gather x2 -> x0, blocking collectives: 29.1 us -> none  [the longest x1 14.9 us: shards(): lax.all_gather(buoyancy, 'shot', axis=0, tiled=True)]
    add x11 -> x0, other arithmetic: 16.9 us -> none  [the longest x8 15.4 us: shards(): 2.0 * centre - crop(prev, excess) + crop(speed_wide, offset) * operated]
    all_to_all x0 -> x1, blocking collectives: none -> 15 us  [shards(): parts = jnp.sum(lax.all_to_all(images, 'shot', 0, 0), axis=0)]
  transfers between devices with their start and end apart: 38 -> 10, of which waited for: 24 -> 5; matrix products, arithmetic and copies ran while one was open for 3% -> 0% of each run, Pallas kernels for 0% -> 7%
where the time goes in v2:
time: 113 us; the launch traced here: 112 us
  starting transfers between devices  38.3 us (34%)
  Pallas kernels  33.6 us (30%)
  waiting for transfers between devices  22.2 us (20%)
  blocking collectives  15 us (13%)
  other arithmetic  1.42 us (1%)
    all_to_all x1, blocking collectives, shards(): parts = jnp.sum(lax.all_to_all(images, 'shot', 0, 0), axis=0)  15 us
    pallas_call x1, Pallas kernels, steps_one(): pl.pallas_call(first_kernel, out_shape=(shape(40, BX, BY), image, image)...  13.5 us
    pallas_call x1, Pallas kernels, steps_two(): pl.pallas_call(second_kernel, out_shape=(shape(NZ, BX, BY), shape(NZ, BX,...  12.1 us
    ppermute x2, starting transfers between devices, swap(): lax.ppermute(x, axis, [(a, b) for a, b in pairs] + [(b, a) for a, b in pa...  9.76 us
    ppermute x1, waiting for transfers between devices, shards(): low = lax.ppermute(centre, 'gx', up)  9.69 us
    pallas_call x1, Pallas kernels, shards(): pl.pallas_call(find_kernel, out_shape=(listed, listed, listed, shape(1, d...  7.28 us
    all_to_all x1, starting transfers between devices, shards(): lax.all_to_all(own, 'shot', 0, 0, axis_index_groups=[[0, 2, 4, 6], [1, 3,...  6.03 us
    ppermute x1, waiting for transfers between devices, shards(): high = lax.ppermute(send, 'gx', down)  5.83 us
  transfers between devices with their start and end apart: 10, of which 5 were waited for; matrix products, arithmetic and copies ran while one was open for 0% of the time, Pallas kernels for 7%

profile of v2, /device:TPU:6, one launch (start us, length us, event | category | flops | bytes accessed | tf_op | source)
XLA Modules:
  0.0 112.2 jit_solution(17797486477844171810)
XLA Ops:
  0.6 0.7 broadcast_in_dim.13
  1.4 0.7 pad_maximum_fusion.2
  2.0 6.0 %all-to-all-start = ((f32[4,4,16,128]{3,2,1,0:T(8,128)}), f32[4,4,16,128]{3,2,1,0:T(8,128)S(1)}, u32[]{:S(2)}, u32[]{:S(2)}) async-start(f32[4,4,16,128]{3,2,1,0:T(8,128)} %pad_maximum_fusion.2), calls=%async_computation | async-start | bytes 262144 | tf_op jit(solution)/shard_map/all_to_all | solution.py:416
  8.1 5.2 %collective-permute-start.3 = (f32[32,16,128]{2,1,0:T(8,128)S(1)}, f32[32,16,128]{2,1,0:T(8,128)S(1)}, u32[]{:S(2)}, u32[]{:S(2)}) collective-permute-start(f32[32,16,128]{2,1,0:T(8,128)S(1)} %pad_maximum_fusion.1.fields_ref.centre_fields), channel_id=1, source_target_pairs={{4,0},{8,4},{12,8},{16,12},{20,16},{24,20},{28,24},{32,28},{36,32}... | collective-permute-start | bytes 786440 | tf_op jit(solution)/shard_map/ppermute | solution.py:413
  13.3 1.9 %collective-permute-start.2 = (f32[32,16,128]{2,1,0:T(8,128)S(1)}, f32[32,16,128]{2,1,0:T(8,128)S(1)}, u32[]{:S(2)}, u32[]{:S(2)}) collective-permute-start(f32[32,16,128]{2,1,0:T(8,128)S(1)} %pad_maximum_fusion.1.fields_ref.centre_fields), channel_id=1, source_target_pairs={{0,4},{4,8},{8,12},{12,16},{16,20},{20,24},{24,28},{28,32},{32,36}... | collective-permute-start | bytes 786440 | tf_op jit(solution)/shard_map/ppermute | solution.py:412
  15.2 0.1 pad_add_fusion.where_ref
  15.3 0.7 pack_sides.1
  16.0 9.1 %collective-permute-start = (f32[12,16,128]{2,1,0:T(8,128)S(1)}, f32[12,16,128]{2,1,0:T(8,128)S(1)}, u32[]{:S(2)}, u32[]{:S(2)}) collective-permute-start(f32[12,16,128]{2,1,0:T(8,128)S(1)} %get-tuple-element.31), channel_id=1, source_target_pairs={{0,1},{2,3},{1,0},{3,2},{4,5},{6,7},{5,4},{7,6},{8,9},{10,11},{9,8... | collective-permute-start | bytes 294920 | tf_op jit(solution)/shard_map/ppermute | solution.py:389
  25.2 0.7 collective-permute-start.1
  25.8 7.3 %find_receivers.1 = (s32[264]{0:T(512)S(1)}, s32[264]{0:T(512)S(1)}, s32[264]{0:T(512)S(1)}, s32[1]{0:T(128)}) custom-call(s32[4]{0:T(128)S(1)} %pad_add_fusion.where_ref, s32[256]{0:T(256)S(1)} %bitcast.19), custom_call_target="tpu_custom_call" | custom-call | flops 8000 | bytes 4000 | tf_op jit(solution)/shard_map/find_receivers/pallas_call | solution.py:399
  33.1 0.7 collective-permute-done
  33.9 5.8 %collective-permute-start.5 = (f32[40,16,128]{2,1,0:T(8,128)S(1)}, f32[40,16,128]{2,1,0:T(8,128)S(1)}, u32[]{:S(2)}, u32[]{:S(2)}) collective-permute-start(f32[40,16,128]{2,1,0:T(8,128)S(1)} %pad_maximum_fusion.centre_ref), channel_id=1, source_target_pairs={{4,0},{8,4},{12,8},{16,12},{20,16},{24,20},{28,24},{32,28},{36,32}... | collective-permute-start | bytes 983048 | tf_op jit(solution)/shard_map/ppermute | solution.py:434
  39.6 1.9 %collective-permute-start.4 = (f32[40,16,128]{2,1,0:T(8,128)S(1)}, f32[40,16,128]{2,1,0:T(8,128)S(1)}, u32[]{:S(2)}, u32[]{:S(2)}) collective-permute-start(f32[40,16,128]{2,1,0:T(8,128)S(1)} %pad_maximum_fusion.centre_ref), channel_id=1, source_target_pairs={{0,4},{4,8},{8,12},{12,16},{16,20},{20,24},{24,28},{28,32},{32,36}... | collective-permute-start | bytes 983048 | tf_op jit(solution)/shard_map/ppermute | solution.py:433
  41.6 9.7 %collective-permute-done.4.low_ref = f32[40,16,128]{2,1,0:T(8,128)S(1)} collective-permute-done((f32[40,16,128]{2,1,0:T(8,128)S(1)}, f32[40,16,128]{2,1,0:T(8,128)S(1)}, u32[]{:S(2)}, u32[]{:S(2)}) %collective-permute-start.4) | collective-permute-done | bytes 327712 | tf_op jit(solution)/shard_map/ppermute | solution.py:433
  51.4 1.9 %collective-permute-start.6 = (f32[72,16,128]{2,1,0:T(8,128)S(1)}, f32[72,16,128]{2,1,0:T(8,128)S(1)}, u32[]{:S(2)}, u32[]{:S(2)}) collective-permute-start(f32[72,16,128]{2,1,0:T(8,128)S(1)} %slice_dynamic-update-slice_fusion.3), channel_id=1, source_target_pairs={{0,64},{64,0},{128,192},{192,128},{256,320},{320,256},{384,448},{4... | collective-permute-start | bytes 1769480 | tf_op jit(solution)/shard_map/ppermute | solution.py:439
  53.4 1.9 %collective-permute-done.6.other_ref = f32[72,16,128]{2,1,0:T(8,128)S(1)} collective-permute-done((f32[72,16,128]{2,1,0:T(8,128)S(1)}, f32[72,16,128]{2,1,0:T(8,128)S(1)}, u32[]{:S(2)}, u32[]{:S(2)}) %collective-permute-start.6) | collective-permute-done | bytes 589856 | tf_op jit(solution)/shard_map/ppermute | solution.py:439
  55.3 13.5 %first_steps.1 = (f32[40,16,128]{2,1,0:T(8,128)S(1)}, f32[16,24,128]{2,1,0:T(8,128)S(1)}, f32[16,24,128]{2,1,0:T(8,128)S(1)}, f32[16,48,128]{2,1,0:T(8,128)S(1)}...) custom-call(s32[4]{0:T(128)S(1)} %pad_add_fusion.where_ref, ...), custom_call_target="tpu_custom_call" | custom-call | tf_op jit(solution)/shard_map/first_steps/pallas_call | solution.py:361
  68.8 1.9 %collective-permute-start.8 = (f32[40,16,128]{2,1,0:T(8,128)S(1)}, f32[40,16,128]{2,1,0:T(8,128)S(1)}, u32[]{:S(2)}, u32[]{:S(2)}) collective-permute-start(f32[40,16,128]{2,1,0:T(8,128)S(1)} %get-tuple-element.44.centre_ref), channel_id=1, source_target_pairs={{4,0},{8,4},{12,8},{16,12},{20,16},{24,20},{28,24},{32,28},{36,32}... | collective-permute-start | bytes 983048 | tf_op jit(solution)/shard_map/ppermute | solution.py:446
  70.8 3.9 %collective-permute-start.7 = (f32[40,16,128]{2,1,0:T(8,128)S(1)}, f32[40,16,128]{2,1,0:T(8,128)S(1)}, u32[]{:S(2)}, u32[]{:S(2)}) collective-permute-start(f32[40,16,128]{2,1,0:T(8,128)S(1)} %get-tuple-element.44.centre_ref), channel_id=1, source_target_pairs={{0,4},{4,8},{8,12},{12,16},{16,20},{20,24},{24,28},{28,32},{32,36}... | collective-permute-start | bytes 983048 | tf_op jit(solution)/shard_map/ppermute | solution.py:445
  74.7 5.8 %collective-permute-done.8.high_ref = f32[40,16,128]{2,1,0:T(8,128)S(1)} collective-permute-done((f32[40,16,128]{2,1,0:T(8,128)S(1)}, f32[40,16,128]{2,1,0:T(8,128)S(1)}, u32[]{:S(2)}, u32[]{:S(2)}) %collective-permute-start.8) | collective-permute-done | bytes 327712 | tf_op jit(solution)/shard_map/ppermute | solution.py:446
  80.5 4.0 %collective-permute-done.7.low_ref = f32[40,16,128]{2,1,0:T(8,128)S(1)} collective-permute-done((f32[40,16,128]{2,1,0:T(8,128)S(1)}, f32[40,16,128]{2,1,0:T(8,128)S(1)}, u32[]{:S(2)}, u32[]{:S(2)}) %collective-permute-start.7) | collective-permute-done | bytes 327712 | tf_op jit(solution)/shard_map/ppermute | solution.py:445
  84.6 12.1 %second_steps.1 = (f32[16,16,128]{2,1,0:T(8,128)}, f32[16,16,128]{2,1,0:T(8,128)}, f32[8,4,16,128]{3,2,1,0:T(8,128)S(1)}) custom-call(s32[264]{0:T(512)S(1)} %get-tuple-element.37.place_ref, s32[264]{0:T(512)S(1)} %get-tuple-element.38.which_ref, s32[1]{0:T(128)} %get-tuple-element.39.count_ref, f32[8,256]{1,0:T(8,128)S(1)} %bitcast.18, ...), custom_call_target="tpu_custom_call" | custom-call | tf_op jit(solution)/shard_map/second_steps/pallas_call | solution.py:377
  96.6 15.0 %all_to_all.10 = f32[8,4,16,128]{3,2,1,0:T(8,128)S(1)} all-to-all(f32[8,4,16,128]{3,2,1,0:T(8,128)S(1)} %get-tuple-element.55), channel_id=1, replica_groups=mesh['shot'=8,'gx'=16,'gy'=4] {'shot'}, dimensions={0} | all-to-all | bytes 524288 | tf_op jit(solution)/shard_map/all_to_all | solution.py:448
  111.6 0.6 fusion.1
  (31 shorter events, 0.2 us)
Async XLA Ops:
  0.6 0.7 copy-start.5
  2.0 6.0 %copy-start.3 = (f32[1,16,16,128]{3,2,1,0:T(8,128)S(1)}, f32[1,16,16,128]{3,2,1,0:T(8,128)}, u32[]{:S(2)}) copy-start(f32[1,16,16,128]{3,2,1,0:T(8,128)} %param.11) | copy-start | bytes 393220
  2.0 6.0 %copy-start.4 = (f32[1,16,16,128]{3,2,1,0:T(8,128)S(1)}, f32[1,16,16,128]{3,2,1,0:T(8,128)}, u32[]{:S(2)}) copy-start(f32[1,16,16,128]{3,2,1,0:T(8,128)} %param.10) | copy-start | bytes 393220
  2.0 13.3 %all-to-all-start = ((f32[4,4,16,128]{3,2,1,0:T(8,128)}), f32[4,4,16,128]{3,2,1,0:T(8,128)S(1)}, u32[]{:S(2)}, u32[]{:S(2)}) async-start(f32[4,4,16,128]{3,2,1,0:T(8,128)} %pad_maximum_fusion.2), calls=%async_computation | async-start | bytes 262144 | tf_op jit(solution)/shard_map/all_to_all | solution.py:416
  8.1 25.7 %collective-permute-start.3 = (f32[32,16,128]{2,1,0:T(8,128)S(1)}, f32[32,16,128]{2,1,0:T(8,128)S(1)}, u32[]{:S(2)}, u32[]{:S(2)}) collective-permute-start(f32[32,16,128]{2,1,0:T(8,128)S(1)} %pad_maximum_fusion.1.fields_ref.centre_fields), channel_id=1, source_target_pairs={{4,0},{8,4},{12,8},{16,12},{20,16},{24,20},{28,24},{32,28},{36,32}... | collective-permute-start | bytes 786440 | tf_op jit(solution)/shard_map/ppermute | solution.py:413
  13.3 20.6 %collective-permute-start.2 = (f32[32,16,128]{2,1,0:T(8,128)S(1)}, f32[32,16,128]{2,1,0:T(8,128)S(1)}, u32[]{:S(2)}, u32[]{:S(2)}) collective-permute-start(f32[32,16,128]{2,1,0:T(8,128)S(1)} %pad_maximum_fusion.1.fields_ref.centre_fields), channel_id=1, source_target_pairs={{0,4},{4,8},{8,12},{12,16},{16,20},{20,24},{24,28},{28,32},{32,36}... | collective-permute-start | bytes 786440 | tf_op jit(solution)/shard_map/ppermute | solution.py:412
  16.0 17.8 %collective-permute-start = (f32[12,16,128]{2,1,0:T(8,128)S(1)}, f32[12,16,128]{2,1,0:T(8,128)S(1)}, u32[]{:S(2)}, u32[]{:S(2)}) collective-permute-start(f32[12,16,128]{2,1,0:T(8,128)S(1)} %get-tuple-element.31), channel_id=1, source_target_pairs={{0,1},{2,3},{1,0},{3,2},{4,5},{6,7},{5,4},{7,6},{8,9},{10,11},{9,8... | collective-permute-start | bytes 294920 | tf_op jit(solution)/shard_map/ppermute | solution.py:389
  25.1 0.7 copy-start.1
  25.2 8.7 %collective-permute-start.1 = (f32[12,16,128]{2,1,0:T(8,128)S(1)}, f32[12,16,128]{2,1,0:T(8,128)S(1)}, u32[]{:S(2)}, u32[]{:S(2)}) collective-permute-start(f32[12,16,128]{2,1,0:T(8,128)S(1)} %get-tuple-element.32), channel_id=1, source_target_pairs={{1,2},{2,1},{5,6},{6,5},{9,10},{10,9},{13,14},{14,13},{17,18},{18,... | collective-permute-start | bytes 294920 | tf_op jit(solution)/shard_map/ppermute | solution.py:389
  33.9 17.5 %collective-permute-start.5 = (f32[40,16,128]{2,1,0:T(8,128)S(1)}, f32[40,16,128]{2,1,0:T(8,128)S(1)}, u32[]{:S(2)}, u32[]{:S(2)}) collective-permute-start(f32[40,16,128]{2,1,0:T(8,128)S(1)} %pad_maximum_fusion.centre_ref), channel_id=1, source_target_pairs={{4,0},{8,4},{12,8},{16,12},{20,16},{24,20},{28,24},{32,28},{36,32}... | collective-permute-start | bytes 983048 | tf_op jit(solution)/shard_map/ppermute | solution.py:434
  39.6 11.7 %collective-permute-start.4 = (f32[40,16,128]{2,1,0:T(8,128)S(1)}, f32[40,16,128]{2,1,0:T(8,128)S(1)}, u32[]{:S(2)}, u32[]{:S(2)}) collective-permute-start(f32[40,16,128]{2,1,0:T(8,128)S(1)} %pad_maximum_fusion.centre_ref), channel_id=1, source_target_pairs={{0,4},{4,8},{8,12},{12,16},{16,20},{20,24},{24,28},{28,32},{32,36}... | collective-permute-start | bytes 983048 | tf_op jit(solution)/shard_map/ppermute | solution.py:433
  41.6 11.8 %copy-start.2 = (bf16[1,8,16,16,128]{4,3,2,1,0:T(8,128)(2,1)S(1)}, bf16[1,8,16,16,128]{4,3,2,1,0:T(8,128)(2,1)}, u32[]{:S(2)}) copy-start(bf16[1,8,16,16,128]{4,3,2,1,0:T(8,128)(2,1)} %param.9) | copy-start | bytes 1572868
  51.4 3.9 %collective-permute-start.6 = (f32[72,16,128]{2,1,0:T(8,128)S(1)}, f32[72,16,128]{2,1,0:T(8,128)S(1)}, u32[]{:S(2)}, u32[]{:S(2)}) collective-permute-start(f32[72,16,128]{2,1,0:T(8,128)S(1)} %slice_dynamic-update-slice_fusion.3), channel_id=1, source_target_pairs={{0,64},{64,0},{128,192},{192,128},{256,320},{320,256},{384,448},{4... | collective-permute-start | bytes 1769480 | tf_op jit(solution)/shard_map/ppermute | solution.py:439
  53.3 2.0 %copy-start = (f32[1,8,256]{2,1,0:T(8,128)S(1)}, f32[1,8,256]{2,1,0:T(8,128)}, u32[]{:S(2)}) copy-start(f32[1,8,256]{2,1,0:T(8,128)} %param.13) | copy-start | bytes 24580
  68.8 11.7 %collective-permute-start.8 = (f32[40,16,128]{2,1,0:T(8,128)S(1)}, f32[40,16,128]{2,1,0:T(8,128)S(1)}, u32[]{:S(2)}, u32[]{:S(2)}) collective-permute-start(f32[40,16,128]{2,1,0:T(8,128)S(1)} %get-tuple-element.44.centre_ref), channel_id=1, source_target_pairs={{4,0},{8,4},{12,8},{16,12},{20,16},{24,20},{28,24},{32,28},{36,32}... | collective-permute-start | bytes 983048 | tf_op jit(solution)/shard_map/ppermute | solution.py:446
  70.8 13.8 %collective-permute-start.7 = (f32[40,16,128]{2,1,0:T(8,128)S(1)}, f32[40,16,128]{2,1,0:T(8,128)S(1)}, u32[]{:S(2)}, u32[]{:S(2)}) collective-permute-start(f32[40,16,128]{2,1,0:T(8,128)S(1)} %get-tuple-element.44.centre_ref), channel_id=1, source_target_pairs={{0,4},{4,8},{8,12},{12,16},{16,20},{20,24},{24,28},{28,32},{32,36}... | collective-permute-start | bytes 983048 | tf_op jit(solution)/shard_map/ppermute | solution.py:445

commit v3 on v2

--- a/solution.py
+++ b/solution.py
@@ -2,6 +2,7 @@
 
 import jax
 import jax.numpy as jnp
+import numpy as np
 from jax import lax
 from jax.experimental import pallas as pl
 from jax.experimental.pallas import tpu as pltpu
@@ -68,7 +69,7 @@
         which_ref[count] = j
         return count + inside.astype(jnp.int32)
 
-    count_ref[0] = lax.fori_loop(0, RECV, body, jnp.int32(0))
+    count_ref[0] = lax.fori_loop(0, RECV, body, jnp.int32(0), unroll=4)
 
 
 def pack_kernel(where_ref, fields_ref, model_ref, first_ref, second_ref):
@@ -126,64 +127,118 @@
         ref[z] = jnp.zeros(ref.shape[1:], jnp.float32)
 
 
-def clear(ref):
-    def body(z, _):
-        ref[z] = jnp.zeros(ref.shape[1:], jnp.float32)
+PARTS = 3
+
+
+def side_columns(groups):
+    w = BY // groups
+    lane = np.arange(BY)
+    t = lane % w
+    return lane // w, np.where(t < w // 2, BY + t, t - w)
+
+
+def shift_weights(group_to, y_to, group_from, y_from):
+    lap_k = np.array((0, 8064, -1008, 128, -9) + (0,) * 4, np.float32)
+    slope_k = np.array((0, 672, -168, 32, -3) + (0,) * 4, np.float32)
+    away = y_from[:, None] - y_to[None, :]
+    k = np.where((group_from[:, None] == group_to[None, :]) & (abs(away) < 5), abs(away), 0)
+    return np.concatenate([lap_k[k], slope_k[k] * np.sign(away)], axis=1)
+
+
+def layer_weights(groups):
+    side_group, side_y = side_columns(groups)
+    y = np.arange(BY)
+    both = []
+    for g in range(groups):
+        own = np.full(BY, g)
+        both.append(np.concatenate([shift_weights(own, y, own, y), shift_weights(own, y, side_group, side_y)], axis=0))
+    return jnp.asarray(np.stack(both), jnp.bfloat16)
+
+
+def side_weights(groups):
+    side_group, side_y = side_columns(groups)
+    y = np.arange(BY)
+    rows = [shift_weights(side_group, side_y, side_group, side_y)]
+    rows += [shift_weights(side_group, side_y, np.full(BY, g), y) for g in range(groups)]
+    return jnp.asarray(np.concatenate(rows, axis=0), jnp.bfloat16)
+
+
+def shift_along_y(ref, groups, start, n, work, sides=True, lap_too=True):
+    cut_layers, cut_sides, layer_w, side_w, y_lap, y_slope = work
+    per = NZ // groups
+    rows = pl.ds(PAD + start, n)
+
+    def cut(at, to, z):
+        x = ref[at, rows, :]
+        for part in range(PARTS):
+            piece = x.astype(jnp.bfloat16)
+            to[part, z, pl.ds(0, n), :] = piece
+            x = x - piece.astype(jnp.float32)
+
+    def cut_group(p, _):
+        for g in range(groups):
+            cut(4 + p + g * per, cut_layers, p + g * per)
+        cut(LAYERS + 4 + p, cut_sides, p)
         return 0
 
-    lax.fori_loop(0, ref.shape[0], body, 0)
-
-
-def derivs(ref, at, row, n, here, edges, lane, width, lap_too=True):
-    inner = lane & (width - 1)
-    lap = lap_ratio[0] * here if lap_too else None
-    dz = dx = dy = None
+    lax.fori_loop(0, per, cut_group, 0, unroll=True)
+    if sides:
+        repeat_sides(ref, groups)
+
+    def product(pieces, weights, first):
+        weights = weights if lap_too else weights[:, BY:]
+        found = jnp.dot(
+            jnp.concatenate(pieces, axis=1), jnp.concatenate([weights] * PARTS, axis=0), preferred_element_type=jnp.float32
+        )
+        if lap_too:
+            y_lap[first : first + per, pl.ds(start, n), :] = found[:, :BY].reshape(per, n, BY)
+        y_slope[first : first + per, pl.ds(start, n), :] = found[:, -BY:].reshape(per, n, BY)
+
+    def layer_piece(part, g):
+        return cut_layers[part, g * per : (g + 1) * per, pl.ds(0, n), :].reshape(per * n, BY)
+
+    def side_piece(part):
+        return cut_sides[part, :, pl.ds(0, n), :].reshape(per * n, BY)
+
+    for g in range(groups):
+        pieces = [x for part in range(PARTS) for x in (layer_piece(part, g), side_piece(part))]
+        product(pieces, layer_w[g], g * per)
+    if sides:
+        pieces = []
+        for part in range(PARTS):
+            pieces += [side_piece(part)] + [layer_piece(part, g) for g in range(groups)]
+        product(pieces, side_w[...], NZ)
+
+
+def along_zx(ref, at, row, n, lap_too=True):
+    lap = dz = dx = None
     for k in (4, 3, 2, 1):
-        up = roll(jnp.where(inner < k, edges, here), -k)
-        down = roll(jnp.where(inner >= width - k, edges, here), k)
         zp = ref[at + k, pl.ds(row, n), :]
         zm = ref[at - k, pl.ds(row, n), :]
         xp = ref[at, pl.ds(row + k, n), :]
         xm = ref[at, pl.ds(row - k, n), :]
         if lap_too:
-            both = ((zp + zm) + (xp + xm)) + (up + down)
-            lap = lap + (both if k == 4 else lap_ratio[k] * both)
-        if k == 4:
-            dz, dx, dy = zp - zm, xp - xm, up - down
-        else:
-            c = slope_ratio[k - 1]
-            dz, dx, dy = dz + c * (zp - zm), dx + c * (xp - xm), dy + c * (up - down)
-    return lap, dz, dx, dy
-
-
-def group_derivs(ref, p, lo, n, groups, sides=True, lap_too=True):
+            both = (zp + zm) + (xp + xm)
+            lap = both if k == 4 else lap + lap_ratio[k] * both
+        c = slope_ratio[k - 1] if k < 4 else None
+        dz = zp - zm if k == 4 else dz + c * (zp - zm)
+        dx = xp - xm if k == 4 else dx + c * (xp - xm)
+    return lap, dz, dx
+
+
+def group_places(p, groups, sides=True):
     per = NZ // groups
-    w = BY // groups
-    lane = lane_of(n)
-    row = PAD + lo
-    spot = pl.ds(row, n)
-    side_at = LAYERS + 4 + p
-    side = ref[side_at, spot, :]
-    mains = [ref[4 + p + g * per, spot, :] for g in range(groups)]
-    for g in range(groups):
-        edges = jnp.where(lane < 64, roll(side, -g * w), roll(side, -(g + 1) * w))
-        at = 4 + p + g * per
-        yield 0, p + g * per, at, mains[g], derivs(ref, at, row, n, mains[g], edges, lane, BY, lap_too)
-    if sides:
-        edges = None
-        for g in range(groups):
-            first = roll(mains[(g - 1) % groups], g * w)
-            last = roll(mains[(g + 1) % groups], (g + 1) * w)
-            for start, value in ((g * w, first), (g * w + w // 2, last)):
-                edges = value if edges is None else jnp.where(lane >= start, value, edges)
-        yield 1, p, side_at, side, derivs(ref, side_at, row, n, side, edges, lane, w, lap_too)
+    places = [(0, p + g * per, 4 + p + g * per, p + g * per) for g in range(groups)]
+    return places + [(1, p, LAYERS + 4 + p, NZ + p)] * sides
 
 
 PLANS = ((4, 12, 20, 28, 36), (8, 16, 24, 32), (12, 20, 28), (16, 24))
-
-
-def run_steps(first_step, groups, cur, old, coefs, fwd_ref, image, place_ref, which_ref, count_ref, trace_ref, last):
+WINDOWS = ((0, 48), (8, 32), (8, 32), (16, 16))
+
+
+def run_steps(first_step, groups, cur, old, coefs, fwd_ref, image, place_ref, which_ref, count_ref, trace_ref, work, last):
     lane1 = lane_of(1)
+    y_lap, y_slope = work[-2:]
     for j, plan in enumerate(PLANS):
 
         def add(i, _, cur=cur, step=first_step + j):
@@ -194,22 +249,26 @@
             return 0
 
         lax.fori_loop(0, count_ref[0], add, 0)
-        repeat_sides(cur, groups)
         sides = not (last and j == ROUND - 1)
+        shift_along_y(cur, groups, *WINDOWS[j], work, sides)
 
         def layers(p, _, cur=cur, old=old, plan=plan, j=j, sides=sides):
             for lo in plan:
                 rows = pl.ds(lo, 8)
-                for kind, z, at, here, found in group_derivs(cur, p, lo, 8, groups, sides):
+                for kind, z, at, y in group_places(p, groups, sides):
+                    lap, dz, dx = along_zx(cur, at, PAD + lo, 8)
+                    spot = (at, pl.ds(PAD + lo, 8), slice(None))
+                    here = cur[spot]
+                    lap = (lap + (-1.0 / 9.0) * y_lap[y, rows, :]) + lap_ratio[0] * here
+                    found = lap, dz, dx, y_slope[y, rows, :]
                     terms = [coefs[c][kind][z, rows, :] * found[c] for c in range(4)]
                     change = (terms[0] + terms[1]) + (terms[2] + terms[3])
-                    spot = (at, pl.ds(PAD + lo, 8), slice(None))
                     old[spot] = ((here + here) - old[spot]) + change
                     if kind == 0 and BX - 8 < lo < 2 * BX:
                         seen = pl.ds(lo - (BX - 4), 8)
                         snapshot = fwd_ref[j, z, seen, :]
-                        image[0][z, seen, :] += snapshot * change
-                        image[1][z, seen, :] += snapshot * found[0]
+                        for total, term in zip(image, (snapshot * change, snapshot * lap)):
+                            total[z, seen, :] = total[z, seen, :] + term if j else term
             return 0
 
         lax.fori_loop(0, NZ // groups, layers, 0)
@@ -229,17 +288,16 @@
 
 def first_kernel(
     where_ref, place_ref, which_ref, count_ref, trace_ref,
-    centre_ref, low_ref, high_ref, centre_fields, low_fields, high_fields, other_ref, fwd_ref,
+    centre_ref, low_ref, high_ref, centre_fields, low_fields, high_fields, other_ref, fwd_ref, layer_w, side_w,
     send_ref, iv_ref, ib_ref, m0, m1, m2, m3, f0, f1, f2, f3,
-    cur, old, buoy, speed, speed_side, t0, t1, t2, t3, wide,
+    cur, old, buoy, speed, speed_side, t0, t1, t2, t3, wide, cut_layers, cut_sides, y_lap, y_slope,
 ):
+    work = cut_layers, cut_sides, layer_w, side_w, y_lap, y_slope
     even = where_ref[2] == 0
     core = where_ref[3]
     lane = lane_of(BX)
     for ref in (cur, old, buoy):
         clear_ends(ref)
-    clear(iv_ref)
-    clear(ib_ref)
     widen(fwd_ref, wide)
     at = LAYERS + 4
     blocks = ((low_ref, low_fields), (centre_ref, centre_fields), (high_ref, high_fields))
@@ -275,18 +333,21 @@
                         buoy[4 + z + 4 * i, rows, :] = planes[i]
                     for i in range(2):
                         buoy[at + z + 4 * i, rows, :] = pair[i]
-    repeat_sides(buoy, 2)
     coefs = ((m0, t0), (m1, t1), (m2, t2), (m3, t3))
+
+    shift_along_y(buoy, 2, 0, EXT, work, lap_too=False)
 
     def slopes(p, _):
         for lo in PLANS[0]:
             rows = pl.ds(lo, 8)
-            for kind, z, _, here, found in group_derivs(buoy, p, lo, 8, 2, lap_too=False):
+            for kind, z, at, y in group_places(p, 2):
+                _lap, dz, dx = along_zx(buoy, at, PAD + lo, 8, lap_too=False)
                 pace = (speed, speed_side)[kind][z, rows, :]
-                coefs[0][kind][z, rows, :] = (lap_unit * pace) * here
+                coefs[0][kind][z, rows, :] = (lap_unit * pace) * buoy[at, pl.ds(PAD + lo, 8), :]
                 steep = (slope_unit * slope_unit) * pace
-                for c in (1, 2, 3):
-                    coefs[c][kind][z, rows, :] = steep * found[c]
+                coefs[1][kind][z, rows, :] = steep * dz
+                coefs[2][kind][z, rows, :] = steep * dx
+                coefs[3][kind][z, rows, :] = ((1.0 / 840.0 / 840.0) * pace) * y_slope[y, rows, :]
         return 0
 
     lax.fori_loop(0, NZ // 2, slopes, 0)
@@ -297,7 +358,7 @@
                 rows = pl.ds(lo, 8)
                 side[p, rows, :] = four_from_two(wide_side[p, rows, :], wide_side[p + 4, rows, :], lane8)
     now, prev = run_steps(
-        0, 2, cur, old, coefs, wide, (iv_ref, ib_ref), place_ref, which_ref, count_ref, trace_ref, False
+        0, 2, cur, old, coefs, wide, (iv_ref, ib_ref), place_ref, which_ref, count_ref, trace_ref, work, False
     )
     rows = pl.ds(PAD + BX, BX)
     for f, field in enumerate((now, prev)):
@@ -308,15 +369,14 @@
 
 
 def second_kernel(
-    place_ref, which_ref, count_ref, trace_ref,
-    centre_ref, low_ref, high_ref, fwd_ref, iv_ref, ib_ref, m0, m1, m2, m3, f0, f1, f2, f3,
-    now_ref, prev_ref, images_ref,
-    cur, old, iv, ib, wide,
+    where_ref, place_ref, which_ref, count_ref, trace_ref,
+    centre_ref, low_ref, high_ref, fwd_ref, iv_ref, ib_ref, m0, m1, m2, m3, f0, f1, f2, f3, layer_w, side_w,
+    now_ref, prev_ref, keep_ref, give_ref,
+    cur, old, iv, ib, wide, cut_layers, cut_sides, y_lap, y_slope,
 ):
+    work = cut_layers, cut_sides, layer_w, side_w, y_lap, y_slope
     for ref in (cur, old):
         clear_ends(ref)
-    clear(iv)
-    clear(ib)
     widen(fwd_ref, wide)
     at = LAYERS + 4
     for block, ref in enumerate((low_ref, centre_ref, high_ref)):
@@ -328,15 +388,20 @@
                 field[at + p, rows, :] = ref[2 * NZ + 4 * f + p]
     now, prev = run_steps(
         ROUND, 4, cur, old, ((m0, f0), (m1, f1), (m2, f2), (m3, f3)), wide, (iv, ib),
-        place_ref, which_ref, count_ref, trace_ref, True,
+        place_ref, which_ref, count_ref, trace_ref, work, True,
     )
     rows = pl.ds(PAD + BX, BX)
     wanted = pl.ds(4, BX)
+    core = where_ref[3]
     for z in range(NZ):
         now_ref[z] = now[4 + z, rows, :]
         prev_ref[z] = prev[4 + z, rows, :]
-        images_ref[z // 2, z % 2] = iv[z, wanted, :] + iv_ref[z, wanted, :]
-        images_ref[z // 2, 2 + z % 2] = ib[z, wanted, :] + ib_ref[z, wanted, :]
+    for i in range(4):
+        for ref, turn in ((keep_ref, core), (give_ref, 1 - core)):
+            for v in (0, 1):
+                z = 4 * i + 2 * turn + v
+                ref[i, v] = iv[z, wanted, :] + iv_ref[z, wanted, :]
+                ref[i, 2 + v] = ib[z, wanted, :] + ib_ref[z, wanted, :]
 
 
 def shape(*dims, dtype=jnp.float32):
@@ -352,6 +417,16 @@
 
 def buffer(*dims):
     return pltpu.VMEM(dims, jnp.float32)
+
+
+def work_buffers(groups):
+    planes = NZ + NZ // groups
+    return [
+        pltpu.VMEM((PARTS, NZ, EXT, BY), jnp.bfloat16),
+        pltpu.VMEM((PARTS, NZ // groups, EXT, BY), jnp.bfloat16),
+        buffer(planes, EXT, BY),
+        buffer(planes, EXT, BY),
+    ]
 
 
 def steps_one(*operands):
@@ -361,28 +436,31 @@
     return pl.pallas_call(
         first_kernel,
         out_shape=(shape(40, BX, BY), image, image) + (ext,) * 4 + (side_ext,) * 4,
-        in_specs=[SM] * 5 + [VM] * 8,
+        in_specs=[SM] * 5 + [VM] * 10,
         out_specs=(VM,) * 11,
         scratch_shapes=[buffer(block, ROWS, BY)] * 3
         + [buffer(NZ, EXT, BY)]
         + [buffer(NZ // 2, EXT, BY)] * 5
-        + [buffer(ROUND, NZ, IMG, BY)],
+        + [buffer(ROUND, NZ, IMG, BY)]
+        + work_buffers(2),
         compiler_params=PARAMS,
         name="first_steps",
-    )(*operands)
+    )(*operands, layer_weights(2), side_weights(2))
 
 
 def steps_two(*operands):
     block = LAYERS + side_planes(4)
     return pl.pallas_call(
         second_kernel,
-        out_shape=(shape(NZ, BX, BY), shape(NZ, BX, BY), shape(SHOTS, 4, BX, BY)),
-        in_specs=[SM] * 4 + [VM] * 14,
-        out_specs=(VM,) * 3,
-        scratch_shapes=[buffer(block, ROWS, BY)] * 2 + [buffer(NZ, IMG, BY)] * 2 + [buffer(ROUND, NZ, IMG, BY)],
+        out_shape=(shape(NZ, BX, BY),) * 2 + (shape(4, 4, BX, BY),) * 2,
+        in_specs=[SM] * 5 + [VM] * 16,
+        out_specs=(VM,) * 4,
+        scratch_shapes=[buffer(block, ROWS, BY)] * 2 + [buffer(NZ, IMG, BY)] * 2
+        + [buffer(ROUND, NZ, IMG, BY)]
+        + work_buffers(4),
         compiler_params=PARAMS,
         name="second_steps",
-    )(*operands)
+    )(*operands, layer_weights(4), side_weights(4))
 
 
 def swap(x, axis, pairs):
@@ -393,6 +471,8 @@
     now, prev, fwd = adjoint_now[0], adjoint_prev[0], fwd_field[0]
     gx, gy, shot = lax.axis_index("gx"), lax.axis_index("gy"), lax.axis_index("shot")
     where = jnp.stack([gx * BX, gy * BY, gy % 2, shot % 2]).astype(jnp.int32)
+    same_core = [list(range(core, SHOTS, 2)) for core in (0, 1)]
+    other_core = [(i, i ^ 1) for i in range(SHOTS)]
     count_y, count_x = lax.axis_size("gy"), lax.axis_size("gx")
 
     listed = shape(RECV + 8, dtype=jnp.int32)
@@ -413,7 +493,7 @@
     high_fields = lax.ppermute(fields, "gx", down)
 
     own = jnp.concatenate([jnp.broadcast_to(part, (4,) + part.shape) for part in (velocity, buoyancy)], axis=1)
-    half = lax.all_to_all(own, "shot", 0, 0, axis_index_groups=[[0, 2, 4, 6], [1, 3, 5, 7]]).reshape(16, BX, BY)
+    half = lax.all_to_all(own, "shot", 0, 0, axis_index_groups=same_core).reshape(16, BX, BY)
 
     first, second = pl.pallas_call(
         pack_kernel,
@@ -436,7 +516,7 @@
     model = jnp.concatenate(
         [part for block in (centre, low, high) for part in (block[0:16], block[24:28], block[36:40])], axis=0
     )
-    other = lax.ppermute(model, "shot", [(i, i ^ 1) for i in range(SHOTS)])
+    other = lax.ppermute(model, "shot", other_core)
 
     outs = steps_one(
         where, place, which, count, traces[0], centre, low, high, fields, low_fields, high_fields, other, fwd[:ROUND]
@@ -444,8 +524,9 @@
     send, iv, ib, coefs = outs[0], outs[1], outs[2], outs[3:]
     low = lax.ppermute(send, "gx", up)
     high = lax.ppermute(send, "gx", down)
-    now, prev, images = steps_two(place4, which, count, traces[0], send, low, high, fwd[ROUND:], iv, ib, *coefs)
-    parts = jnp.sum(lax.all_to_all(images, "shot", 0, 0), axis=0)
+    now, prev, keep, give = steps_two(where, place4, which, count, traces[0], send, low, high, fwd[ROUND:], iv, ib, *coefs)
+    pair = keep + lax.ppermute(give, "shot", other_core)
+    parts = jnp.sum(lax.all_to_all(pair, "shot", 0, 0, axis_index_groups=same_core), axis=0)
     scale = 1.0 / (SHOTS * STEPS) ** 0.5
     grad_vel = 2.0 * parts[:2] / velocity * scale
     grad_buoy = courant * velocity * velocity * (lap_unit * parts[2:]) * scale

time: 113 us -> 106 us (0.938)
  Pallas kernels: 33.6 us -> 25.9 us
  blocking collectives: 15 us -> 11.5 us
  starting transfers between devices: 38.3 us -> 40.4 us
  waiting for transfers between devices: 22.2 us -> 23.9 us
    pallas_call x1, Pallas kernels: 12.1 us -> 8.57 us  [steps_two(): pl.pallas_call(second_kernel, out_shape=(shape(NZ, BX, BY),) * 2 + (shape...]
    all_to_all x1, blocking collectives: 15 us -> 11.5 us  [shards(): lax.all_to_all(pair, 'shot', 0, 0, axis_index_groups=same_core)]
    pallas_call x1, Pallas kernels: 13.5 us -> 10.6 us  [steps_one(): pl.pallas_call(first_kernel, out_shape=(shape(40, BX, BY), image, image)...]
    ppermute x1 -> x2, starting transfers between devices: 1.92 us -> 3.96 us  [the longest x1 2.05 us: shards(): other = lax.ppermute(model, 'shot', other_core)]
    ppermute x1 -> x2, waiting for transfers between devices: 1.9 us -> 3.22 us  [the longest x1 1.9 us: shards(): other = lax.ppermute(model, 'shot', other_core)]
    ppermute x2, waiting for transfers between devices: 0.68 us -> 1.93 us  [swap(): lax.ppermute(x, axis, [(a, b) for a, b in pairs] + [(b, a) for a, b in pa...]
    pallas_call x1, Pallas kernels: 7.28 us -> 6.03 us  [shards(): pl.pallas_call(find_kernel, out_shape=(listed, listed, listed, shape(1, d...]
  transfers between devices with their start and end apart: 10 -> 11, of which waited for: 5 -> 6; matrix products, arithmetic and copies ran while one was open for 0% -> 0% of each run, Pallas kernels for 7% -> 6%
where the time goes in v3:
time: 106 us; the launch traced here: 105 us
  starting transfers between devices  40.4 us (38%)
  Pallas kernels  25.9 us (24%)
  waiting for transfers between devices  23.9 us (23%)
  blocking collectives  11.5 us (11%)
  other arithmetic  1.43 us (1%)
    all_to_all x1, blocking collectives, shards(): lax.all_to_all(pair, 'shot', 0, 0, axis_index_groups=same_core)  11.5 us
    pallas_call x1, Pallas kernels, steps_one(): pl.pallas_call(first_kernel, out_shape=(shape(40, BX, BY), image, image)...  10.6 us
    ppermute x2, starting transfers between devices, swap(): lax.ppermute(x, axis, [(a, b) for a, b in pairs] + [(b, a) for a, b in pa...  9.76 us
    ppermute x1, waiting for transfers between devices, shards(): low = lax.ppermute(centre, 'gx', up)  9.09 us
    pallas_call x1, Pallas kernels, steps_two(): pl.pallas_call(second_kernel, out_shape=(shape(NZ, BX, BY),) * 2 + (shape...  8.57 us
    pallas_call x1, Pallas kernels, shards(): pl.pallas_call(find_kernel, out_shape=(listed, listed, listed, shape(1, d...  6.03 us
    all_to_all x1, starting transfers between devices, shards(): lax.all_to_all(own, 'shot', 0, 0, axis_index_groups=same_core)  6.03 us
    ppermute x1, starting transfers between devices, shards(): high = lax.ppermute(centre, 'gx', down)  5.75 us
  transfers between devices with their start and end apart: 11, of which 6 were waited for; matrix products, arithmetic and copies ran while one was open for 0% of the time, Pallas kernels for 6%

profile of v3, /device:TPU:6, one launch (start us, length us, event | category | flops | bytes accessed | tf_op | source)
XLA Modules:
  0.0 105.1 jit_solution(4435032394044854606)
XLA Ops:
  0.6 0.7 broadcast_in_dim.13
  1.4 0.7 pad_maximum_fusion.2
  2.0 6.0 %all-to-all-start = ((f32[4,4,16,128]{3,2,1,0:T(8,128)}), f32[4,4,16,128]{3,2,1,0:T(8,128)S(1)}, u32[]{:S(2)}, u32[]{:S(2)}) async-start(f32[4,4,16,128]{3,2,1,0:T(8,128)} %pad_maximum_fusion.2), calls=%async_computation | async-start | bytes 262144 | tf_op jit(solution)/shard_map/all_to_all | solution.py:496
  8.1 5.2 %collective-permute-start.3 = (f32[32,16,128]{2,1,0:T(8,128)S(1)}, f32[32,16,128]{2,1,0:T(8,128)S(1)}, u32[]{:S(2)}, u32[]{:S(2)}) collective-permute-start(f32[32,16,128]{2,1,0:T(8,128)S(1)} %pad_maximum_fusion.1.fields_ref.centre_fields), channel_id=1, source_target_pairs={{4,0},{8,4},{12,8},{16,12},{20,16},{24,20},{28,24},{32,28},{36,32}... | collective-permute-start | bytes 786440 | tf_op jit(solution)/shard_map/ppermute | solution.py:493
  13.3 1.9 %collective-permute-start.2 = (f32[32,16,128]{2,1,0:T(8,128)S(1)}, f32[32,16,128]{2,1,0:T(8,128)S(1)}, u32[]{:S(2)}, u32[]{:S(2)}) collective-permute-start(f32[32,16,128]{2,1,0:T(8,128)S(1)} %pad_maximum_fusion.1.fields_ref.centre_fields), channel_id=1, source_target_pairs={{0,4},{4,8},{8,12},{12,16},{16,20},{20,24},{24,28},{28,32},{32,36}... | collective-permute-start | bytes 786440 | tf_op jit(solution)/shard_map/ppermute | solution.py:492
  15.3 0.7 pack_sides.1
  16.0 9.1 %collective-permute-start = (f32[12,16,128]{2,1,0:T(8,128)S(1)}, f32[12,16,128]{2,1,0:T(8,128)S(1)}, u32[]{:S(2)}, u32[]{:S(2)}) collective-permute-start(f32[12,16,128]{2,1,0:T(8,128)S(1)} %get-tuple-element.32), channel_id=1, source_target_pairs={{0,1},{2,3},{1,0},{3,2},{4,5},{6,7},{5,4},{7,6},{8,9},{10,11},{9,8... | collective-permute-start | bytes 294920 | tf_op jit(solution)/shard_map/ppermute | solution.py:467
  25.2 0.7 collective-permute-start.1
  25.8 6.0 %find_receivers.1 = (s32[264]{0:T(512)S(1)}, s32[264]{0:T(512)S(1)}, s32[264]{0:T(512)S(1)}, s32[1]{0:T(128)}) custom-call(s32[4]{0:T(128)S(1)} %pad_add_fusion.where_ref, s32[256]{0:T(256)S(1)} %bitcast.19), custom_call_target="tpu_custom_call" | custom-call | flops 8000 | bytes 4000 | tf_op jit(solution)/shard_map/find_receivers/pallas_call | solution.py:479
  31.9 1.9 %collective-permute-done = f32[12,16,128]{2,1,0:T(8,128)S(1)} collective-permute-done((f32[12,16,128]{2,1,0:T(8,128)S(1)}, f32[12,16,128]{2,1,0:T(8,128)S(1)}, u32[]{:S(2)}, u32[]{:S(2)}) %collective-permute-start) | collective-permute-done | bytes 98336 | tf_op jit(solution)/shard_map/ppermute | solution.py:467
  33.9 5.8 %collective-permute-start.5 = (f32[40,16,128]{2,1,0:T(8,128)S(1)}, f32[40,16,128]{2,1,0:T(8,128)S(1)}, u32[]{:S(2)}, u32[]{:S(2)}) collective-permute-start(f32[40,16,128]{2,1,0:T(8,128)S(1)} %pad_maximum_fusion.centre_ref), channel_id=1, source_target_pairs={{4,0},{8,4},{12,8},{16,12},{20,16},{24,20},{28,24},{32,28},{36,32}... | collective-permute-start | bytes 983048 | tf_op jit(solution)/shard_map/ppermute | solution.py:514
  39.6 1.9 %collective-permute-start.4 = (f32[40,16,128]{2,1,0:T(8,128)S(1)}, f32[40,16,128]{2,1,0:T(8,128)S(1)}, u32[]{:S(2)}, u32[]{:S(2)}) collective-permute-start(f32[40,16,128]{2,1,0:T(8,128)S(1)} %pad_maximum_fusion.centre_ref), channel_id=1, source_target_pairs={{0,4},{4,8},{8,12},{12,16},{16,20},{20,24},{24,28},{28,32},{32,36}... | collective-permute-start | bytes 983048 | tf_op jit(solution)/shard_map/ppermute | solution.py:513
  41.6 9.1 %collective-permute-done.4.low_ref = f32[40,16,128]{2,1,0:T(8,128)S(1)} collective-permute-done((f32[40,16,128]{2,1,0:T(8,128)S(1)}, f32[40,16,128]{2,1,0:T(8,128)S(1)}, u32[]{:S(2)}, u32[]{:S(2)}) %collective-permute-start.4) | collective-permute-done | bytes 327712 | tf_op jit(solution)/shard_map/ppermute | solution.py:513
  50.8 2.1 %collective-permute-start.6 = (f32[72,16,128]{2,1,0:T(8,128)S(1)}, f32[72,16,128]{2,1,0:T(8,128)S(1)}, u32[]{:S(2)}, u32[]{:S(2)}) collective-permute-start(f32[72,16,128]{2,1,0:T(8,128)S(1)} %slice_dynamic-update-slice_fusion.3), channel_id=1, source_target_pairs={{0,64},{64,0},{128,192},{192,128},{256,320},{320,256},{384,448},{4... | collective-permute-start | bytes 1769480 | tf_op jit(solution)/shard_map/ppermute | solution.py:519
  53.0 1.9 %collective-permute-done.6.other_ref = f32[72,16,128]{2,1,0:T(8,128)S(1)} collective-permute-done((f32[72,16,128]{2,1,0:T(8,128)S(1)}, f32[72,16,128]{2,1,0:T(8,128)S(1)}, u32[]{:S(2)}, u32[]{:S(2)}) %collective-permute-start.6) | collective-permute-done | bytes 589856 | tf_op jit(solution)/shard_map/ppermute | solution.py:519
  54.9 10.6 %first_steps.1 = (f32[40,16,128]{2,1,0:T(8,128)S(1)}, f32[16,24,128]{2,1,0:T(8,128)S(1)}, f32[16,24,128]{2,1,0:T(8,128)S(1)}, f32[16,48,128]{2,1,0:T(8,128)S(1)}...) custom-call(s32[4]{0:T(128)S(1)} %pad_add_fusion.where_ref, ...), custom_call_target="tpu_custom_call" | custom-call | tf_op jit(solution)/shard_map/first_steps/pallas_call | solution.py:436
  65.5 1.9 %collective-permute-start.8 = (f32[40,16,128]{2,1,0:T(8,128)S(1)}, f32[40,16,128]{2,1,0:T(8,128)S(1)}, u32[]{:S(2)}, u32[]{:S(2)}) collective-permute-start(f32[40,16,128]{2,1,0:T(8,128)S(1)} %get-tuple-element.45.centre_ref), channel_id=1, source_target_pairs={{4,0},{8,4},{12,8},{16,12},{20,16},{24,20},{28,24},{32,28},{36,32}... | collective-permute-start | bytes 983048 | tf_op jit(solution)/shard_map/ppermute | solution.py:526
  67.5 3.9 %collective-permute-start.7 = (f32[40,16,128]{2,1,0:T(8,128)S(1)}, f32[40,16,128]{2,1,0:T(8,128)S(1)}, u32[]{:S(2)}, u32[]{:S(2)}) collective-permute-start(f32[40,16,128]{2,1,0:T(8,128)S(1)} %get-tuple-element.45.centre_ref), channel_id=1, source_target_pairs={{0,4},{4,8},{8,12},{12,16},{16,20},{20,24},{24,28},{28,32},{32,36}... | collective-permute-start | bytes 983048 | tf_op jit(solution)/shard_map/ppermute | solution.py:525
  71.4 5.6 %collective-permute-done.8.high_ref = f32[40,16,128]{2,1,0:T(8,128)S(1)} collective-permute-done((f32[40,16,128]{2,1,0:T(8,128)S(1)}, f32[40,16,128]{2,1,0:T(8,128)S(1)}, u32[]{:S(2)}, u32[]{:S(2)}) %collective-permute-start.8) | collective-permute-done | bytes 327712 | tf_op jit(solution)/shard_map/ppermute | solution.py:526
  77.0 4.0 %collective-permute-done.7.low_ref = f32[40,16,128]{2,1,0:T(8,128)S(1)} collective-permute-done((f32[40,16,128]{2,1,0:T(8,128)S(1)}, f32[40,16,128]{2,1,0:T(8,128)S(1)}, u32[]{:S(2)}, u32[]{:S(2)}) %collective-permute-start.7) | collective-permute-done | bytes 327712 | tf_op jit(solution)/shard_map/ppermute | solution.py:525
  81.1 8.6 %second_steps.1 = (f32[16,16,128]{2,1,0:T(8,128)}, f32[16,16,128]{2,1,0:T(8,128)}, f32[4,4,16,128]{3,2,1,0:T(8,128)S(1)}, f32[4,4,16,128]{3,2,1,0:T(8,128)S(1)}) custom-call(s32[4]{0:T(128)S(1)} %pad_add_fusion.where_ref, s32[264]{0:T(512)S(1)} %get-tuple-element.38.place_ref, s32[264]{0:T(512)S(1)} %get-tuple-element.39.which_ref, ...), custom_call_target="tpu_custom_call" | custom-call | tf_op jit(solution)/shard_map/second_steps/pallas_call | solution.py:453
  89.7 1.9 %collective-permute-start.9 = (f32[4,4,16,128]{3,2,1,0:T(8,128)S(1)}, f32[4,4,16,128]{3,2,1,0:T(8,128)S(1)}, u32[]{:S(2)}, u32[]{:S(2)}) collective-permute-start(f32[4,4,16,128]{3,2,1,0:T(8,128)S(1)} %get-tuple-element.57), channel_id=1, source_target_pairs={{0,64},{64,0},{128,192},{192,128},{256,320},{320,256},{384,448},{4... | collective-permute-start | bytes 393224 | tf_op jit(solution)/shard_map/ppermute | solution.py:528
  91.6 1.3 %collective-permute-done.9 = f32[4,4,16,128]{3,2,1,0:T(8,128)S(1)} collective-permute-done((f32[4,4,16,128]{3,2,1,0:T(8,128)S(1)}, f32[4,4,16,128]{3,2,1,0:T(8,128)S(1)}, u32[]{:S(2)}, u32[]{:S(2)}) %collective-permute-start.9) | collective-permute-done | bytes 131104 | tf_op jit(solution)/shard_map/ppermute | solution.py:528
  92.9 11.5 %all_to_all.10 = f32[4,4,16,128]{3,2,1,0:T(8,128)S(1)} all-to-all(f32[4,4,16,128]{3,2,1,0:T(8,128)S(1)} %add.12), channel_id=1, replica_groups={{0,128,256,384},{64,192,320,448},{1,129,257,385},{65,193,321,449},{2,13..., dimensions={0} | all-to-all | bytes 262144 | tf_op jit(solution)/shard_map/all_to_all | solution.py:529
  (42 shorter events, 0.9 us)
Async XLA Ops:
  0.6 0.7 copy-start.9
  2.0 6.0 %copy-start.7 = (f32[1,16,16,128]{3,2,1,0:T(8,128)S(1)}, f32[1,16,16,128]{3,2,1,0:T(8,128)}, u32[]{:S(2)}) copy-start(f32[1,16,16,128]{3,2,1,0:T(8,128)} %param.15) | copy-start | bytes 393220
  2.0 6.0 %copy-start.8 = (f32[1,16,16,128]{3,2,1,0:T(8,128)S(1)}, f32[1,16,16,128]{3,2,1,0:T(8,128)}, u32[]{:S(2)}) copy-start(f32[1,16,16,128]{3,2,1,0:T(8,128)} %param.14) | copy-start | bytes 393220
  2.0 13.3 %all-to-all-start = ((f32[4,4,16,128]{3,2,1,0:T(8,128)}), f32[4,4,16,128]{3,2,1,0:T(8,128)S(1)}, u32[]{:S(2)}, u32[]{:S(2)}) async-start(f32[4,4,16,128]{3,2,1,0:T(8,128)} %pad_maximum_fusion.2), calls=%async_computation | async-start | bytes 262144 | tf_op jit(solution)/shard_map/all_to_all | solution.py:496
  8.1 25.7 %collective-permute-start.3 = (f32[32,16,128]{2,1,0:T(8,128)S(1)}, f32[32,16,128]{2,1,0:T(8,128)S(1)}, u32[]{:S(2)}, u32[]{:S(2)}) collective-permute-start(f32[32,16,128]{2,1,0:T(8,128)S(1)} %pad_maximum_fusion.1.fields_ref.centre_fields), channel_id=1, source_target_pairs={{4,0},{8,4},{12,8},{16,12},{20,16},{24,20},{28,24},{32,28},{36,32}... | collective-permute-start | bytes 786440 | tf_op jit(solution)/shard_map/ppermute | solution.py:493
  13.3 20.6 %collective-permute-start.2 = (f32[32,16,128]{2,1,0:T(8,128)S(1)}, f32[32,16,128]{2,1,0:T(8,128)S(1)}, u32[]{:S(2)}, u32[]{:S(2)}) collective-permute-start(f32[32,16,128]{2,1,0:T(8,128)S(1)} %pad_maximum_fusion.1.fields_ref.centre_fields), channel_id=1, source_target_pairs={{0,4},{4,8},{8,12},{12,16},{16,20},{20,24},{24,28},{28,32},{32,36}... | collective-permute-start | bytes 786440 | tf_op jit(solution)/shard_map/ppermute | solution.py:492
  16.0 17.8 %collective-permute-start = (f32[12,16,128]{2,1,0:T(8,128)S(1)}, f32[12,16,128]{2,1,0:T(8,128)S(1)}, u32[]{:S(2)}, u32[]{:S(2)}) collective-permute-start(f32[12,16,128]{2,1,0:T(8,128)S(1)} %get-tuple-element.32), channel_id=1, source_target_pairs={{0,1},{2,3},{1,0},{3,2},{4,5},{6,7},{5,4},{7,6},{8,9},{10,11},{9,8... | collective-permute-start | bytes 294920 | tf_op jit(solution)/shard_map/ppermute | solution.py:467
  25.1 0.7 copy-start.5
  25.2 8.7 %collective-permute-start.1 = (f32[12,16,128]{2,1,0:T(8,128)S(1)}, f32[12,16,128]{2,1,0:T(8,128)S(1)}, u32[]{:S(2)}, u32[]{:S(2)}) collective-permute-start(f32[12,16,128]{2,1,0:T(8,128)S(1)} %get-tuple-element.33), channel_id=1, source_target_pairs={{1,2},{2,1},{5,6},{6,5},{9,10},{10,9},{13,14},{14,13},{17,18},{18,... | collective-permute-start | bytes 294920 | tf_op jit(solution)/shard_map/ppermute | solution.py:467
  33.9 16.9 %collective-permute-start.5 = (f32[40,16,128]{2,1,0:T(8,128)S(1)}, f32[40,16,128]{2,1,0:T(8,128)S(1)}, u32[]{:S(2)}, u32[]{:S(2)}) collective-permute-start(f32[40,16,128]{2,1,0:T(8,128)S(1)} %pad_maximum_fusion.centre_ref), channel_id=1, source_target_pairs={{4,0},{8,4},{12,8},{16,12},{20,16},{24,20},{28,24},{32,28},{36,32}... | collective-permute-start | bytes 983048 | tf_op jit(solution)/shard_map/ppermute | solution.py:514
  39.6 11.1 %collective-permute-start.4 = (f32[40,16,128]{2,1,0:T(8,128)S(1)}, f32[40,16,128]{2,1,0:T(8,128)S(1)}, u32[]{:S(2)}, u32[]{:S(2)}) collective-permute-start(f32[40,16,128]{2,1,0:T(8,128)S(1)} %pad_maximum_fusion.centre_ref), channel_id=1, source_target_pairs={{0,4},{4,8},{8,12},{12,16},{16,20},{20,24},{24,28},{28,32},{32,36}... | collective-permute-start | bytes 983048 | tf_op jit(solution)/shard_map/ppermute | solution.py:513
  41.6 11.3 %copy-start.6 = (bf16[1,8,16,16,128]{4,3,2,1,0:T(8,128)(2,1)S(1)}, bf16[1,8,16,16,128]{4,3,2,1,0:T(8,128)(2,1)}, u32[]{:S(2)}) copy-start(bf16[1,8,16,16,128]{4,3,2,1,0:T(8,128)(2,1)} %param.13) | copy-start | bytes 1572868
  50.8 4.1 %copy-start.2 = (bf16[2,256,256]{2,1,0:T(8,128)(2,1)S(1)}, bf16[2,256,256]{2,1,0:T(8,128)(2,1)}, u32[]{:S(2)}) copy-start(bf16[2,256,256]{2,1,0:T(8,128)(2,1)} %constant.54.clone.layer_w) | copy-start | bytes 786436
  50.8 4.0 %copy-start.3 = (bf16[384,256]{1,0:T(8,128)(2,1)S(1)}, bf16[384,256]{1,0:T(8,128)(2,1)}, u32[]{:S(2)}) copy-start(bf16[384,256]{1,0:T(8,128)(2,1)} %constant.55.clone.side_w) | copy-start | bytes 589828
  50.8 4.0 %collective-permute-start.6 = (f32[72,16,128]{2,1,0:T(8,128)S(1)}, f32[72,16,128]{2,1,0:T(8,128)S(1)}, u32[]{:S(2)}, u32[]{:S(2)}) collective-permute-start(f32[72,16,128]{2,1,0:T(8,128)S(1)} %slice_dynamic-update-slice_fusion.3), channel_id=1, source_target_pairs={{0,64},{64,0},{128,192},{192,128},{256,320},{320,256},{384,448},{4... | collective-permute-start | bytes 1769480 | tf_op jit(solution)/shard_map/ppermute | solution.py:519
  52.9 2.0 %copy-start.4 = (f32[1,8,256]{2,1,0:T(8,128)S(1)}, f32[1,8,256]{2,1,0:T(8,128)}, u32[]{:S(2)}) copy-start(f32[1,8,256]{2,1,0:T(8,128)} %param.17) | copy-start | bytes 24580
  54.9 26.2 %copy-start = (bf16[4,256,256]{2,1,0:T(8,128)(2,1)S(1)}, bf16[4,256,256]{2,1,0:T(8,128)(2,1)}, u32[]{:S(2)}) copy-start(bf16[4,256,256]{2,1,0:T(8,128)(2,1)} %constant.56.clone.layer_w) | copy-start | bytes 1572868
  54.9 26.2 %copy-start.1 = (bf16[640,256]{1,0:T(8,128)(2,1)S(1)}, bf16[640,256]{1,0:T(8,128)(2,1)}, u32[]{:S(2)}) copy-start(bf16[640,256]{1,0:T(8,128)(2,1)} %constant.57.clone.side_w) | copy-start | bytes 983044
  65.5 11.5 %collective-permute-start.8 = (f32[40,16,128]{2,1,0:T(8,128)S(1)}, f32[40,16,128]{2,1,0:T(8,128)S(1)}, u32[]{:S(2)}, u32[]{:S(2)}) collective-permute-start(f32[40,16,128]{2,1,0:T(8,128)S(1)} %get-tuple-element.45.centre_ref), channel_id=1, source_target_pairs={{4,0},{8,4},{12,8},{16,12},{20,16},{24,20},{28,24},{32,28},{36,32}... | collective-permute-start | bytes 983048 | tf_op jit(solution)/shard_map/ppermute | solution.py:526
  67.5 13.6 %collective-permute-start.7 = (f32[40,16,128]{2,1,0:T(8,128)S(1)}, f32[40,16,128]{2,1,0:T(8,128)S(1)}, u32[]{:S(2)}, u32[]{:S(2)}) collective-permute-start(f32[40,16,128]{2,1,0:T(8,128)S(1)} %get-tuple-element.45.centre_ref), channel_id=1, source_target_pairs={{0,4},{4,8},{8,12},{12,16},{16,20},{20,24},{24,28},{28,32},{32,36}... | collective-permute-start | bytes 983048 | tf_op jit(solution)/shard_map/ppermute | solution.py:525
  89.7 3.2 %collective-permute-start.9 = (f32[4,4,16,128]{3,2,1,0:T(8,128)S(1)}, f32[4,4,16,128]{3,2,1,0:T(8,128)S(1)}, u32[]{:S(2)}, u32[]{:S(2)}) collective-permute-start(f32[4,4,16,128]{3,2,1,0:T(8,128)S(1)} %get-tuple-element.57), channel_id=1, source_target_pairs={{0,64},{64,0},{128,192},{192,128},{256,320},{320,256},{384,448},{4... | collective-permute-start | bytes 393224 | tf_op jit(solution)/shard_map/ppermute | solution.py:528

commit v4 on v3

--- a/solution.py
+++ b/solution.py
@@ -69,7 +69,12 @@
         which_ref[count] = j
         return count + inside.astype(jnp.int32)
 
-    count_ref[0] = lax.fori_loop(0, RECV, body, jnp.int32(0), unroll=4)
+    count = lax.fori_loop(0, RECV, body, jnp.int32(0), unroll=4)
+    count_ref[0] = count
+    for u in range(3):
+        place_ref[count + u] = (4 * 64 + PAD) * 256 + 255
+        place4_ref[count + u] = (4 * 64 + PAD) * 256 + 255
+        which_ref[count + u] = 0
 
 
 def pack_kernel(where_ref, fields_ref, model_ref, first_ref, second_ref):
@@ -187,9 +192,11 @@
 
     def product(pieces, weights, first):
         weights = weights if lap_too else weights[:, BY:]
-        found = jnp.dot(
-            jnp.concatenate(pieces, axis=1), jnp.concatenate([weights] * PARTS, axis=0), preferred_element_type=jnp.float32
-        )
+        stacked = jnp.concatenate([weights] * PARTS, axis=0)
+        joined = jnp.concatenate(pieces, axis=1)
+        half = per * n // 2 if first == NZ else per * n
+        found = [jnp.dot(joined[i : i + half], stacked, preferred_element_type=jnp.float32) for i in range(0, per * n, half)]
+        found = jnp.concatenate(found, axis=0) if len(found) > 1 else found[0]
         if lap_too:
             y_lap[first : first + per, pl.ds(start, n), :] = found[:, :BY].reshape(per, n, BY)
         y_slope[first : first + per, pl.ds(start, n), :] = found[:, -BY:].reshape(per, n, BY)
@@ -242,13 +249,15 @@
     for j, plan in enumerate(PLANS):
 
         def add(i, _, cur=cur, step=first_step + j):
-            place = place_ref[i]
-            value = trace_ref[step, which_ref[i]]
-            spot = (lax.shift_right_logical(place, 14), pl.ds(lax.shift_right_logical(place, 8) & 63, 1), slice(None))
-            cur[spot] = cur[spot] + jnp.where(lane1 == (place & 255), value, 0.0)
+            for u in range(4):
+                place = place_ref[4 * i + u]
+                value = trace_ref[step, which_ref[4 * i + u]]
+                row = lax.shift_right_logical(place, 8) & 63
+                spot = (lax.shift_right_logical(place, 14), pl.ds(row, 1), slice(None))
+                cur[spot] = cur[spot] + jnp.where(lane1 == (place & 255), value, 0.0)
             return 0
 
-        lax.fori_loop(0, count_ref[0], add, 0)
+        lax.fori_loop(0, lax.shift_right_logical(count_ref[0] + 3, 2), add, 0)
         sides = not (last and j == ROUND - 1)
         shift_along_y(cur, groups, *WINDOWS[j], work, sides)
 

time: 106 us -> 104 us (0.981)
  Pallas kernels: 25.9 us -> 24.2 us
where the time goes in v4:
time: 104 us
  starting transfers between devices  40.4 us (39%)
  Pallas kernels  24.2 us (23%)
  waiting for transfers between devices  24 us (23%)
  blocking collectives  11.9 us (11%)
  other arithmetic  1.43 us (1%)
    all_to_all x1, blocking collectives, shards(): lax.all_to_all(pair, 'shot', 0, 0, axis_index_groups=same_core)  11.9 us
    ppermute x2, starting transfers between devices, swap(): lax.ppermute(x, axis, [(a, b) for a, b in pairs] + [(b, a) for a, b in pa...  9.76 us
    pallas_call x1, Pallas kernels, steps_one(): pl.pallas_call(first_kernel, out_shape=(shape(40, BX, BY), image, image)...  9.63 us
    ppermute x1, waiting for transfers between devices, shards(): low = lax.ppermute(centre, 'gx', up)  9.09 us
    pallas_call x1, Pallas kernels, steps_two(): pl.pallas_call(second_kernel, out_shape=(shape(NZ, BX, BY),) * 2 + (shape...  7.86 us
    pallas_call x1, Pallas kernels, shards(): pl.pallas_call(find_kernel, out_shape=(listed, listed, listed, shape(1, d...  6.04 us
    all_to_all x1, starting transfers between devices, shards(): lax.all_to_all(own, 'shot', 0, 0, axis_index_groups=same_core)  6.03 us
    ppermute x1, starting transfers between devices, shards(): high = lax.ppermute(centre, 'gx', down)  5.75 us
  transfers between devices with their start and end apart: 11, of which 6 were waited for; matrix products, arithmetic and copies ran while one was open for 0% of the time, Pallas kernels for 6%

profile of v4, /device:TPU:6, one launch (start us, length us, event | category | flops | bytes accessed | tf_op | source)
XLA Modules:
  0.0 103.8 jit_solution(11292891780981804879)
XLA Ops:
  0.6 0.7 broadcast_in_dim.13
  1.4 0.7 pad_maximum_fusion.2
  2.0 6.0 %all-to-all-start = ((f32[4,4,16,128]{3,2,1,0:T(8,128)}), f32[4,4,16,128]{3,2,1,0:T(8,128)S(1)}, u32[]{:S(2)}, u32[]{:S(2)}) async-start(f32[4,4,16,128]{3,2,1,0:T(8,128)} %pad_maximum_fusion.2), calls=%async_computation | async-start | bytes 262144 | tf_op jit(solution)/shard_map/all_to_all | solution.py:505
  8.1 5.2 %collective-permute-start.3 = (f32[32,16,128]{2,1,0:T(8,128)S(1)}, f32[32,16,128]{2,1,0:T(8,128)S(1)}, u32[]{:S(2)}, u32[]{:S(2)}) collective-permute-start(f32[32,16,128]{2,1,0:T(8,128)S(1)} %pad_maximum_fusion.1.fields_ref.centre_fields), channel_id=1, source_target_pairs={{4,0},{8,4},{12,8},{16,12},{20,16},{24,20},{28,24},{32,28},{36,32}... | collective-permute-start | bytes 786440 | tf_op jit(solution)/shard_map/ppermute | solution.py:502
  13.3 1.9 %collective-permute-start.2 = (f32[32,16,128]{2,1,0:T(8,128)S(1)}, f32[32,16,128]{2,1,0:T(8,128)S(1)}, u32[]{:S(2)}, u32[]{:S(2)}) collective-permute-start(f32[32,16,128]{2,1,0:T(8,128)S(1)} %pad_maximum_fusion.1.fields_ref.centre_fields), channel_id=1, source_target_pairs={{0,4},{4,8},{8,12},{12,16},{16,20},{20,24},{24,28},{28,32},{32,36}... | collective-permute-start | bytes 786440 | tf_op jit(solution)/shard_map/ppermute | solution.py:501
  15.3 0.7 pack_sides.1
  16.0 9.1 %collective-permute-start = (f32[12,16,128]{2,1,0:T(8,128)S(1)}, f32[12,16,128]{2,1,0:T(8,128)S(1)}, u32[]{:S(2)}, u32[]{:S(2)}) collective-permute-start(f32[12,16,128]{2,1,0:T(8,128)S(1)} %get-tuple-element.32), channel_id=1, source_target_pairs={{0,1},{2,3},{1,0},{3,2},{4,5},{6,7},{5,4},{7,6},{8,9},{10,11},{9,8... | collective-permute-start | bytes 294920 | tf_op jit(solution)/shard_map/ppermute | solution.py:476
  25.2 0.7 collective-permute-start.1
  25.8 6.0 %find_receivers.1 = (s32[264]{0:T(512)S(1)}, s32[264]{0:T(512)S(1)}, s32[264]{0:T(512)S(1)}, s32[1]{0:T(128)}) custom-call(s32[4]{0:T(128)S(1)} %pad_add_fusion.where_ref, s32[256]{0:T(256)S(1)} %bitcast.19), custom_call_target="tpu_custom_call" | custom-call | flops 8000 | bytes 4000 | tf_op jit(solution)/shard_map/find_receivers/pallas_call | solution.py:488
  31.9 1.9 %collective-permute-done = f32[12,16,128]{2,1,0:T(8,128)S(1)} collective-permute-done((f32[12,16,128]{2,1,0:T(8,128)S(1)}, f32[12,16,128]{2,1,0:T(8,128)S(1)}, u32[]{:S(2)}, u32[]{:S(2)}) %collective-permute-start) | collective-permute-done | bytes 98336 | tf_op jit(solution)/shard_map/ppermute | solution.py:476
  33.9 5.8 %collective-permute-start.5 = (f32[40,16,128]{2,1,0:T(8,128)S(1)}, f32[40,16,128]{2,1,0:T(8,128)S(1)}, u32[]{:S(2)}, u32[]{:S(2)}) collective-permute-start(f32[40,16,128]{2,1,0:T(8,128)S(1)} %pad_maximum_fusion.centre_ref), channel_id=1, source_target_pairs={{4,0},{8,4},{12,8},{16,12},{20,16},{24,20},{28,24},{32,28},{36,32}... | collective-permute-start | bytes 983048 | tf_op jit(solution)/shard_map/ppermute | solution.py:523
  39.6 1.9 %collective-permute-start.4 = (f32[40,16,128]{2,1,0:T(8,128)S(1)}, f32[40,16,128]{2,1,0:T(8,128)S(1)}, u32[]{:S(2)}, u32[]{:S(2)}) collective-permute-start(f32[40,16,128]{2,1,0:T(8,128)S(1)} %pad_maximum_fusion.centre_ref), channel_id=1, source_target_pairs={{0,4},{4,8},{8,12},{12,16},{16,20},{20,24},{24,28},{28,32},{32,36}... | collective-permute-start | bytes 983048 | tf_op jit(solution)/shard_map/ppermute | solution.py:522
  41.6 9.1 %collective-permute-done.4.low_ref = f32[40,16,128]{2,1,0:T(8,128)S(1)} collective-permute-done((f32[40,16,128]{2,1,0:T(8,128)S(1)}, f32[40,16,128]{2,1,0:T(8,128)S(1)}, u32[]{:S(2)}, u32[]{:S(2)}) %collective-permute-start.4) | collective-permute-done | bytes 327712 | tf_op jit(solution)/shard_map/ppermute | solution.py:522
  50.8 2.1 %collective-permute-start.6 = (f32[72,16,128]{2,1,0:T(8,128)S(1)}, f32[72,16,128]{2,1,0:T(8,128)S(1)}, u32[]{:S(2)}, u32[]{:S(2)}) collective-permute-start(f32[72,16,128]{2,1,0:T(8,128)S(1)} %slice_dynamic-update-slice_fusion.3), channel_id=1, source_target_pairs={{0,64},{64,0},{128,192},{192,128},{256,320},{320,256},{384,448},{4... | collective-permute-start | bytes 1769480 | tf_op jit(solution)/shard_map/ppermute | solution.py:528
  53.0 1.9 %collective-permute-done.6.other_ref = f32[72,16,128]{2,1,0:T(8,128)S(1)} collective-permute-done((f32[72,16,128]{2,1,0:T(8,128)S(1)}, f32[72,16,128]{2,1,0:T(8,128)S(1)}, u32[]{:S(2)}, u32[]{:S(2)}) %collective-permute-start.6) | collective-permute-done | bytes 589856 | tf_op jit(solution)/shard_map/ppermute | solution.py:528
  54.9 9.6 %first_steps.1 = (f32[40,16,128]{2,1,0:T(8,128)S(1)}, f32[16,24,128]{2,1,0:T(8,128)S(1)}, f32[16,24,128]{2,1,0:T(8,128)S(1)}, f32[16,48,128]{2,1,0:T(8,128)S(1)}...) custom-call(s32[4]{0:T(128)S(1)} %pad_add_fusion.where_ref, ...), custom_call_target="tpu_custom_call" | custom-call | tf_op jit(solution)/shard_map/first_steps/pallas_call | solution.py:445
  64.5 1.9 %collective-permute-start.8 = (f32[40,16,128]{2,1,0:T(8,128)S(1)}, f32[40,16,128]{2,1,0:T(8,128)S(1)}, u32[]{:S(2)}, u32[]{:S(2)}) collective-permute-start(f32[40,16,128]{2,1,0:T(8,128)S(1)} %get-tuple-element.45.centre_ref), channel_id=1, source_target_pairs={{4,0},{8,4},{12,8},{16,12},{20,16},{24,20},{28,24},{32,28},{36,32}... | collective-permute-start | bytes 983048 | tf_op jit(solution)/shard_map/ppermute | solution.py:535
  66.5 3.9 %collective-permute-start.7 = (f32[40,16,128]{2,1,0:T(8,128)S(1)}, f32[40,16,128]{2,1,0:T(8,128)S(1)}, u32[]{:S(2)}, u32[]{:S(2)}) collective-permute-start(f32[40,16,128]{2,1,0:T(8,128)S(1)} %get-tuple-element.45.centre_ref), channel_id=1, source_target_pairs={{0,4},{4,8},{8,12},{12,16},{16,20},{20,24},{24,28},{28,32},{32,36}... | collective-permute-start | bytes 983048 | tf_op jit(solution)/shard_map/ppermute | solution.py:534
  70.4 5.8 %collective-permute-done.8.high_ref = f32[40,16,128]{2,1,0:T(8,128)S(1)} collective-permute-done((f32[40,16,128]{2,1,0:T(8,128)S(1)}, f32[40,16,128]{2,1,0:T(8,128)S(1)}, u32[]{:S(2)}, u32[]{:S(2)}) %collective-permute-start.8) | collective-permute-done | bytes 327712 | tf_op jit(solution)/shard_map/ppermute | solution.py:535
  76.1 4.0 %collective-permute-done.7.low_ref = f32[40,16,128]{2,1,0:T(8,128)S(1)} collective-permute-done((f32[40,16,128]{2,1,0:T(8,128)S(1)}, f32[40,16,128]{2,1,0:T(8,128)S(1)}, u32[]{:S(2)}, u32[]{:S(2)}) %collective-permute-start.7) | collective-permute-done | bytes 327712 | tf_op jit(solution)/shard_map/ppermute | solution.py:534
  80.2 7.9 %second_steps.1 = (f32[16,16,128]{2,1,0:T(8,128)}, f32[16,16,128]{2,1,0:T(8,128)}, f32[4,4,16,128]{3,2,1,0:T(8,128)S(1)}, f32[4,4,16,128]{3,2,1,0:T(8,128)S(1)}) custom-call(s32[4]{0:T(128)S(1)} %pad_add_fusion.where_ref, s32[264]{0:T(512)S(1)} %get-tuple-element.38.place_ref, s32[264]{0:T(512)S(1)} %get-tuple-element.39.which_ref, ...), custom_call_target="tpu_custom_call" | custom-call | tf_op jit(solution)/shard_map/second_steps/pallas_call | solution.py:462
  88.0 1.9 %collective-permute-start.9 = (f32[4,4,16,128]{3,2,1,0:T(8,128)S(1)}, f32[4,4,16,128]{3,2,1,0:T(8,128)S(1)}, u32[]{:S(2)}, u32[]{:S(2)}) collective-permute-start(f32[4,4,16,128]{3,2,1,0:T(8,128)S(1)} %get-tuple-element.57), channel_id=1, source_target_pairs={{0,64},{64,0},{128,192},{192,128},{256,320},{320,256},{384,448},{4... | collective-permute-start | bytes 393224 | tf_op jit(solution)/shard_map/ppermute | solution.py:537
  90.0 1.3 %collective-permute-done.9 = f32[4,4,16,128]{3,2,1,0:T(8,128)S(1)} collective-permute-done((f32[4,4,16,128]{3,2,1,0:T(8,128)S(1)}, f32[4,4,16,128]{3,2,1,0:T(8,128)S(1)}, u32[]{:S(2)}, u32[]{:S(2)}) %collective-permute-start.9) | collective-permute-done | bytes 131104 | tf_op jit(solution)/shard_map/ppermute | solution.py:537
  91.3 11.9 %all_to_all.10 = f32[4,4,16,128]{3,2,1,0:T(8,128)S(1)} all-to-all(f32[4,4,16,128]{3,2,1,0:T(8,128)S(1)} %add.12), channel_id=1, replica_groups={{0,128,256,384},{64,192,320,448},{1,129,257,385},{65,193,321,449},{2,13..., dimensions={0} | all-to-all | bytes 262144 | tf_op jit(solution)/shard_map/all_to_all | solution.py:538
  (42 shorter events, 0.9 us)
Async XLA Ops:
  0.6 0.7 copy-start.9
  2.0 6.0 %copy-start.7 = (f32[1,16,16,128]{3,2,1,0:T(8,128)S(1)}, f32[1,16,16,128]{3,2,1,0:T(8,128)}, u32[]{:S(2)}) copy-start(f32[1,16,16,128]{3,2,1,0:T(8,128)} %param.15) | copy-start | bytes 393220
  2.0 6.0 %copy-start.8 = (f32[1,16,16,128]{3,2,1,0:T(8,128)S(1)}, f32[1,16,16,128]{3,2,1,0:T(8,128)}, u32[]{:S(2)}) copy-start(f32[1,16,16,128]{3,2,1,0:T(8,128)} %param.14) | copy-start | bytes 393220
  2.0 13.3 %all-to-all-start = ((f32[4,4,16,128]{3,2,1,0:T(8,128)}), f32[4,4,16,128]{3,2,1,0:T(8,128)S(1)}, u32[]{:S(2)}, u32[]{:S(2)}) async-start(f32[4,4,16,128]{3,2,1,0:T(8,128)} %pad_maximum_fusion.2), calls=%async_computation | async-start | bytes 262144 | tf_op jit(solution)/shard_map/all_to_all | solution.py:505
  8.1 25.7 %collective-permute-start.3 = (f32[32,16,128]{2,1,0:T(8,128)S(1)}, f32[32,16,128]{2,1,0:T(8,128)S(1)}, u32[]{:S(2)}, u32[]{:S(2)}) collective-permute-start(f32[32,16,128]{2,1,0:T(8,128)S(1)} %pad_maximum_fusion.1.fields_ref.centre_fields), channel_id=1, source_target_pairs={{4,0},{8,4},{12,8},{16,12},{20,16},{24,20},{28,24},{32,28},{36,32}... | collective-permute-start | bytes 786440 | tf_op jit(solution)/shard_map/ppermute | solution.py:502
  13.3 20.6 %collective-permute-start.2 = (f32[32,16,128]{2,1,0:T(8,128)S(1)}, f32[32,16,128]{2,1,0:T(8,128)S(1)}, u32[]{:S(2)}, u32[]{:S(2)}) collective-permute-start(f32[32,16,128]{2,1,0:T(8,128)S(1)} %pad_maximum_fusion.1.fields_ref.centre_fields), channel_id=1, source_target_pairs={{0,4},{4,8},{8,12},{12,16},{16,20},{20,24},{24,28},{28,32},{32,36}... | collective-permute-start | bytes 786440 | tf_op jit(solution)/shard_map/ppermute | solution.py:501
  16.0 17.8 %collective-permute-start = (f32[12,16,128]{2,1,0:T(8,128)S(1)}, f32[12,16,128]{2,1,0:T(8,128)S(1)}, u32[]{:S(2)}, u32[]{:S(2)}) collective-permute-start(f32[12,16,128]{2,1,0:T(8,128)S(1)} %get-tuple-element.32), channel_id=1, source_target_pairs={{0,1},{2,3},{1,0},{3,2},{4,5},{6,7},{5,4},{7,6},{8,9},{10,11},{9,8... | collective-permute-start | bytes 294920 | tf_op jit(solution)/shard_map/ppermute | solution.py:476
  25.1 0.7 copy-start.5
  25.2 8.7 %collective-permute-start.1 = (f32[12,16,128]{2,1,0:T(8,128)S(1)}, f32[12,16,128]{2,1,0:T(8,128)S(1)}, u32[]{:S(2)}, u32[]{:S(2)}) collective-permute-start(f32[12,16,128]{2,1,0:T(8,128)S(1)} %get-tuple-element.33), channel_id=1, source_target_pairs={{1,2},{2,1},{5,6},{6,5},{9,10},{10,9},{13,14},{14,13},{17,18},{18,... | collective-permute-start | bytes 294920 | tf_op jit(solution)/shard_map/ppermute | solution.py:476
  33.9 16.9 %collective-permute-start.5 = (f32[40,16,128]{2,1,0:T(8,128)S(1)}, f32[40,16,128]{2,1,0:T(8,128)S(1)}, u32[]{:S(2)}, u32[]{:S(2)}) collective-permute-start(f32[40,16,128]{2,1,0:T(8,128)S(1)} %pad_maximum_fusion.centre_ref), channel_id=1, source_target_pairs={{4,0},{8,4},{12,8},{16,12},{20,16},{24,20},{28,24},{32,28},{36,32}... | collective-permute-start | bytes 983048 | tf_op jit(solution)/shard_map/ppermute | solution.py:523
  39.6 11.1 %collective-permute-start.4 = (f32[40,16,128]{2,1,0:T(8,128)S(1)}, f32[40,16,128]{2,1,0:T(8,128)S(1)}, u32[]{:S(2)}, u32[]{:S(2)}) collective-permute-start(f32[40,16,128]{2,1,0:T(8,128)S(1)} %pad_maximum_fusion.centre_ref), channel_id=1, source_target_pairs={{0,4},{4,8},{8,12},{12,16},{16,20},{20,24},{24,28},{28,32},{32,36}... | collective-permute-start | bytes 983048 | tf_op jit(solution)/shard_map/ppermute | solution.py:522
  41.6 11.3 %copy-start.6 = (bf16[1,8,16,16,128]{4,3,2,1,0:T(8,128)(2,1)S(1)}, bf16[1,8,16,16,128]{4,3,2,1,0:T(8,128)(2,1)}, u32[]{:S(2)}) copy-start(bf16[1,8,16,16,128]{4,3,2,1,0:T(8,128)(2,1)} %param.13) | copy-start | bytes 1572868
  50.8 4.1 %copy-start.2 = (bf16[2,256,256]{2,1,0:T(8,128)(2,1)S(1)}, bf16[2,256,256]{2,1,0:T(8,128)(2,1)}, u32[]{:S(2)}) copy-start(bf16[2,256,256]{2,1,0:T(8,128)(2,1)} %constant.54.clone.layer_w) | copy-start | bytes 786436
  50.8 4.0 %copy-start.3 = (bf16[384,256]{1,0:T(8,128)(2,1)S(1)}, bf16[384,256]{1,0:T(8,128)(2,1)}, u32[]{:S(2)}) copy-start(bf16[384,256]{1,0:T(8,128)(2,1)} %constant.55.clone.side_w) | copy-start | bytes 589828
  50.8 4.0 %collective-permute-start.6 = (f32[72,16,128]{2,1,0:T(8,128)S(1)}, f32[72,16,128]{2,1,0:T(8,128)S(1)}, u32[]{:S(2)}, u32[]{:S(2)}) collective-permute-start(f32[72,16,128]{2,1,0:T(8,128)S(1)} %slice_dynamic-update-slice_fusion.3), channel_id=1, source_target_pairs={{0,64},{64,0},{128,192},{192,128},{256,320},{320,256},{384,448},{4... | collective-permute-start | bytes 1769480 | tf_op jit(solution)/shard_map/ppermute | solution.py:528
  52.9 2.0 %copy-start.4 = (f32[1,8,256]{2,1,0:T(8,128)S(1)}, f32[1,8,256]{2,1,0:T(8,128)}, u32[]{:S(2)}) copy-start(f32[1,8,256]{2,1,0:T(8,128)} %param.17) | copy-start | bytes 24580
  54.9 25.3 %copy-start = (bf16[4,256,256]{2,1,0:T(8,128)(2,1)S(1)}, bf16[4,256,256]{2,1,0:T(8,128)(2,1)}, u32[]{:S(2)}) copy-start(bf16[4,256,256]{2,1,0:T(8,128)(2,1)} %constant.56.clone.layer_w) | copy-start | bytes 1572868
  54.9 25.3 %copy-start.1 = (bf16[640,256]{1,0:T(8,128)(2,1)S(1)}, bf16[640,256]{1,0:T(8,128)(2,1)}, u32[]{:S(2)}) copy-start(bf16[640,256]{1,0:T(8,128)(2,1)} %constant.57.clone.side_w) | copy-start | bytes 983044
  64.5 11.6 %collective-permute-start.8 = (f32[40,16,128]{2,1,0:T(8,128)S(1)}, f32[40,16,128]{2,1,0:T(8,128)S(1)}, u32[]{:S(2)}, u32[]{:S(2)}) collective-permute-start(f32[40,16,128]{2,1,0:T(8,128)S(1)} %get-tuple-element.45.centre_ref), channel_id=1, source_target_pairs={{4,0},{8,4},{12,8},{16,12},{20,16},{24,20},{28,24},{32,28},{36,32}... | collective-permute-start | bytes 983048 | tf_op jit(solution)/shard_map/ppermute | solution.py:535
  66.5 13.7 %collective-permute-start.7 = (f32[40,16,128]{2,1,0:T(8,128)S(1)}, f32[40,16,128]{2,1,0:T(8,128)S(1)}, u32[]{:S(2)}, u32[]{:S(2)}) collective-permute-start(f32[40,16,128]{2,1,0:T(8,128)S(1)} %get-tuple-element.45.centre_ref), channel_id=1, source_target_pairs={{0,4},{4,8},{8,12},{12,16},{16,20},{20,24},{24,28},{28,32},{32,36}... | collective-permute-start | bytes 983048 | tf_op jit(solution)/shard_map/ppermute | solution.py:534
  88.0 3.2 %collective-permute-start.9 = (f32[4,4,16,128]{3,2,1,0:T(8,128)S(1)}, f32[4,4,16,128]{3,2,1,0:T(8,128)S(1)}, u32[]{:S(2)}, u32[]{:S(2)}) collective-permute-start(f32[4,4,16,128]{3,2,1,0:T(8,128)S(1)} %get-tuple-element.57), channel_id=1, source_target_pairs={{0,64},{64,0},{128,192},{192,128},{256,320},{320,256},{384,448},{4... | collective-permute-start | bytes 393224 | tf_op jit(solution)/shard_map/ppermute | solution.py:537

commit v5 on v4

--- a/solution.py
+++ b/solution.py
@@ -280,7 +280,7 @@
                             total[z, seen, :] = total[z, seen, :] + term if j else term
             return 0
 
-        lax.fori_loop(0, NZ // groups, layers, 0)
+        lax.fori_loop(0, NZ // groups, layers, 0, unroll=4)
         cur, old = old, cur
     return cur, old
 
@@ -359,7 +359,7 @@
                 coefs[3][kind][z, rows, :] = ((1.0 / 840.0 / 840.0) * pace) * y_slope[y, rows, :]
         return 0
 
-    lax.fori_loop(0, NZ // 2, slopes, 0)
+    lax.fori_loop(0, NZ // 2, slopes, 0, unroll=2)
     lane8 = lane_of(8)
     for wide_side, side in ((t0, f0), (t1, f1), (t2, f2), (t3, f3)):
         for p in range(4):

time: 104 us -> 104 us (level)
  Pallas kernels: 24.2 us -> 22.9 us
  transfers between devices with their start and end apart: 11 -> 11, of which waited for: 6 -> 6; matrix products, arithmetic and copies ran while one was open for 0% -> 0% of each run, Pallas kernels for 6% -> 7%
where the time goes in v5:
time: 104 us; the launch traced here: 103 us
  starting transfers between devices  40.4 us (39%)
  waiting for transfers between devices  24.1 us (23%)
  Pallas kernels  22.9 us (22%)
  blocking collectives  12.1 us (12%)
  other arithmetic  1.43 us (1%)
    all_to_all x1, blocking collectives, shards(): lax.all_to_all(pair, 'shot', 0, 0, axis_index_groups=same_core)  12.1 us
    ppermute x2, starting transfers between devices, swap(): lax.ppermute(x, axis, [(a, b) for a, b in pairs] + [(b, a) for a, b in pa...  9.76 us
    pallas_call x1, Pallas kernels, steps_one(): pl.pallas_call(first_kernel, out_shape=(shape(40, BX, BY), image, image)...  9.13 us
    ppermute x1, waiting for transfers between devices, shards(): low = lax.ppermute(centre, 'gx', up)  9.09 us
    pallas_call x1, Pallas kernels, steps_two(): pl.pallas_call(second_kernel, out_shape=(shape(NZ, BX, BY),) * 2 + (shape...  7.07 us
    pallas_call x1, Pallas kernels, shards(): pl.pallas_call(find_kernel, out_shape=(listed, listed, listed, shape(1, d...  6.04 us
    all_to_all x1, starting transfers between devices, shards(): lax.all_to_all(own, 'shot', 0, 0, axis_index_groups=same_core)  6.03 us
    ppermute x1, waiting for transfers between devices, shards(): high = lax.ppermute(send, 'gx', down)  5.8 us
  transfers between devices with their start and end apart: 11, of which 6 were waited for; matrix products, arithmetic and copies ran while one was open for 0% of the time, Pallas kernels for 7%

profile of v5, /device:TPU:6, one launch (start us, length us, event | category | flops | bytes accessed | tf_op | source)
XLA Modules:
  0.0 102.8 jit_solution(9237063673662743394)
XLA Ops:
  0.6 0.7 broadcast_in_dim.13
  1.4 0.7 pad_maximum_fusion.2
  2.0 6.0 %all-to-all-start = ((f32[4,4,16,128]{3,2,1,0:T(8,128)}), f32[4,4,16,128]{3,2,1,0:T(8,128)S(1)}, u32[]{:S(2)}, u32[]{:S(2)}) async-start(f32[4,4,16,128]{3,2,1,0:T(8,128)} %pad_maximum_fusion.2), calls=%async_computation | async-start | bytes 262144 | tf_op jit(solution)/shard_map/all_to_all | solution.py:505
  8.1 5.2 %collective-permute-start.3 = (f32[32,16,128]{2,1,0:T(8,128)S(1)}, f32[32,16,128]{2,1,0:T(8,128)S(1)}, u32[]{:S(2)}, u32[]{:S(2)}) collective-permute-start(f32[32,16,128]{2,1,0:T(8,128)S(1)} %pad_maximum_fusion.1.fields_ref.centre_fields), channel_id=1, source_target_pairs={{4,0},{8,4},{12,8},{16,12},{20,16},{24,20},{28,24},{32,28},{36,32}... | collective-permute-start | bytes 786440 | tf_op jit(solution)/shard_map/ppermute | solution.py:502
  13.3 1.9 %collective-permute-start.2 = (f32[32,16,128]{2,1,0:T(8,128)S(1)}, f32[32,16,128]{2,1,0:T(8,128)S(1)}, u32[]{:S(2)}, u32[]{:S(2)}) collective-permute-start(f32[32,16,128]{2,1,0:T(8,128)S(1)} %pad_maximum_fusion.1.fields_ref.centre_fields), channel_id=1, source_target_pairs={{0,4},{4,8},{8,12},{12,16},{16,20},{20,24},{24,28},{28,32},{32,36}... | collective-permute-start | bytes 786440 | tf_op jit(solution)/shard_map/ppermute | solution.py:501
  15.3 0.7 pack_sides.1
  16.0 9.1 %collective-permute-start = (f32[12,16,128]{2,1,0:T(8,128)S(1)}, f32[12,16,128]{2,1,0:T(8,128)S(1)}, u32[]{:S(2)}, u32[]{:S(2)}) collective-permute-start(f32[12,16,128]{2,1,0:T(8,128)S(1)} %get-tuple-element.32), channel_id=1, source_target_pairs={{0,1},{2,3},{1,0},{3,2},{4,5},{6,7},{5,4},{7,6},{8,9},{10,11},{9,8... | collective-permute-start | bytes 294920 | tf_op jit(solution)/shard_map/ppermute | solution.py:476
  25.2 0.7 collective-permute-start.1
  25.8 6.0 %find_receivers.1 = (s32[264]{0:T(512)S(1)}, s32[264]{0:T(512)S(1)}, s32[264]{0:T(512)S(1)}, s32[1]{0:T(128)}) custom-call(s32[4]{0:T(128)S(1)} %pad_add_fusion.where_ref, s32[256]{0:T(256)S(1)} %bitcast.19), custom_call_target="tpu_custom_call" | custom-call | flops 8000 | bytes 4000 | tf_op jit(solution)/shard_map/find_receivers/pallas_call | solution.py:488
  31.9 1.9 %collective-permute-done = f32[12,16,128]{2,1,0:T(8,128)S(1)} collective-permute-done((f32[12,16,128]{2,1,0:T(8,128)S(1)}, f32[12,16,128]{2,1,0:T(8,128)S(1)}, u32[]{:S(2)}, u32[]{:S(2)}) %collective-permute-start) | collective-permute-done | bytes 98336 | tf_op jit(solution)/shard_map/ppermute | solution.py:476
  33.9 5.8 %collective-permute-start.5 = (f32[40,16,128]{2,1,0:T(8,128)S(1)}, f32[40,16,128]{2,1,0:T(8,128)S(1)}, u32[]{:S(2)}, u32[]{:S(2)}) collective-permute-start(f32[40,16,128]{2,1,0:T(8,128)S(1)} %pad_maximum_fusion.centre_ref), channel_id=1, source_target_pairs={{4,0},{8,4},{12,8},{16,12},{20,16},{24,20},{28,24},{32,28},{36,32}... | collective-permute-start | bytes 983048 | tf_op jit(solution)/shard_map/ppermute | solution.py:523
  39.6 1.9 %collective-permute-start.4 = (f32[40,16,128]{2,1,0:T(8,128)S(1)}, f32[40,16,128]{2,1,0:T(8,128)S(1)}, u32[]{:S(2)}, u32[]{:S(2)}) collective-permute-start(f32[40,16,128]{2,1,0:T(8,128)S(1)} %pad_maximum_fusion.centre_ref), channel_id=1, source_target_pairs={{0,4},{4,8},{8,12},{12,16},{16,20},{20,24},{24,28},{28,32},{32,36}... | collective-permute-start | bytes 983048 | tf_op jit(solution)/shard_map/ppermute | solution.py:522
  41.6 9.1 %collective-permute-done.4.low_ref = f32[40,16,128]{2,1,0:T(8,128)S(1)} collective-permute-done((f32[40,16,128]{2,1,0:T(8,128)S(1)}, f32[40,16,128]{2,1,0:T(8,128)S(1)}, u32[]{:S(2)}, u32[]{:S(2)}) %collective-permute-start.4) | collective-permute-done | bytes 327712 | tf_op jit(solution)/shard_map/ppermute | solution.py:522
  50.8 2.1 %collective-permute-start.6 = (f32[72,16,128]{2,1,0:T(8,128)S(1)}, f32[72,16,128]{2,1,0:T(8,128)S(1)}, u32[]{:S(2)}, u32[]{:S(2)}) collective-permute-start(f32[72,16,128]{2,1,0:T(8,128)S(1)} %slice_dynamic-update-slice_fusion.3), channel_id=1, source_target_pairs={{0,64},{64,0},{128,192},{192,128},{256,320},{320,256},{384,448},{4... | collective-permute-start | bytes 1769480 | tf_op jit(solution)/shard_map/ppermute | solution.py:528
  53.0 1.9 %collective-permute-done.6.other_ref = f32[72,16,128]{2,1,0:T(8,128)S(1)} collective-permute-done((f32[72,16,128]{2,1,0:T(8,128)S(1)}, f32[72,16,128]{2,1,0:T(8,128)S(1)}, u32[]{:S(2)}, u32[]{:S(2)}) %collective-permute-start.6) | collective-permute-done | bytes 589856 | tf_op jit(solution)/shard_map/ppermute | solution.py:528
  54.9 9.1 %first_steps.1 = (f32[40,16,128]{2,1,0:T(8,128)S(1)}, f32[16,24,128]{2,1,0:T(8,128)S(1)}, f32[16,24,128]{2,1,0:T(8,128)S(1)}, f32[16,48,128]{2,1,0:T(8,128)S(1)}...) custom-call(s32[4]{0:T(128)S(1)} %pad_add_fusion.where_ref, ...), custom_call_target="tpu_custom_call" | custom-call | tf_op jit(solution)/shard_map/first_steps/pallas_call | solution.py:445
  64.0 1.9 %collective-permute-start.8 = (f32[40,16,128]{2,1,0:T(8,128)S(1)}, f32[40,16,128]{2,1,0:T(8,128)S(1)}, u32[]{:S(2)}, u32[]{:S(2)}) collective-permute-start(f32[40,16,128]{2,1,0:T(8,128)S(1)} %get-tuple-element.45.centre_ref), channel_id=1, source_target_pairs={{4,0},{8,4},{12,8},{16,12},{20,16},{24,20},{28,24},{32,28},{36,32}... | collective-permute-start | bytes 983048 | tf_op jit(solution)/shard_map/ppermute | solution.py:535
  66.0 3.9 %collective-permute-start.7 = (f32[40,16,128]{2,1,0:T(8,128)S(1)}, f32[40,16,128]{2,1,0:T(8,128)S(1)}, u32[]{:S(2)}, u32[]{:S(2)}) collective-permute-start(f32[40,16,128]{2,1,0:T(8,128)S(1)} %get-tuple-element.45.centre_ref), channel_id=1, source_target_pairs={{0,4},{4,8},{8,12},{12,16},{16,20},{20,24},{24,28},{28,32},{32,36}... | collective-permute-start | bytes 983048 | tf_op jit(solution)/shard_map/ppermute | solution.py:534
  69.9 5.8 %collective-permute-done.8.high_ref = f32[40,16,128]{2,1,0:T(8,128)S(1)} collective-permute-done((f32[40,16,128]{2,1,0:T(8,128)S(1)}, f32[40,16,128]{2,1,0:T(8,128)S(1)}, u32[]{:S(2)}, u32[]{:S(2)}) %collective-permute-start.8) | collective-permute-done | bytes 327712 | tf_op jit(solution)/shard_map/ppermute | solution.py:535
  75.7 4.0 %collective-permute-done.7.low_ref = f32[40,16,128]{2,1,0:T(8,128)S(1)} collective-permute-done((f32[40,16,128]{2,1,0:T(8,128)S(1)}, f32[40,16,128]{2,1,0:T(8,128)S(1)}, u32[]{:S(2)}, u32[]{:S(2)}) %collective-permute-start.7) | collective-permute-done | bytes 327712 | tf_op jit(solution)/shard_map/ppermute | solution.py:534
  79.7 7.1 %second_steps.1 = (f32[16,16,128]{2,1,0:T(8,128)}, f32[16,16,128]{2,1,0:T(8,128)}, f32[4,4,16,128]{3,2,1,0:T(8,128)S(1)}, f32[4,4,16,128]{3,2,1,0:T(8,128)S(1)}) custom-call(s32[4]{0:T(128)S(1)} %pad_add_fusion.where_ref, s32[264]{0:T(512)S(1)} %get-tuple-element.38.place_ref, s32[264]{0:T(512)S(1)} %get-tuple-element.39.which_ref, ...), custom_call_target="tpu_custom_call" | custom-call | tf_op jit(solution)/shard_map/second_steps/pallas_call | solution.py:462
  86.8 1.9 %collective-permute-start.9 = (f32[4,4,16,128]{3,2,1,0:T(8,128)S(1)}, f32[4,4,16,128]{3,2,1,0:T(8,128)S(1)}, u32[]{:S(2)}, u32[]{:S(2)}) collective-permute-start(f32[4,4,16,128]{3,2,1,0:T(8,128)S(1)} %get-tuple-element.57), channel_id=1, source_target_pairs={{0,64},{64,0},{128,192},{192,128},{256,320},{320,256},{384,448},{4... | collective-permute-start | bytes 393224 | tf_op jit(solution)/shard_map/ppermute | solution.py:537
  88.7 1.3 %collective-permute-done.9 = f32[4,4,16,128]{3,2,1,0:T(8,128)S(1)} collective-permute-done((f32[4,4,16,128]{3,2,1,0:T(8,128)S(1)}, f32[4,4,16,128]{3,2,1,0:T(8,128)S(1)}, u32[]{:S(2)}, u32[]{:S(2)}) %collective-permute-start.9) | collective-permute-done | bytes 131104 | tf_op jit(solution)/shard_map/ppermute | solution.py:537
  90.1 12.1 %all_to_all.10 = f32[4,4,16,128]{3,2,1,0:T(8,128)S(1)} all-to-all(f32[4,4,16,128]{3,2,1,0:T(8,128)S(1)} %add.12), channel_id=1, replica_groups={{0,128,256,384},{64,192,320,448},{1,129,257,385},{65,193,321,449},{2,13..., dimensions={0} | all-to-all | bytes 262144 | tf_op jit(solution)/shard_map/all_to_all | solution.py:538
  (42 shorter events, 0.9 us)
Async XLA Ops:
  0.6 0.7 copy-start.9
  2.0 6.0 %copy-start.7 = (f32[1,16,16,128]{3,2,1,0:T(8,128)S(1)}, f32[1,16,16,128]{3,2,1,0:T(8,128)}, u32[]{:S(2)}) copy-start(f32[1,16,16,128]{3,2,1,0:T(8,128)} %param.15) | copy-start | bytes 393220
  2.0 6.0 %copy-start.8 = (f32[1,16,16,128]{3,2,1,0:T(8,128)S(1)}, f32[1,16,16,128]{3,2,1,0:T(8,128)}, u32[]{:S(2)}) copy-start(f32[1,16,16,128]{3,2,1,0:T(8,128)} %param.14) | copy-start | bytes 393220
  2.0 13.3 %all-to-all-start = ((f32[4,4,16,128]{3,2,1,0:T(8,128)}), f32[4,4,16,128]{3,2,1,0:T(8,128)S(1)}, u32[]{:S(2)}, u32[]{:S(2)}) async-start(f32[4,4,16,128]{3,2,1,0:T(8,128)} %pad_maximum_fusion.2), calls=%async_computation | async-start | bytes 262144 | tf_op jit(solution)/shard_map/all_to_all | solution.py:505
  8.1 25.7 %collective-permute-start.3 = (f32[32,16,128]{2,1,0:T(8,128)S(1)}, f32[32,16,128]{2,1,0:T(8,128)S(1)}, u32[]{:S(2)}, u32[]{:S(2)}) collective-permute-start(f32[32,16,128]{2,1,0:T(8,128)S(1)} %pad_maximum_fusion.1.fields_ref.centre_fields), channel_id=1, source_target_pairs={{4,0},{8,4},{12,8},{16,12},{20,16},{24,20},{28,24},{32,28},{36,32}... | collective-permute-start | bytes 786440 | tf_op jit(solution)/shard_map/ppermute | solution.py:502
  13.3 20.6 %collective-permute-start.2 = (f32[32,16,128]{2,1,0:T(8,128)S(1)}, f32[32,16,128]{2,1,0:T(8,128)S(1)}, u32[]{:S(2)}, u32[]{:S(2)}) collective-permute-start(f32[32,16,128]{2,1,0:T(8,128)S(1)} %pad_maximum_fusion.1.fields_ref.centre_fields), channel_id=1, source_target_pairs={{0,4},{4,8},{8,12},{12,16},{16,20},{20,24},{24,28},{28,32},{32,36}... | collective-permute-start | bytes 786440 | tf_op jit(solution)/shard_map/ppermute | solution.py:501
  16.0 17.8 %collective-permute-start = (f32[12,16,128]{2,1,0:T(8,128)S(1)}, f32[12,16,128]{2,1,0:T(8,128)S(1)}, u32[]{:S(2)}, u32[]{:S(2)}) collective-permute-start(f32[12,16,128]{2,1,0:T(8,128)S(1)} %get-tuple-element.32), channel_id=1, source_target_pairs={{0,1},{2,3},{1,0},{3,2},{4,5},{6,7},{5,4},{7,6},{8,9},{10,11},{9,8... | collective-permute-start | bytes 294920 | tf_op jit(solution)/shard_map/ppermute | solution.py:476
  25.1 0.7 copy-start.5
  25.2 8.7 %collective-permute-start.1 = (f32[12,16,128]{2,1,0:T(8,128)S(1)}, f32[12,16,128]{2,1,0:T(8,128)S(1)}, u32[]{:S(2)}, u32[]{:S(2)}) collective-permute-start(f32[12,16,128]{2,1,0:T(8,128)S(1)} %get-tuple-element.33), channel_id=1, source_target_pairs={{1,2},{2,1},{5,6},{6,5},{9,10},{10,9},{13,14},{14,13},{17,18},{18,... | collective-permute-start | bytes 294920 | tf_op jit(solution)/shard_map/ppermute | solution.py:476
  33.9 16.9 %collective-permute-start.5 = (f32[40,16,128]{2,1,0:T(8,128)S(1)}, f32[40,16,128]{2,1,0:T(8,128)S(1)}, u32[]{:S(2)}, u32[]{:S(2)}) collective-permute-start(f32[40,16,128]{2,1,0:T(8,128)S(1)} %pad_maximum_fusion.centre_ref), channel_id=1, source_target_pairs={{4,0},{8,4},{12,8},{16,12},{20,16},{24,20},{28,24},{32,28},{36,32}... | collective-permute-start | bytes 983048 | tf_op jit(solution)/shard_map/ppermute | solution.py:523
  39.6 11.1 %collective-permute-start.4 = (f32[40,16,128]{2,1,0:T(8,128)S(1)}, f32[40,16,128]{2,1,0:T(8,128)S(1)}, u32[]{:S(2)}, u32[]{:S(2)}) collective-permute-start(f32[40,16,128]{2,1,0:T(8,128)S(1)} %pad_maximum_fusion.centre_ref), channel_id=1, source_target_pairs={{0,4},{4,8},{8,12},{12,16},{16,20},{20,24},{24,28},{28,32},{32,36}... | collective-permute-start | bytes 983048 | tf_op jit(solution)/shard_map/ppermute | solution.py:522
  41.6 11.3 %copy-start.6 = (bf16[1,8,16,16,128]{4,3,2,1,0:T(8,128)(2,1)S(1)}, bf16[1,8,16,16,128]{4,3,2,1,0:T(8,128)(2,1)}, u32[]{:S(2)}) copy-start(bf16[1,8,16,16,128]{4,3,2,1,0:T(8,128)(2,1)} %param.13) | copy-start | bytes 1572868
  50.8 4.1 %copy-start.2 = (bf16[2,256,256]{2,1,0:T(8,128)(2,1)S(1)}, bf16[2,256,256]{2,1,0:T(8,128)(2,1)}, u32[]{:S(2)}) copy-start(bf16[2,256,256]{2,1,0:T(8,128)(2,1)} %constant.54.clone.layer_w) | copy-start | bytes 786436
  50.8 4.0 %copy-start.3 = (bf16[384,256]{1,0:T(8,128)(2,1)S(1)}, bf16[384,256]{1,0:T(8,128)(2,1)}, u32[]{:S(2)}) copy-start(bf16[384,256]{1,0:T(8,128)(2,1)} %constant.55.clone.side_w) | copy-start | bytes 589828
  50.8 4.0 %collective-permute-start.6 = (f32[72,16,128]{2,1,0:T(8,128)S(1)}, f32[72,16,128]{2,1,0:T(8,128)S(1)}, u32[]{:S(2)}, u32[]{:S(2)}) collective-permute-start(f32[72,16,128]{2,1,0:T(8,128)S(1)} %slice_dynamic-update-slice_fusion.3), channel_id=1, source_target_pairs={{0,64},{64,0},{128,192},{192,128},{256,320},{320,256},{384,448},{4... | collective-permute-start | bytes 1769480 | tf_op jit(solution)/shard_map/ppermute | solution.py:528
  52.9 2.0 %copy-start.4 = (f32[1,8,256]{2,1,0:T(8,128)S(1)}, f32[1,8,256]{2,1,0:T(8,128)}, u32[]{:S(2)}) copy-start(f32[1,8,256]{2,1,0:T(8,128)} %param.17) | copy-start | bytes 24580
  54.9 24.9 %copy-start = (bf16[4,256,256]{2,1,0:T(8,128)(2,1)S(1)}, bf16[4,256,256]{2,1,0:T(8,128)(2,1)}, u32[]{:S(2)}) copy-start(bf16[4,256,256]{2,1,0:T(8,128)(2,1)} %constant.56.clone.layer_w) | copy-start | bytes 1572868
  54.9 24.9 %copy-start.1 = (bf16[640,256]{1,0:T(8,128)(2,1)S(1)}, bf16[640,256]{1,0:T(8,128)(2,1)}, u32[]{:S(2)}) copy-start(bf16[640,256]{1,0:T(8,128)(2,1)} %constant.57.clone.side_w) | copy-start | bytes 983044
  64.0 11.7 %collective-permute-start.8 = (f32[40,16,128]{2,1,0:T(8,128)S(1)}, f32[40,16,128]{2,1,0:T(8,128)S(1)}, u32[]{:S(2)}, u32[]{:S(2)}) collective-permute-start(f32[40,16,128]{2,1,0:T(8,128)S(1)} %get-tuple-element.45.centre_ref), channel_id=1, source_target_pairs={{4,0},{8,4},{12,8},{16,12},{20,16},{24,20},{28,24},{32,28},{36,32}... | collective-permute-start | bytes 983048 | tf_op jit(solution)/shard_map/ppermute | solution.py:535
  66.0 13.8 %collective-permute-start.7 = (f32[40,16,128]{2,1,0:T(8,128)S(1)}, f32[40,16,128]{2,1,0:T(8,128)S(1)}, u32[]{:S(2)}, u32[]{:S(2)}) collective-permute-start(f32[40,16,128]{2,1,0:T(8,128)S(1)} %get-tuple-element.45.centre_ref), channel_id=1, source_target_pairs={{0,4},{4,8},{8,12},{12,16},{16,20},{20,24},{24,28},{28,32},{32,36}... | collective-permute-start | bytes 983048 | tf_op jit(solution)/shard_map/ppermute | solution.py:534
  86.8 3.2 %collective-permute-start.9 = (f32[4,4,16,128]{3,2,1,0:T(8,128)S(1)}, f32[4,4,16,128]{3,2,1,0:T(8,128)S(1)}, u32[]{:S(2)}, u32[]{:S(2)}) collective-permute-start(f32[4,4,16,128]{3,2,1,0:T(8,128)S(1)} %get-tuple-element.57), channel_id=1, source_target_pairs={{0,64},{64,0},{128,192},{192,128},{256,320},{320,256},{384,448},{4... | collective-permute-start | bytes 393224 | tf_op jit(solution)/shard_map/ppermute | solution.py:537
